TPU v7x, 32 devices: a whole 2x2x4 slice. The times are simulated.
32 devices in a mesh: seq: 4 (over z), fsdp: 8 (over y, x, core).
Axes of the slice: x: 2, y: 2, z: 4, core: 2. Of those that a mesh axis runs over, the one named last changes fastest.
Arguments:
- history: bfloat16 [9, 8, 512, 2048], P(None, 'fsdp', 'seq'), may hold values from -6 to 6
- cotangent: bfloat16 [8, 512, 2048], P('fsdp', 'seq'), may hold values from -6 to 6
- seq_lengths: int32 [8, 3], P('fsdp'), may hold values from 1 to 510, as said below
- wq: float32 [2048, 2048], P('fsdp'), may hold values from -0.125 to 0.125
- wk: float32 [2048, 2048], P('fsdp'), may hold values from -0.125 to 0.125
- wv: float32 [2048, 2048], P('fsdp'), may hold values from -0.125 to 0.125
- wo: float32 [2048, 2048], P('fsdp'), may hold values from -2 to 2
- w_in: float32 [2048, 8192], P('fsdp'), may hold values from -0.125 to 0.125
- w_out: float32 [8192, 2048], P('fsdp'), may hold values from -0.125 to 0.125
- mix_in: float32 [2048, 100], replicated, may hold values from -0.125 to 0.125
- mix_out: float32 [100, 36], replicated, may hold values from -0.625 to 0.625
- attn_gain: float32 [2048], replicated, may hold values from 0.25 to 1.75
- mlp_gain: float32 [2048], replicated, may hold values from 0.25 to 1.75
- mix_gain: float32 [2048], replicated, may hold values from 0.25 to 1.75
Outputs:
- layer_out: bfloat16 [8, 512, 2048], P('fsdp', 'seq')
- history_grad: bfloat16 [9, 8, 512, 2048], P(None, 'fsdp', 'seq')
- wq_grad: float32 [2048, 2048], P('fsdp')
- wk_grad: float32 [2048, 2048], P('fsdp')
- wv_grad: float32 [2048, 2048], P('fsdp')
- wo_grad: float32 [2048, 2048], P('fsdp')
- w_in_grad: float32 [2048, 8192], P('fsdp')
- w_out_grad: float32 [8192, 2048], P('fsdp')
- mix_in_grad: float32 [2048, 100], replicated
- mix_out_grad: float32 [100, 36], replicated
- attn_gain_grad: float32 [2048], replicated
- mlp_gain_grad: float32 [2048], replicated
- mix_gain_grad: float32 [2048], replicated
Inputs may be any that keep to these rules, and one draw needn't show every extreme that they name: `seq_lengths`: each group packs three sequences in order; the first and the last have fewer than 128 tokens, and the three sum to 512.
All inputs are finite; a program needn't handle non-finite values.
Results may differ from a plain program's by a relative error of at most 0.018.
The roundings to bfloat16 on the way count: a program that leaves them out, or rounds other values in their place, can miss the bound.
Values may be sent and summed in bfloat16 or wider, within the bound.
A program may use at most 576 MiB of HBM per device.

v0:
```python
from functools import partial

import jax
import jax.numpy as jnp
from jax import lax
from jax.sharding import PartitionSpec as P

D = 2048
HEADS = 16
HEAD = 128
ROT = 32
HIST = 9
STREAMS = 4


EPSILON = 1e-05
NEGATIVE = -1e30


def token_marks(tok_index, lengths):
    first_end = lengths[0]
    second_end = lengths[0] + lengths[1]
    segment = (tok_index >= first_end).astype(jnp.int32) + (tok_index >= second_end).astype(
        jnp.int32
    )
    seq_begin = jnp.where(segment == 0, 0, jnp.where(segment == 1, first_end, second_end))
    return (segment, tok_index - seq_begin)


def rope_tables(tok_place):
    inverse = 10000.0 ** (-jnp.arange(0, ROT, 2, dtype=jnp.float32) / ROT)
    angles = tok_place.astype(jnp.float32)[:, None] * inverse[None, :]
    angles = jnp.concatenate([angles, angles], axis=1)
    return (jnp.cos(angles), jnp.sin(angles))


def rotate(values, cosine_table, sine_table):
    half_rot = ROT // 2
    rot_part = values[..., :ROT]
    turned = jnp.concatenate([-rot_part[..., half_rot:], rot_part[..., :half_rot]], axis=-1)
    moved = rot_part * cosine_table[:, None, :] + turned * sine_table[:, None, :]
    return jnp.concatenate([moved, values[..., ROT:]], axis=-1)


def rotate_back(grads, cosine_table, sine_table):
    _, pullback = jax.vjp(
        partial(rotate, cosine_table=cosine_table, sine_table=sine_table), jnp.zeros_like(grads)
    )
    return pullback(grads)[0]


def norm_rows(values, gain_vec):
    inverse = lax.rsqrt(jnp.mean(values * values, axis=-1, keepdims=True) + EPSILON)
    return values * inverse * gain_vec


def norm_back(values, gain_vec, grads):
    _, pullback = jax.vjp(norm_rows, values, gain_vec)
    return pullback(grads)


def gelu_exact(values):
    return jax.nn.gelu(values, approximate=False)


def gelu_back(values, grads):
    _, pullback = jax.vjp(gelu_exact, values)
    return pullback(grads)[0]


def times_t(left_op, right_op):
    return lax.dot_general(
        left_op, right_op, (((1,), (1,)), ((), ())), preferred_element_type=jnp.float32
    )


def contract_rows(left_op, right_op):
    return lax.dot_general(
        left_op, right_op, (((0,), (0,)), ((), ())), preferred_element_type=jnp.float32
    )


def local(
    history,
    cotangent,
    seq_lengths,
    wq,
    wk,
    wv,
    wo,
    w_in,
    w_out,
    mix_in,
    mix_out,
    attn_gain,
    mlp_gain,
    mix_gain,
):
    entries = history[:, 0].astype(jnp.float32)
    tok_rows = entries.shape[1]
    lengths = seq_lengths[0]
    tok_index = lax.axis_index("seq") * tok_rows + jnp.arange(tok_rows, dtype=jnp.int32)
    segment, tok_place = token_marks(tok_index, lengths)
    cosine_table, sine_table = rope_tables(tok_place)
    score_scale = HEAD ** (-0.5)
    full_q, full_k, full_v, full_o, full_in, full_out = (
        lax.all_gather(wq.astype(jnp.bfloat16), "fsdp", axis=0, tiled=True),
        lax.all_gather(wk.astype(jnp.bfloat16), "fsdp", axis=0, tiled=True),
        lax.all_gather(wv.astype(jnp.bfloat16), "fsdp", axis=0, tiled=True),
        lax.all_gather(wo.astype(jnp.bfloat16), "fsdp", axis=0, tiled=True),
        lax.all_gather(w_in.astype(jnp.bfloat16), "fsdp", axis=0, tiled=True),
        lax.all_gather(w_out.astype(jnp.bfloat16), "fsdp", axis=0, tiled=True),
    )
    last_entry = entries[HIST - 1]
    mixed_low = norm_rows(last_entry, mix_gain).astype(jnp.bfloat16)
    mix_in_low = mix_in.astype(jnp.bfloat16)
    mix_out_low = mix_out.astype(jnp.bfloat16)
    mix_pre = jnp.dot(mixed_low, mix_in_low, preferred_element_type=jnp.float32)
    act_low = gelu_exact(mix_pre).astype(jnp.bfloat16)
    mix_coef = jnp.dot(act_low, mix_out_low, preferred_element_type=jnp.float32).reshape(
        tok_rows, STREAMS, HIST
    )
    stream = jnp.einsum("ncj,jnd->cnd", mix_coef, entries, precision=lax.Precision.HIGHEST)
    normed_q = norm_rows(stream[0], attn_gain).astype(jnp.bfloat16)
    normed_k = norm_rows(stream[1], attn_gain).astype(jnp.bfloat16)
    normed_v = norm_rows(stream[2], attn_gain).astype(jnp.bfloat16)
    normed_r = norm_rows(stream[3], mlp_gain).astype(jnp.bfloat16)
    q_lin = jnp.dot(normed_q, full_q, preferred_element_type=jnp.float32).reshape(
        tok_rows, HEADS, HEAD
    )
    queries = rotate(q_lin, cosine_table, sine_table).astype(jnp.bfloat16)
    k_lin = jnp.dot(normed_k, full_k, preferred_element_type=jnp.float32).reshape(
        tok_rows, HEADS, HEAD
    )
    keys_low = rotate(k_lin, cosine_table, sine_table).astype(jnp.bfloat16)
    values_low = (
        jnp.dot(normed_v, full_v, preferred_element_type=jnp.float32)
        .astype(jnp.bfloat16)
        .reshape(tok_rows, HEADS, HEAD)
    )

    def visible(piece_rows):
        key_index = jnp.arange(piece_rows, dtype=jnp.int32)
        key_segment, _ = token_marks(key_index, lengths)
        return (
            (segment[:, None] == key_segment[None, :]) & (tok_index[:, None] >= key_index[None, :])
        )[None]

    weighted = jnp.zeros((tok_rows, HEADS, HEAD), jnp.float32)
    running_max = jnp.full((HEADS, tok_rows), NEGATIVE, jnp.float32)
    key_piece = lax.all_gather(keys_low, "seq", axis=0, tiled=True)
    value_piece = lax.all_gather(values_low, "seq", axis=0, tiled=True)
    allowed = visible(key_piece.shape[0])
    scores = (
        jnp.einsum("nhd,rhd->hnr", queries, key_piece, preferred_element_type=jnp.float32)
        * score_scale
    )
    scores = jnp.where(allowed, scores, NEGATIVE)
    new_max = jnp.maximum(running_max, jnp.max(scores, axis=2))
    shrink = jnp.exp(running_max - new_max)
    expo = jnp.exp(jnp.where(allowed, scores - new_max[:, :, None], NEGATIVE))
    expo = jnp.where(allowed, expo, 0.0)
    row_mass = jnp.sum(expo, axis=2)
    weighted = weighted * shrink.T[:, :, None] + jnp.einsum(
        "hnr,rhd->nhd", expo.astype(jnp.bfloat16), value_piece, preferred_element_type=jnp.float32
    )
    weighted, running_max, row_mass = (weighted, new_max, row_mass)
    attended = weighted / row_mass.T[:, :, None]
    logsum = running_max + jnp.log(row_mass)
    attn_low = attended.reshape(tok_rows, D).astype(jnp.bfloat16)
    attn_out = jnp.dot(attn_low, full_o, preferred_element_type=jnp.float32)
    up_proj = jnp.dot(normed_r, full_in, preferred_element_type=jnp.float32)
    hidden_low = gelu_exact(up_proj).astype(jnp.bfloat16)
    mlp_out = jnp.dot(hidden_low, full_out, preferred_element_type=jnp.float32)
    layer_out = (stream[3] + attn_out + mlp_out).astype(jnp.bfloat16)[None]
    grad_out = cotangent[0]
    grad_up = gelu_back(up_proj, times_t(grad_out, full_out)).astype(jnp.bfloat16)
    grad_normed_r = times_t(grad_up, full_in)
    grad_attn = times_t(grad_out, full_o).astype(jnp.bfloat16).reshape(tok_rows, HEADS, HEAD)
    delta_rows = jnp.sum(grad_attn.astype(jnp.float32) * attended, axis=2).T
    key_piece = lax.all_gather(keys_low, "seq", axis=0, tiled=True)
    value_piece = lax.all_gather(values_low, "seq", axis=0, tiled=True)
    piece_rows = key_piece.shape[0]
    allowed = visible(piece_rows)
    scores = (
        jnp.einsum("nhd,rhd->hnr", queries, key_piece, preferred_element_type=jnp.float32)
        * score_scale
    )
    prob_rows = jnp.where(
        allowed, jnp.exp(jnp.where(allowed, scores - logsum[:, :, None], NEGATIVE)), 0.0
    )
    grad_prob = jnp.einsum(
        "nhd,rhd->hnr", grad_attn, value_piece, preferred_element_type=jnp.float32
    )
    grad_scores = (prob_rows * (grad_prob - delta_rows[:, :, None])).astype(jnp.bfloat16)
    grad_query = (
        jnp.einsum("hnr,rhd->nhd", grad_scores, key_piece, preferred_element_type=jnp.float32)
        * score_scale
    )
    key_term = (
        jnp.einsum("hnr,nhd->rhd", grad_scores, queries, preferred_element_type=jnp.float32)
        * score_scale
    )
    value_term = jnp.einsum(
        "hnr,nhd->rhd",
        prob_rows.astype(jnp.bfloat16),
        grad_attn,
        preferred_element_type=jnp.float32,
    )
    grad_keys = key_term
    grad_values = value_term
    grad_query, grad_keys, grad_values = (grad_query, grad_keys, grad_values)
    own_keys, own_values = (
        lax.psum_scatter(
            grad_keys.astype(jnp.bfloat16), "seq", scatter_dimension=0, tiled=True
        ).astype(jnp.float32),
        lax.psum_scatter(
            grad_values.astype(jnp.bfloat16), "seq", scatter_dimension=0, tiled=True
        ).astype(jnp.float32),
    )
    grad_q_lin = (
        rotate_back(grad_query.astype(jnp.bfloat16).astype(jnp.float32), cosine_table, sine_table)
        .reshape(tok_rows, D)
        .astype(jnp.bfloat16)
    )
    grad_k_lin = (
        rotate_back(own_keys.astype(jnp.bfloat16).astype(jnp.float32), cosine_table, sine_table)
        .reshape(tok_rows, D)
        .astype(jnp.bfloat16)
    )
    grad_v_lin = own_values.astype(jnp.bfloat16).reshape(tok_rows, D)
    grad_sq, gain_q = norm_back(stream[0], attn_gain, times_t(grad_q_lin, full_q))
    grad_sk, gain_k = norm_back(stream[1], attn_gain, times_t(grad_k_lin, full_k))
    grad_sv, gain_v = norm_back(stream[2], attn_gain, times_t(grad_v_lin, full_v))
    grad_sr, gain_mlp = norm_back(stream[3], mlp_gain, grad_normed_r)
    grad_stream = jnp.stack(
        [grad_sq, grad_sk, grad_sv, grad_sr + grad_out.astype(jnp.float32)], axis=0
    )
    grad_coef = (
        jnp.einsum("cnd,jnd->ncj", grad_stream, entries, precision=lax.Precision.HIGHEST)
        .reshape(tok_rows, STREAMS * HIST)
        .astype(jnp.bfloat16)
    )
    grad_entries = jnp.einsum(
        "ncj,cnd->jnd", mix_coef, grad_stream, precision=lax.Precision.HIGHEST
    )
    grad_pre = gelu_back(mix_pre, times_t(grad_coef, mix_out_low)).astype(jnp.bfloat16)
    grad_last, gain_mix = norm_back(last_entry, mix_gain, times_t(grad_pre, mix_in_low))
    grad_entries = grad_entries.at[HIST - 1].add(grad_last)
    history_grad = grad_entries.astype(jnp.bfloat16)[:, None]
    small_sums = lax.psum(
        (
            contract_rows(mixed_low, grad_pre),
            contract_rows(act_low, grad_coef),
            gain_q + gain_k + gain_v,
            gain_mlp,
            gain_mix,
        ),
        ("seq", "fsdp"),
    )
    row_lefts = (normed_q, normed_k, normed_v, attn_low, normed_r)
    row_rights = (grad_q_lin, grad_k_lin, grad_v_lin, grad_out, grad_up)
    row_part = lax.psum_scatter(
        jnp.concatenate(
            [contract_rows(left_op, right_op) for left_op, right_op in zip(row_lefts, row_rights)],
            axis=1,
        ).astype(jnp.bfloat16),
        "fsdp",
        scatter_dimension=0,
        tiled=True,
    ).astype(jnp.float32)
    out_part = lax.psum_scatter(
        contract_rows(hidden_low, grad_out).astype(jnp.bfloat16),
        "fsdp",
        scatter_dimension=0,
        tiled=True,
    ).astype(jnp.float32)
    row_part, out_part = (
        lax.psum(row_part.astype(jnp.bfloat16), "seq").astype(jnp.float32),
        lax.psum(out_part.astype(jnp.bfloat16), "seq").astype(jnp.float32),
    )
    return (
        layer_out,
        history_grad,
        row_part[:, 0:D],
        row_part[:, D : 2 * D],
        row_part[:, 2 * D : 3 * D],
        row_part[:, 3 * D : 4 * D],
        row_part[:, 4 * D :],
        out_part,
        small_sums[0],
        small_sums[1],
        small_sums[2],
        small_sums[3],
        small_sums[4],
    )


def solution(mesh):
    in_specs = (
        P(None, "fsdp", "seq", None),
        P("fsdp", "seq", None),
        P("fsdp", None),
        P("fsdp", None),
        P("fsdp", None),
        P("fsdp", None),
        P("fsdp", None),
        P("fsdp", None),
        P("fsdp", None),
        P(),
        P(),
        P(),
        P(),
        P(),
    )
    out_specs = (
        P("fsdp", "seq", None),
        P(None, "fsdp", "seq", None),
        P("fsdp", None),
        P("fsdp", None),
        P("fsdp", None),
        P("fsdp", None),
        P("fsdp", None),
        P("fsdp", None),
        P(),
        P(),
        P(),
        P(),
        P(),
    )
    return jax.shard_map(local, mesh=mesh, in_specs=in_specs, out_specs=out_specs, check_vma=False)
```

profile of v0, /device:TPU:0, one launch (start us, length us, event | category | flops | bytes accessed | tf_op | source)
XLA Modules:
  0.0 1918.7 jit_solution(3100857009939584825)
XLA Ops:
  7.2 2.9 convert_element_type.221
  11.4 2.9 convert_element_type.223
  23.7 8.0 fusion.13
  34.8 5.4 multiply_convert_fusion.3
  40.6 27.1 %all-gather.11.cloned.1.call-done = bf16[2048,2048]{1,0:T(8,128)(2,1)} async-done(((bf16[256,2048]{1,0:T(8,128)(2,1)}), bf16[2048,2048]{1,0:T(8,128)(2,1)}) %all-gather.11.cloned.1.call-update) | async-done | bytes 8388624 | tf_op jit(solution)/shard_map/all_gather | solution.py:108
  67.6 12.3 copy.80
  79.9 6.2 fusion.81
  87.1 37.4 %all-gather.9.cloned.1.call-done = bf16[2048,2048]{1,0:T(8,128)(2,1)} async-done(((bf16[256,2048]{1,0:T(8,128)(2,1)}), bf16[2048,2048]{1,0:T(8,128)(2,1)}) %all-gather.9.cloned.1.call-update) | async-done | bytes 8388624 | tf_op jit(solution)/shard_map/all_gather | solution.py:107
  124.5 12.4 copy.79
  138.0 6.0 fusion.90
  147.5 33.9 %all-gather.15.cloned.1.call-done = bf16[2048,2048]{1,0:T(8,128)(2,1)} async-done(((bf16[256,2048]{1,0:T(8,128)(2,1)}), bf16[2048,2048]{1,0:T(8,128)(2,1)}) %all-gather.15.cloned.1.call-update) | async-done | bytes 8388624 | tf_op jit(solution)/shard_map/all_gather | solution.py:109
  181.4 5.7 convolution_convert_fusion.6
  189.2 6.8 convert_element_type.230
  199.4 38.8 %all-gather.19.cloned.1.call-done = bf16[2048,2048]{1,0:T(8,128)(2,1)} async-done(((bf16[256,2048]{1,0:T(8,128)(2,1)}), bf16[2048,2048]{1,0:T(8,128)(2,1)}) %all-gather.19.cloned.1.call-update) | async-done | bytes 8388624 | tf_op jit(solution)/shard_map/all_gather | solution.py:110
  238.1 6.3 convolution_convert_fusion.5
  245.4 41.0 %all-gather.13.cloned.1.call-done = bf16[512,16,128]{0,2,1:T(8,128)(2,1)} async-done(((bf16[128,16,128]{0,2,1:T(8,128)(2,1)}), bf16[512,16,128]{0,2,1:T(8,128)(2,1)}) %all-gather.13.cloned.1.call-update) | async-done | bytes 2097168 | tf_op jit(solution)/shard_map/all_gather | solution.py:151
  286.4 2.7 select_reduce_fusion
  293.4 39.5 %all-gather.17.cloned.1.call-done = bf16[512,16,128]{0,2,1:T(8,128)(2,1)} async-done(((bf16[128,16,128]{0,2,1:T(8,128)(2,1)}), bf16[512,16,128]{0,2,1:T(8,128)(2,1)}) %all-gather.17.cloned.1.call-update) | async-done | bytes 2097168 | tf_op jit(solution)/shard_map/all_gather | solution.py:152
  332.9 4.7 multiply_reduce_fusion.3
  343.2 4.2 copy.107
  347.5 6.1 fusion.35
  353.6 3.9 copy.109
  357.6 6.1 convert_element_type.232
  364.1 130.3 %all-gather.21.cloned.1.call-done = bf16[2048,8192]{1,0:T(8,128)(2,1)} async-done(((bf16[256,8192]{1,0:T(8,128)(2,1)}), bf16[2048,8192]{1,0:T(8,128)(2,1)}) %all-gather.21.cloned.1.call-update) | async-done | bytes 33554448 | tf_op jit(solution)/shard_map/all_gather | solution.py:111
  494.4 17.9 fusion.137
  512.3 23.4 %convolution_convert_fusion = bf16[8192,2048]{1,0:T(8,128)(2,1)} fusion(bf16[1,128,2048]{2,1,0:T(8,128)(2,1)S(1)} %copy-done.15, f32[128,8192]{1,0:T(8,128)} %fusion.137), kind=kOutput, calls=%fused_computation.1 | convolution fusion | flops 4379901952 | bytes 38273024 | tf_op jit(solution)/shard_map/dot_general | solution.py:78
  535.8 2.9 fusion.46
  539.7 5.8 convolution_convert_fusion.4
  545.5 12.5 copy.96
  562.5 5.9 convolution_convert_fusion.3
  568.4 12.3 copy.93
  581.9 7.0 convolution_convert_fusion.2
  588.9 12.7 copy.94
  601.6 7.3 convolution_convert_fusion.1
  608.9 12.5 copy.95
  621.5 8.3 constant_dynamic-update-slice_fusion.3
  629.7 8.2 constant_dynamic-update-slice_fusion.2
  637.9 8.2 constant_dynamic-update-slice_fusion.1
  646.2 8.4 constant_dynamic-update-slice_fusion
  654.6 95.2 %all-gather.23.cloned.1.call-done = bf16[8192,2048]{1,0:T(8,128)(2,1)} async-done(((bf16[1024,2048]{1,0:T(8,128)(2,1)}), bf16[8192,2048]{1,0:T(8,128)(2,1)}) %all-gather.23.cloned.1.call-update) | async-done | bytes 33554448 | tf_op jit(solution)/shard_map/all_gather | solution.py:112
  749.8 25.8 %add_convert_fusion = bf16[128,8192]{1,0:T(8,128)(2,1)} fusion(f32[128,8192]{1,0:T(8,128)} %fusion.137, bf16[8192,2048]{1,0:T(8,128)(2,1)} %all-gather.23.cloned.1.call-done, bf16[1,128,2048]{2,1,0:T(8,128)(2,1)} %param.17), kind=kOutput, calls=%fused_computation.14 | convolution fusion | flops 4370464768 | bytes 40370176 | tf_op jit(solution)/shard_map/dot_general | solution.py:72
  775.6 22.1 %convert_dynamic-update-slice_fusion = bf16[2048,16384]{1,0:T(8,128)(2,1)} fusion(bf16[2048,16384]{1,0:T(8,128)(2,1)} %constant_dynamic-update-slice_fusion, bf16[128,8192]{1,0:T(8,128)(2,1)} %add_convert_fusion, f32[1,128,2048]{2,0,1:T(1,128)S(1)} %get-tuple-element.89, f32[2048]{0:T(1024)S(1)} %copy-done.30, f32[128]{0:T(128)S(1)} %fusion.128), kind=kOutput, calls=%fused_computation | convolution fusion | flops 4312530944 | bytes 36708864 | tf_op jit(solution)/shard_map/dot_general | solution.py:78
  797.8 160.9 %reduce-scatter.11.cloned.1.call-done = bf16[1024,2048]{1,0:T(8,128)(2,1)} async-done(((bf16[8192,2048]{1,0:T(8,128)(2,1)}), bf16[1024,2048]{1,0:T(8,128)(2,1)}) %reduce-scatter.11.cloned.1.call-update) | async-done | bytes 4194320 | tf_op jit(solution)/shard_map/reduce_scatter | solution.py:272
  958.7 387.6 %reduce-scatter.9.cloned.1.call-done = bf16[256,16384]{1,0:T(8,128)(2,1)} async-done(((bf16[2048,16384]{1,0:T(8,128)(2,1)}), bf16[256,16384]{1,0:T(8,128)(2,1)}) %reduce-scatter.9.cloned.1.call-update) | async-done | bytes 8388624 | tf_op jit(solution)/shard_map/reduce_scatter | solution.py:263
  1346.8 6.0 convolution_add_fusion.1
  1352.8 7.6 fusion.145
  1360.5 6.4 fusion.144
  1367.0 4.3 fusion.74
  1371.4 2.6 fusion.56
  1374.0 16.6 multiply_reduce_fusion
  1393.2 15.5 fusion.11
  1408.7 5.8 copy-done
  1415.2 13.4 fusion.49
  1433.6 20.4 %scatter-add.4 = f32[9,128,2048]{2,0,1:T(8,128)} dynamic-update-slice(f32[9,128,2048]{2,0,1:T(8,128)} %bitcast.198, f32[1,128,2048]{2,0,1:T(1,128)S(1)} %copy.92, s32[]{:T(128)} %constant.43.clone.1, s32[]{:T(128)} %constant.79.clone.1, s32[]{:T(128)} %constant.79.clone.1) | dynamic-update-slice | bytes 2097156 | tf_op jit(solution)/shard_map/scatter-add | solution.py:249
  1454.1 6.6 convert_bitcast_fusion
  1460.7 5.0 copy.97
  1465.8 2.3 fusion.107
  1468.2 46.7 %all-reduce.8 = (f32[100,36]{0,1:T(8,128)}, f32[2048]{0:T(1024)}, f32[2048]{0:T(1024)}, f32[2048]{0:T(1024)}) all-reduce(f32[100,36]{0,1:T(8,128)S(1)} %fusion.146, f32[2048]{0:T(1024)S(1)} %add_add_fusion.5, f32[2048]{0:T(1024)S(1)} %get-tuple-element.66, ...), channel_id=1, replica_groups=mesh['seq'=4,'fsdp'=8] {'seq','fsdp'}, use_global_device_ids=true, to_apply=%region_20.21 | all-reduce | flops 9744 | bytes 77952 | tf_op jit(solution)/shard_map/psum | solution.py:251
  1514.9 20.4 %fusion.20 = bf16[1,128,2048]{2,1,0:T(8,128)(2,1)} fusion(f32[128,2048]{1,0:T(8,128)S(1)} %copy-done.26, bf16[8192,2048]{1,0:T(8,128)(2,1)} %all-gather.23.cloned.1.call-done, f32[128,8192]{1,0:T(8,128)} %fusion.137), kind=kOutput, calls=%fused_computation.46 | convolution fusion | flops 4363649024 | bytes 39321600 | tf_op jit(solution)/shard_map/dot_general | solution.py:174
  1535.3 241.5 %all-reduce.15.cloned.1.call-done = (bf16[256,16384]{1,0:T(8,128)(2,1)}, bf16[1024,2048]{1,0:T(8,128)(2,1)}) async-done(((bf16[256,16384]{1,0:T(8,128)(2,1)}, bf16[1024,2048]{1,0:T(8,128)(2,1)}), (bf16[256,16384]{1,0:T(8,128)(2,1)}, bf16[1024,2048]{1,0:T(8,128)(2,1)})) %all-reduce.15.cloned.1.call-update) | async-done | bytes 12582928 | tf_op jit(solution)/shard_map/psum | solution.py:279
  1776.8 6.7 slice.142
  1783.5 5.3 convert_element_type.260
  1790.0 3.8 fusion.139
  1793.7 116.1 %all-reduce.13.cloned.1.call-done = f32[2048,100]{0,1:T(8,128)} async-done(((f32[2048,100]{0,1:T(8,128)}), f32[2048,100]{0,1:T(8,128)}) %all-reduce.13.cloned.1.call-update) | async-done | bytes 819216 | tf_op jit(solution)/shard_map/psum | solution.py:251
  (246 shorter events, 53.9 us)
Async XLA Ops:
  7.2 60.4 %all-gather.11.cloned.1.call-start = ((), (), s32[]{:S(2)}) async-start(), calls=%async_computation.5 | async-start | bytes 9437184 | tf_op jit(solution)/shard_map/all_gather | solution.py:108
  10.1 114.4 %all-gather.9.cloned.1.call-start = ((), (), s32[]{:S(2)}) async-start(), calls=%async_computation.4 | async-start | bytes 9437184 | tf_op jit(solution)/shard_map/all_gather | solution.py:107
  11.3 6.0 copy-start.28
  11.3 6.0 copy-start.42
  11.3 170.1 %all-gather.15.cloned.1.call-start = ((), (), s32[]{:S(2)}) async-start(), calls=%async_computation.7 | async-start | bytes 9437184 | tf_op jit(solution)/shard_map/all_gather | solution.py:109
  14.3 5.8 copy-start.45
  14.3 6.1 copy-start.57
  14.3 223.9 %all-gather.19.cloned.1.call-start = ((), (), s32[]{:S(2)}) async-start(), calls=%async_computation.9 | async-start | bytes 9437184 | tf_op jit(solution)/shard_map/all_gather | solution.py:110
  15.5 270.9 %all-gather.13.cloned.1.call-start = ((), (), s32[]{:S(2)}) async-start(), calls=%async_computation.6 | async-start | bytes 2621440 | tf_op jit(solution)/shard_map/all_gather | solution.py:151
  20.4 11.3 copy-start.17
  33.6 6.6 copy-start.6
  33.6 147.8 %copy-start.1 = (f32[1,128,2048]{2,0,1:T(1,128)}, f32[1,128,2048]{2,0,1:T(1,128)S(1)}, u32[]{:S(2)}) copy-start(f32[1,128,2048]{2,0,1:T(1,128)S(1)} %get-tuple-element.91) | copy-start | bytes 3145732
  34.2 5.9 copy-start.66
  34.8 146.6 %copy-start.47 = (f32[128]{0:T(128)}, f32[128]{0:T(128)S(1)}, u32[]{:S(2)}) copy-start(f32[128]{0:T(128)S(1)} %fusion.127) | copy-start | bytes 1540
  34.8 5.4 copy-start.53
  40.5 39.4 %copy-start.60 = (f32[128]{0:T(128)}, f32[128]{0:T(128)S(1)}, u32[]{:S(2)}) copy-start(f32[128]{0:T(128)S(1)} %fusion.71) | copy-start | bytes 1540
  40.6 97.4 %copy-start.49 = (f32[128]{0:T(128)}, f32[128]{0:T(128)S(1)}, u32[]{:S(2)}) copy-start(f32[128]{0:T(128)S(1)} %fusion.125) | copy-start | bytes 1540
  137.9 7.0 copy-start.36
  138.0 7.0 copy-start.38
  147.5 185.4 %all-gather.17.cloned.1.call-start = ((), (), s32[]{:S(2)}) async-start(), calls=%async_computation.8 | async-start | bytes 2621440 | tf_op jit(solution)/shard_map/all_gather | solution.py:152
  189.2 305.2 %all-gather.21.cloned.1.call-start = ((), (), s32[]{:S(2)}) async-start(), calls=%async_computation.10 | async-start | bytes 37748736 | tf_op jit(solution)/shard_map/all_gather | solution.py:111
  196.0 42.2 %copy-start.15 = (bf16[1,128,2048]{2,1,0:T(8,128)(2,1)S(1)}, bf16[1,128,2048]{2,1,0:T(8,128)(2,1)}, u32[]{:S(2)}) copy-start(bf16[1,128,2048]{2,1,0:T(8,128)(2,1)} %param.17) | copy-start | bytes 1572868
  196.0 362.0 %reduce-scatter.13.cloned.1.call-start = ((), (), s32[]{:S(2)}) async-start(), calls=%async_computation.15 | async-start | bytes 2621440
  245.4 45.7 %copy-start.31 = (pred[128,512]{1,0:T(8,128)(4,1)S(1)}, pred[128,512]{1,0:T(8,128)(4,1)}, u32[]{:S(2)}) copy-start(pred[128,512]{1,0:T(8,128)(4,1)} %fusion.100) | copy-start | bytes 196612
  292.8 40.1 %copy-start.44 = (f32[16,128]{1,0:T(8,128)}, f32[16,128]{1,0:T(8,128)S(1)}, u32[]{:S(2)}) copy-start(f32[16,128]{1,0:T(8,128)S(1)} %fusion.17) | copy-start | bytes 24580
  332.9 4.7 copy-start.5
  332.9 4.7 copy-start.32
  332.9 4.7 copy-start.35
  332.9 4.8 copy-start.51
  332.9 5.1 copy-start.68
  337.6 202.1 %copy-start.14 = (bf16[128,16,128]{0,2,1:T(8,128)(2,1)}, bf16[128,16,128]{0,2,1:T(8,128)(2,1)S(1)}, u32[]{:S(2)}) copy-start(bf16[128,16,128]{0,2,1:T(8,128)(2,1)S(1)} %get-tuple-element.93) | copy-start | bytes 1572868
  347.4 254.2 %reduce-scatter.15.cloned.1.call-start = ((), (), s32[]{:S(2)}) async-start(), calls=%async_computation.16 | async-start | bytes 2621440 | tf_op jit(solution)/shard_map/reshape | solution.py:231
  357.5 392.3 %all-gather.23.cloned.1.call-start = ((), (), s32[]{:S(2)}) async-start(), calls=%async_computation.11 | async-start | bytes 37748736 | tf_op jit(solution)/shard_map/all_gather | solution.py:112
  363.6 130.8 %copy-start.30 = (f32[2048]{0:T(1024)S(1)}, f32[2048]{0:T(1024)}, u32[]{:S(2)}) copy-start(f32[2048]{0:T(1024)} %param.28) | copy-start | bytes 24580
  363.6 595.0 %reduce-scatter.11.cloned.1.call-start = ((), (), s32[]{:S(2)}) async-start(), calls=%async_computation.13 | async-start | bytes 37748736 | tf_op jit(solution)/shard_map/reduce_scatter | solution.py:272
  364.1 148.2 %copy-start.62 = (f32[128]{0:T(128)}, f32[128]{0:T(128)S(1)}, u32[]{:S(2)}) copy-start(f32[128]{0:T(128)S(1)} %multiply_reduce_fusion.4) | copy-start | bytes 1540
  535.7 810.5 %reduce-scatter.9.cloned.1.call-start = ((), (), s32[]{:S(2)}) async-start(), calls=%async_computation.12 | async-start | bytes 75497472 | tf_op jit(solution)/shard_map/reduce_scatter | solution.py:263
  558.0 4.4 slice-start.4
  568.4 12.3 copy-start.27
  797.7 979.1 %all-reduce.15.cloned.1.call-start = ((), (), s32[]{:S(2)}) async-start(), calls=%async_computation.17 | async-start | bytes 25165824 | tf_op jit(solution)/shard_map/psum | solution.py:279
  1346.3 563.5 %all-reduce.13.cloned.1.call-start = ((), (), s32[]{:S(2)}) async-start(), calls=%async_computation.14 | async-start | bytes 1703936 | tf_op jit(solution)/shard_map/psum | solution.py:251
  1346.7 6.0 copy-start.22
  1352.8 14.1 slice-start.2
  1360.4 6.5 copy-start.2
  1360.4 6.5 slice-start.3
  1360.4 6.5 copy-start.7
  1360.5 6.5 copy-start.48
  1360.5 6.5 copy-start.54
  1374.0 16.7 copy-start.63
  1374.0 16.7 copy-start.16
  1392.2 22.9 %slice-start = ((s8[4718592]{0:T(1024)(128)(4,1)}), s8[4194304]{0:T(1024)(128)(4,1)S(1)}, s32[]{:S(2)}) async-start(s8[4718592]{0:T(1024)(128)(4,1)} %bitcast.202), calls=%async_computation.18 | async-start | bytes 8388608
  1393.1 22.0 %slice-start.1 = ((s8[4718592]{0:T(1024)(128)(4,1)}), s8[524288]{0:T(1024)(128)(4,1)S(1)}, s32[]{:S(2)}) async-start(s8[4718592]{0:T(1024)(128)(4,1)} %bitcast.202), calls=%async_computation.19 | async-start | bytes 1048576
  1408.7 5.8 copy-start
  1415.2 13.6 copy-start.46
  1415.2 13.6 copy-start.69
  1415.2 13.6 copy-start.70
  1415.2 13.8 copy-start.29
  1415.2 13.8 copy-start.43
  1415.2 13.8 copy-start.56
  1415.2 15.6 copy-start.59
  1460.6 5.1 copy-start.41
  1460.6 54.3 %copy-start.26 = (f32[128,2048]{1,0:T(8,128)S(1)}, f32[128,2048]{1,0:T(8,128)}, u32[]{:S(2)}) copy-start(f32[128,2048]{1,0:T(8,128)} %convolution_add_fusion.1) | copy-start | bytes 3145732
  1776.8 6.7 copy-start.19
  1783.5 6.4 copy-start.3
  (26 other events, 61.4 us)
Sparse Core Ops, SparseCore 0:
  10.5 57.0 all-gather.10
  70.1 54.3 all-gather.8
  127.0 54.3 all-gather.14
  183.7 54.3 all-gather.18
  240.1 46.2 all-gather.12
  288.4 44.4 all-gather.16
  335.3 159.0 all-gather.20
  497.3 43.8 reduce-scatter.12
  544.1 43.1 reduce-scatter.14
  589.7 160.1 all-gather.22
  753.4 205.2 reduce-scatter.10
  962.5 383.7 reduce-scatter.8
  1348.9 427.8 all-reduce.14
  1782.5 127.3 all-reduce.12
where the time goes:
time: 1930 us; the launch traced here: 1920 us
  waiting for transfers between devices  1350 us (70%)
  matrix products  264 us (14%)
  local copies, waits for them, and re-layouts  182 us (9%)
  other arithmetic  58.7 us (3%)
  blocking collectives  46.7 us (2%)
    reduce_scatter x1, waiting for transfers between devices, local(): lax.psum_scatter(jnp.concatenate([contract_rows(left_op, right_op) for le...  388 us
    psum x1, waiting for transfers between devices, local(): lax.psum(row_part.astype(jnp.bfloat16), 'seq').astype(jnp.float32)  241 us
    reduce_scatter x1, waiting for transfers between devices, local(): lax.psum_scatter(contract_rows(hidden_low, grad_out).astype(jnp.bfloat16)...  161 us
    all_gather x1, waiting for transfers between devices, local(): lax.all_gather(w_in.astype(jnp.bfloat16), 'fsdp', axis=0, tiled=True)  130 us
    psum x1, waiting for transfers between devices, local(): lax.psum((contract_rows(mixed_low, grad_pre), contract_rows(act_low, grad...  116 us
    all_gather x1, waiting for transfers between devices, local(): lax.all_gather(w_out.astype(jnp.bfloat16), 'fsdp', axis=0, tiled=True)  95.2 us
    dot_general x8, matrix products, contract_rows(): lax.dot_general(left_op, right_op, (((0,), (0,)), ((), ())), preferred_el...  74 us
    dot_general x8, matrix products, times_t(): lax.dot_general(left_op, right_op, (((1,), (1,)), ((), ())), preferred_el...  69 us
  transfers between devices with their start and end apart: 14, of which 12 were waited for; matrix products, arithmetic and copies ran while one was open for 25% of the time, Pallas kernels for 0%

commit v1 on v0

v1 whole, which is shorter than its diff:
```python
from functools import partial

import jax
import jax.numpy as jnp
from jax import lax
from jax.experimental import pallas as pl
from jax.experimental.pallas import tpu as pltpu
from jax.sharding import PartitionSpec as P

D = 2048
HEADS = 16
HEAD = 128
ROT = 32
HIST = 9
STREAMS = 4
EPSILON = 1e-05
NEGATIVE = -1e30
MESH = pl.DeviceIdType.MESH
BF = jnp.bfloat16
F32 = jnp.float32
MIB = 2**20


def token_marks(tok_index, lengths):
    first_end = lengths[..., 0]
    second_end = first_end + lengths[..., 1]
    segment = (tok_index >= first_end).astype(jnp.int32) + (tok_index >= second_end).astype(
        jnp.int32
    )
    seq_begin = jnp.where(segment == 0, 0, jnp.where(segment == 1, first_end, second_end))
    return (segment, tok_index - seq_begin)


def rope_planes(tok_place):
    inverse = 10000.0 ** (-jnp.arange(0, ROT, 2, dtype=F32) / ROT)
    angles = tok_place.astype(F32)[:, None] * inverse[None, :]
    cosine, sine = jnp.cos(angles), jnp.sin(angles)
    rows = tok_place.shape[0]
    ones = jnp.ones((rows, HEAD - ROT), F32)
    none = jnp.zeros((rows, HEAD - ROT // 2), F32)
    gap = jnp.zeros((rows, ROT // 2), F32)
    return jnp.stack(
        [
            jnp.concatenate([cosine, cosine, ones], axis=1),
            jnp.concatenate([-sine, none], axis=1),
            jnp.concatenate([gap, sine, none[:, : HEAD - ROT]], axis=1),
        ]
    )


def norm_rows(values, gain_vec):
    inverse = lax.rsqrt(jnp.mean(values * values, axis=-1, keepdims=True) + EPSILON)
    return values * inverse * gain_vec


def norm_back(values, gain_vec, grads):
    _, pullback = jax.vjp(norm_rows, values, gain_vec)
    return pullback(grads)


def gelu_exact(values):
    return jax.nn.gelu(values, approximate=False)


def gelu_back(values, grads):
    _, pullback = jax.vjp(gelu_exact, values)
    return pullback(grads)[0]


def dot(left_op, right_op, left_dim=1, right_dim=0):
    return lax.dot_general(
        left_op, right_op, (((left_dim,), (right_dim,)), ((), ())), preferred_element_type=F32
    )


def wrap(value, extent):
    return lax.rem(value + extent, extent)


def tile(index, extent):
    return pl.ds(pl.multiple_of(index * extent, extent), extent)


class Plane:
    def __init__(self, nf):
        self.nf = nf
        self.chips = nf // 2
        self.me = lax.axis_index("fsdp")
        self.chip = self.me // 2
        self.core = lax.rem(self.me, 2)

    def on(self, step, other=0):
        core = 1 - self.core if other else self.core
        return wrap(self.chip + step, self.chips) * 2 + core


def greet(nf, ns=1):
    barrier = pltpu.get_barrier_semaphore()
    for axis, extent in (("fsdp", nf), ("seq", ns)):
        for step in range(1, extent):
            pl.semaphore_signal(
                barrier,
                inc=1,
                device_id={axis: wrap(lax.axis_index(axis) + step, extent)},
                device_id_type=MESH,
            )
    pl.semaphore_wait(barrier, nf - 1 + ns - 1)


def send(src, dst, sems, slot, axis, target):
    return pltpu.make_async_remote_copy(
        src_ref=src,
        dst_ref=dst,
        send_sem=sems[0].at[slot],
        recv_sem=sems[1].at[slot],
        device_id={axis: target},
        device_id_type=MESH,
    )


class Gather:
    def __init__(self, plane, buf, sems, base):
        self.plane, self.buf, self.sems, self.base = plane, buf, sems, base

    def direct(self, step, slot=None):
        slot = self.plane.me if slot is None else slot
        block = self.buf.at[slot]
        return send(
            block, block, self.sems, self.base + step - 1, "fsdp", self.plane.on(step)
        )

    def across(self, step, slot=None):
        slot = self.plane.on(-step) if slot is None else slot
        block = self.buf.at[slot]
        base = self.base + self.plane.chips - 1
        return send(block, block, self.sems, base + step, "fsdp", self.plane.on(0, 1))

    def start(self):
        for step in range(1, self.plane.chips):
            self.direct(step).start()
        self.across(0).start()

    def forward(self):
        for step in range(1, self.plane.chips):
            self.direct(step, self.plane.on(-step)).wait_recv()
            self.across(step).start()

    def finish(self):
        for step in range(self.plane.chips):
            self.across(step, self.plane.on(-step, 1)).wait_recv()

    def drain(self):
        for step in range(1, self.plane.chips):
            self.direct(step).wait_send()
        for step in range(self.plane.chips):
            self.across(step).wait_send()


def gather_sems(nf):
    return nf - 1


class Turn:
    def __init__(self, plane, rows_ref, full_ref, sems, base, chunks):
        self.plane, self.sems, self.base, self.chunks = plane, sems, base, chunks
        self.rows_ref, self.full_ref = rows_ref, full_ref
        self.height = rows_ref.shape[0]
        self.width = full_ref.shape[1]
        self.part = self.width // chunks

    def copy(self, chunk, step, source=None):
        nf = self.plane.nf
        target = wrap(self.plane.me + step, nf)
        source = self.plane.me if source is None else source
        begin = pl.multiple_of(target * self.width + chunk * self.part, self.part)
        return send(
            self.rows_ref.at[:, pl.ds(begin, self.part)],
            self.full_ref.at[tile(source, self.height), tile(chunk, self.part)],
            self.sems,
            self.base + chunk * (nf - 1) + step - 1,
            "fsdp",
            target,
        )

    def start(self, chunk):
        for step in range(1, self.plane.nf):
            self.copy(chunk, step).start()

    def own(self):
        self.full_ref[tile(self.plane.me, self.height), :] = self.rows_ref[
            :, tile(self.plane.me, self.width)
        ]

    def arrive(self, chunk):
        for step in range(1, self.plane.nf):
            self.copy(chunk, step, wrap(self.plane.me - step, self.plane.nf)).wait_recv()

    def drain(self, chunk):
        for step in range(1, self.plane.nf):
            self.copy(chunk, step).wait_send()


class Scatter:
    def __init__(self, plane, part, sib, rec, sems, base, chunks):
        self.plane, self.part, self.sib, self.rec = plane, part, sib, rec
        self.sems, self.base, self.chunks = sems, base, chunks
        self.width = part.shape[-1] // chunks

    def across(self, chunk, step):
        cols = tile(chunk, self.width)
        return send(
            self.part.at[self.plane.on(step, 1), :, cols],
            self.sib.at[wrap(self.plane.chip + step, self.plane.chips), :, cols],
            self.sems,
            self.base + chunk * (self.plane.nf - 1) + step,
            "fsdp",
            self.plane.on(0, 1),
        )

    def direct(self, chunk, step):
        cols = tile(chunk, self.width)
        return send(
            self.part.at[self.plane.on(step), :, cols],
            self.rec.at[step - 1, :, cols],
            self.sems,
            self.base + chunk * (self.plane.nf - 1) + self.plane.chips + step - 1,
            "fsdp",
            self.plane.on(step),
        )

    def start(self, chunk):
        for step in range(self.plane.chips):
            self.across(chunk, step).start()

    def combine(self, chunk):
        cols = tile(chunk, self.width)
        for step in range(1, self.plane.chips):
            chip = wrap(self.plane.chip + step, self.plane.chips)
            mine = self.plane.on(step)
            self.across(chunk, step).wait_recv()
            total = self.part[mine, :, cols].astype(F32) + self.sib[chip, :, cols].astype(F32)
            self.part[mine, :, cols] = total.astype(BF)
            self.direct(chunk, step).start()
        self.across(chunk, 0).wait_recv()

    def total(self, chunk):
        cols = tile(chunk, self.width)
        total = self.part[self.plane.me, :, cols].astype(F32)
        total += self.sib[self.plane.chip, :, cols].astype(F32)
        for step in range(1, self.plane.chips):
            self.direct(chunk, step).wait_recv()
            total += self.rec[step - 1, :, cols].astype(F32)
        return total

    def drain(self, chunk):
        for step in range(self.plane.chips):
            self.across(chunk, step).wait_send()
        for step in range(1, self.plane.chips):
            self.direct(chunk, step).wait_send()


def loop(extent, body):
    lax.fori_loop(0, extent, lambda i, c: (body(i), c)[1], 0)


def rows_of(ref3, begin, count):
    value = ref3[pl.ds(begin, count)]
    return value.reshape(count * value.shape[1], value.shape[2])


CHUNKS = 4


def mlp_kernel(
    nf,
    x_ref,
    g_ref,
    win_ref,
    wout_ref,
    gg_out,
    h_ref,
    dwin_ref,
    dwout_ref,
    dx_ref,
    xg,
    gg,
    wfull,
    dup,
    part,
    sib,
    rec,
    send_sem,
    recv_sem,
    copy_sem,
):
    plane = Plane(nf)
    sems = (send_sem, recv_sem)
    width = wfull.shape[1] // CHUNKS
    blocks = min(4, nf)
    tok = x_ref.shape[0]
    greet(nf)
    xg[plane.me] = x_ref[...]
    gg[plane.me] = g_ref[...]
    ag_x = Gather(plane, xg, sems, 0)
    ag_g = Gather(plane, gg, sems, nf - 1)
    turn = Turn(plane, win_ref, wfull, sems, 2 * (nf - 1), CHUNKS)
    scat = Scatter(plane, part, sib, rec, sems, (2 + CHUNKS) * (nf - 1), CHUNKS)
    ag_x.start()
    ag_g.start()
    turn.own()
    ag_x.forward()
    turn.start(0)
    ag_g.forward()
    for chunk in range(1, CHUNKS):
        turn.start(chunk)
    ag_x.finish()
    ag_g.finish()
    keep = pltpu.make_async_copy(gg, gg_out, copy_sem.at[0])
    keep.start()

    def mlp_chunk(chunk):
        turn.arrive(chunk)
        cols = tile(chunk, width)

        def rows_step(i):
            rows = tile(i, blocks * tok)
            up = dot(rows_of(xg, i * blocks, blocks), wfull[:, cols])
            dh = dot(rows_of(gg, i * blocks, blocks), wout_ref[cols, :], 1, 1)
            cdf = 0.5 * (1.0 + lax.erf(up * (0.5**0.5)))
            slope = cdf + up * jnp.exp(-0.5 * up * up) * 0.3989422804014327
            h_ref[rows, cols] = (up * cdf).astype(BF)
            dup[rows, cols] = (dh * slope).astype(BF)

        loop(nf // blocks, rows_step)

        def grad_step(i):
            feats = tile(i, 512)
            every = gg[:, :, feats].reshape(nf * tok, 512)
            dwout_ref[cols, feats] = dot(h_ref[:, cols], every, 0, 0).astype(BF)
            every = xg[:, :, feats].reshape(nf * tok, 512)
            dwin_ref[feats, cols] = dot(every, dup[:, cols], 0, 0).astype(BF)

        loop(D // 512, grad_step)

    loop(CHUNKS, mlp_chunk)

    def dx_chunk(chunk):
        feats = tile(chunk, D // CHUNKS)
        value = dot(dup[...], wfull[feats, :], 1, 1).astype(BF)
        part[:, :, feats] = value.reshape(nf, tok, D // CHUNKS)
        scat.start(chunk)

        @pl.when(chunk > 0)
        def _():
            scat.combine(chunk - 1)

    loop(CHUNKS, dx_chunk)
    scat.combine(CHUNKS - 1)

    def end_chunk(chunk):
        dx_ref[:, tile(chunk, D // CHUNKS)] = scat.total(chunk)
        scat.drain(chunk)
        turn.drain(chunk)

    loop(CHUNKS, end_chunk)
    ag_x.drain()
    ag_g.drain()
    keep.wait()


def rotated(value, planes):
    return value * planes[0] + pltpu.roll(value, HEAD - ROT // 2, 1) * planes[1] + pltpu.roll(
        value, ROT // 2, 1
    ) * planes[2]


def rotated_back(value, planes):
    return value * planes[0] - pltpu.roll(value, HEAD - ROT // 2, 1) * planes[1] - pltpu.roll(
        value, ROT // 2, 1
    ) * planes[2]


class Exchange:
    def __init__(self, ns, sems, base):
        self.ns, self.sems, self.base = ns, sems, base
        self.me = lax.axis_index("seq")

    def copy(self, src, dst, lane, step):
        return send(
            src,
            dst,
            self.sems,
            self.base + lane * (self.ns - 1) + step - 1,
            "seq",
            wrap(self.me + step, self.ns),
        )


def attend_kernel(
    nf,
    ns,
    x_refs,
    w_refs,
    wo_ref,
    planes_ref,
    gg_ref,
    lens_ref,
    xg_outs,
    wfull,
    att_ref,
    dq_ref,
    dk_ref,
    dv_ref,
    xg,
    gg,
    qkva,
    zin,
    zout,
    zback,
    dkv,
    send_sem,
    recv_sem,
    copy_sem,
):
    plane = Plane(nf)
    sems = (send_sem, recv_sem)
    tok = x_refs[0].shape[0]
    wide = wo_ref.shape[0]
    heads = wide // HEAD
    per = nf // ns
    slab = per * tok
    group_tok = ns * tok
    sq = lax.axis_index("seq")
    greet(nf, ns)
    load = pltpu.make_async_copy(gg_ref, gg, copy_sem.at[3])
    load.start()
    gathers = [Gather(plane, xg.at[i], sems, i * (nf - 1)) for i in range(3)]
    turns = [Turn(plane, w_refs[i], wfull.at[i], sems, (3 + i) * (nf - 1), 1) for i in range(3)]
    there = Exchange(ns, sems, 6 * (nf - 1))
    home = Exchange(ns, sems, 6 * (nf - 1) + 4 * (ns - 1))
    for i in range(3):
        xg[i, plane.me] = x_refs[i][...]
        gathers[i].start()
        turns[i].start(0)
        turns[i].own()

    def ship(i):
        for step in range(1, ns):
            target = wrap(sq + step, ns)
            there.copy(qkva.at[i, tile(target, slab), :], zin.at[i, sq], i, step).start()
        zin[i, sq] = qkva[i, tile(sq, slab), :]

    load.wait()

    def da_step(i):
        rows = tile(i, 4 * tok)
        qkva[3, rows, :] = dot(rows_of(gg, i * 4, 4), wo_ref[...], 1, 1).astype(BF)

    loop(nf // 4, da_step)
    ship(3)
    keeps = []
    for i in range(3):
        gathers[i].forward()
        turns[i].arrive(0)
        gathers[i].finish()
        keeps.append(pltpu.make_async_copy(xg.at[i], xg_outs[i], copy_sem.at[i]))
        keeps[i].start()

        def lin_step(r, i=i):
            rows = tile(r, 4 * tok)
            lin = dot(rows_of(xg.at[i], r * 4, 4), wfull[i])
            for head in range(heads):
                cols = slice(head * HEAD, head * HEAD + HEAD)
                piece = lin[:, cols]
                if i < 2:
                    piece = rotated(piece, [planes_ref[k, rows, :] for k in range(3)])
                qkva[i, rows, cols] = piece.astype(BF)

        loop(nf // 4, lin_step)
        ship(i)
    for i in range(4):
        for step in range(1, ns):
            there.copy(zin.at[i, 0], zin.at[i, wrap(sq - step, ns)], i, step).wait_recv()

    scale = HEAD ** (-0.5)
    queries = min(256, group_tok)
    q_slabs = queries // tok

    def pair_step(pair):
        grp = pair // heads
        head = lax.rem(pair, heads)
        cols = tile(head, HEAD)
        toks = tile(grp, tok)
        first_end = lens_ref[sq * per + grp, 0]
        second_end = first_end + lens_ref[sq * per + grp, 1]

        def part_of(i, begin, count):
            return zin[i, pl.ds(begin, count), toks, cols].reshape(count * tok, HEAD)

        keys, values = part_of(1, 0, ns), part_of(2, 0, ns)
        dkv[...] = jnp.zeros_like(dkv)

        def query_step(j):
            begin = j * q_slabs
            query, d_att = part_of(0, begin, q_slabs), part_of(3, begin, q_slabs)
            qi = j * queries + lax.broadcasted_iota(jnp.int32, (queries, group_tok), 0)
            ki = lax.broadcasted_iota(jnp.int32, (queries, group_tok), 1)
            seg_q = (qi >= first_end).astype(jnp.int32) + (qi >= second_end).astype(jnp.int32)
            seg_k = (ki >= first_end).astype(jnp.int32) + (ki >= second_end).astype(jnp.int32)
            allowed = (seg_q == seg_k) & (qi >= ki)
            scores = jnp.where(allowed, dot(query, keys, 1, 1) * scale, NEGATIVE)
            top = jnp.max(scores, axis=1, keepdims=True)
            expo = jnp.where(allowed, jnp.exp(scores - top), 0.0)
            prob = expo / jnp.sum(expo, axis=1, keepdims=True)
            prob_low = prob.astype(BF)
            attended = dot(prob_low, values)
            delta = jnp.sum(d_att.astype(F32) * attended, axis=1, keepdims=True)
            d_score = (prob * (dot(d_att, values, 1, 1) - delta)).astype(BF)
            d_query = dot(d_score, keys) * scale
            dkv[0] += dot(d_score, query, 0, 0)
            dkv[1] += dot(prob_low, d_att, 0, 0)
            where = pl.ds(begin, q_slabs)
            zout[0, where, toks, cols] = attended.astype(BF).reshape(q_slabs, tok, HEAD)
            zout[1, where, toks, cols] = d_query.astype(BF).reshape(q_slabs, tok, HEAD)

        loop(group_tok // queries, query_step)
        zout[2, :, toks, cols] = (dkv[0] * scale).astype(BF).reshape(ns, tok, HEAD)
        zout[3, :, toks, cols] = dkv[1].astype(BF).reshape(ns, tok, HEAD)

    loop(per * heads, pair_step)

    for i in range(4):
        for step in range(1, ns):
            target = wrap(sq + step, ns)
            home.copy(zout.at[i, target], zback.at[i, tile(sq, slab), :], i, step).start()
        zback[i, tile(sq, slab), :] = zout[i, sq]
    outs = (att_ref, dq_ref, dk_ref, dv_ref)
    for i in (1, 2, 3, 0):
        for step in range(1, ns):
            source = wrap(sq - step, ns)
            home.copy(zout.at[i, 0], zback.at[i, tile(source, slab), :], i, step).wait_recv()
        if i in (0, 3):
            outs[i][...] = zback[i]
        else:

            def back_step(r, i=i):
                rows = tile(r, tok)
                for head in range(heads):
                    cols = slice(head * HEAD, head * HEAD + HEAD)
                    piece = zback[i, rows, cols].astype(F32)
                    piece = rotated_back(piece, [planes_ref[k, rows, :] for k in range(3)])
                    outs[i][rows, cols] = piece.astype(BF)

            loop(nf, back_step)
    for i in range(3):
        gathers[i].drain()
        turns[i].drain(0)
        keeps[i].wait()
    for i in range(4):
        for step in range(1, ns):
            there.copy(zin.at[i, 0], zin.at[i, 0], i, step).wait_send()
            home.copy(zout.at[i, 0], zout.at[i, 0], i, step).wait_send()


def return_kernel(
    nf,
    att_ref,
    d_refs,
    wfull,
    wo_ref,
    wout_ref,
    h_ref,
    gg_ref,
    xg_refs,
    y_ref,
    dx_ref,
    dw_ref,
    dwo_ref,
    stage,
    part,
    sib,
    rec,
    send_sem,
    recv_sem,
    copy_sem,
    credit,
):
    plane = Plane(nf)
    sems = (send_sem, recv_sem)
    tok = y_ref.shape[0]
    parts, sibs = part.shape[0], sib.shape[0]
    greet(nf)
    sources = list(xg_refs) + [gg_ref]
    load = pltpu.make_async_copy(sources[0], stage, copy_sem)
    load.start()
    scats = [
        Scatter(
            plane,
            part.at[t % parts],
            sib.at[t % sibs],
            rec.at[t],
            sems,
            t * CHUNKS * (nf - 1),
            CHUNKS,
        )
        for t in range(4)
    ]
    for t in range(4):
        if t >= sibs:
            pl.semaphore_wait(credit, 1)

        def chunk_step(chunk, t=t):
            feats = tile(chunk, D // CHUNKS)
            if t >= parts:
                scats[t - parts].drain(chunk)
            if t < 3:
                value = dot(d_refs[t][...], wfull[t, feats, :], 1, 1)
            else:
                value = dot(att_ref[...], wo_ref[:, feats]) + dot(h_ref[...], wout_ref[:, feats])
            scats[t].part[:, :, feats] = value.astype(BF).reshape(nf, tok, D // CHUNKS)
            scats[t].start(chunk)

            @pl.when(chunk > 0)
            def _():
                scats[t].combine(chunk - 1)

        loop(CHUNKS, chunk_step)
        scats[t].combine(CHUNKS - 1)
        pltpu.make_async_copy(sources[t], stage, copy_sem).wait()

        def grad_step(i, t=t):
            feats = tile(i, 512)
            every = stage[:, :, feats].reshape(nf * tok, 512)
            if t < 3:
                dw_ref[t, feats, :] = dot(every, d_refs[t][...], 0, 0).astype(BF)
            else:
                dwo_ref[:, feats] = dot(att_ref[...], every, 0, 0).astype(BF)

        loop(D // 512, grad_step)
        if t < 3:
            pltpu.make_async_copy(sources[t + 1], stage, copy_sem).start()

        def total_step(chunk, t=t):
            feats = tile(chunk, D // CHUNKS)
            if t < 3:
                dx_ref[t, :, feats] = scats[t].total(chunk)
            else:
                y_ref[:, feats] = scats[t].total(chunk)

        loop(CHUNKS, total_step)
        if t + sibs < 4:
            pl.semaphore_signal(
                credit, inc=1, device_id={"fsdp": plane.on(0, 1)}, device_id_type=MESH
            )
    for t in range(4 - parts, 4):
        loop(CHUNKS, scats[t].drain)


def vmem():
    return pl.BlockSpec(memory_space=pltpu.VMEM)


def hbm():
    return pl.BlockSpec(memory_space=pltpu.HBM)


def shape(dims, dtype=BF):
    return jax.ShapeDtypeStruct(tuple(dims), dtype)


def params(ident, limit=62):
    return pltpu.CompilerParams(
        collective_id=ident, has_side_effects=True, vmem_limit_bytes=limit * MIB
    )


def run_mlp(nf, x_own, g_own, win, wout):
    tok = x_own.shape[0]
    hidden = wout.shape[0]
    chips = nf // 2
    count = (2 + 2 * CHUNKS) * (nf - 1)
    return pl.pallas_call(
        partial(mlp_kernel, nf),
        out_shape=(
            shape((nf, tok, D)),
            shape((nf * tok, hidden)),
            shape((D, hidden)),
            shape((hidden, D)),
            shape((tok, D), F32),
        ),
        in_specs=[vmem()] * 4,
        out_specs=(hbm(), vmem(), vmem(), vmem(), vmem()),
        scratch_shapes=[
            pltpu.VMEM((nf, tok, D), BF),
            pltpu.VMEM((nf, tok, D), BF),
            pltpu.VMEM((D, hidden), BF),
            pltpu.VMEM((nf * tok, hidden), BF),
            pltpu.VMEM((nf, tok, D), BF),
            pltpu.VMEM((chips, tok, D), BF),
            pltpu.VMEM((chips - 1, tok, D), BF),
            pltpu.SemaphoreType.DMA((count,)),
            pltpu.SemaphoreType.DMA((count,)),
            pltpu.SemaphoreType.DMA((1,)),
        ],
        compiler_params=params(1),
        name="mlp",
    )(x_own, g_own, win, wout)


def run_attend(nf, ns, xs, ws, wo, planes, gg, lens):
    tok = xs[0].shape[0]
    wide = wo.shape[0]
    count = 6 * (nf - 1) + 8 * (ns - 1)
    flat = shape((nf * tok, wide))

    def kernel(*refs):
        attend_kernel(
            nf, ns, refs[0:3], refs[3:6], *refs[6:10], refs[10:13], *refs[13:]
        )

    return pl.pallas_call(
        kernel,
        out_shape=(shape((nf, tok, D)),) * 3 + (shape((3, D, wide)), flat, flat, flat, flat),
        in_specs=[vmem()] * 8 + [hbm(), pl.BlockSpec(memory_space=pltpu.SMEM)],
        out_specs=(hbm(),) * 3 + (vmem(),) * 5,
        scratch_shapes=[
            pltpu.VMEM((3, nf, tok, D), BF),
            pltpu.VMEM((nf, tok, D), BF),
            pltpu.VMEM((4, nf * tok, wide), BF),
            pltpu.VMEM((4, ns, nf // ns * tok, wide), BF),
            pltpu.VMEM((4, ns, nf // ns * tok, wide), BF),
            pltpu.VMEM((4, nf * tok, wide), BF),
            pltpu.VMEM((2, ns * tok, HEAD), F32),
            pltpu.SemaphoreType.DMA((count,)),
            pltpu.SemaphoreType.DMA((count,)),
            pltpu.SemaphoreType.DMA((4,)),
        ],
        compiler_params=params(2),
        name="attend",
    )(*xs, *ws, wo, planes, gg, lens)


def run_return(nf, att, ds, wfull, wo, wout, h, gg, xgs):
    tok = gg.shape[1]
    wide = wo.shape[0]
    chips = nf // 2
    count = 4 * CHUNKS * (nf - 1)
    parts = 2 if nf <= 8 else 1

    def kernel(*refs):
        return_kernel(nf, refs[0], refs[1:4], *refs[4:9], refs[9:12], *refs[12:])

    return pl.pallas_call(
        kernel,
        out_shape=(
            shape((tok, D), F32),
            shape((3, tok, D), F32),
            shape((3, D, wide)),
            shape((wide, D)),
        ),
        in_specs=[vmem()] * 8 + [hbm()] * 4,
        out_specs=(vmem(),) * 4,
        scratch_shapes=[
            pltpu.VMEM((nf, tok, D), BF),
            pltpu.VMEM((parts, nf, tok, D), BF),
            pltpu.VMEM((2, chips, tok, D), BF),
            pltpu.VMEM((4, chips - 1, tok, D), BF),
            pltpu.SemaphoreType.DMA((count,)),
            pltpu.SemaphoreType.DMA((count,)),
            pltpu.SemaphoreType.DMA,
            pltpu.SemaphoreType.REGULAR,
        ],
        compiler_params=params(3),
        name="give_back",
    )(att, *ds, wfull, wo, wout, h, gg, *xgs)


def turn_back(nf, ns, grad):
    rows, cols = grad.shape
    piece = rows // nf // ns
    split = grad.reshape(nf, ns, piece, cols)
    split = lax.psum_scatter(split, "seq", scatter_dimension=1, tiled=True)
    split = lax.all_to_all(split, "fsdp", split_axis=0, concat_axis=0, tiled=True)
    whole = lax.all_gather(split, "seq", axis=1, tiled=True)
    return whole.transpose(1, 2, 0, 3).reshape(ns * piece, nf * cols)


def local(
    nf,
    ns,
    history,
    cotangent,
    seq_lengths,
    wq,
    wk,
    wv,
    wo,
    w_in,
    w_out,
    mix_in,
    mix_out,
    attn_gain,
    mlp_gain,
    mix_gain,
):
    entries = history[:, 0].astype(F32)
    tok_rows = entries.shape[1]
    lens = lax.all_gather(seq_lengths, "fsdp", axis=0, tiled=True)
    slab_index = lax.axis_index("seq") * tok_rows + jnp.arange(tok_rows, dtype=jnp.int32)
    every_index = jnp.tile(slab_index, nf)
    _, place = token_marks(every_index, jnp.repeat(lens, tok_rows, axis=0))
    planes = rope_planes(place)

    last_entry = entries[HIST - 1]
    mixed_low = norm_rows(last_entry, mix_gain).astype(BF)
    mix_in_low = mix_in.astype(BF)
    mix_out_low = mix_out.astype(BF)
    mix_pre = dot(mixed_low, mix_in_low)
    act_low = gelu_exact(mix_pre).astype(BF)
    mix_coef = dot(act_low, mix_out_low).reshape(tok_rows, STREAMS, HIST)
    stream = jnp.einsum("ncj,jnd->cnd", mix_coef, entries, precision=lax.Precision.HIGHEST)
    gains = (attn_gain, attn_gain, attn_gain, mlp_gain)
    normed = [norm_rows(stream[c], gains[c]).astype(BF) for c in range(STREAMS)]
    grad_out = cotangent[0]
    ws = [w.astype(BF) for w in (wq, wk, wv)]
    wo_low, win_low, wout_low = wo.astype(BF), w_in.astype(BF), w_out.astype(BF)

    gg, hidden, dwin, dwout, dx_r = run_mlp(nf, normed[3], grad_out, win_low, wout_low)
    *xgs, wfull, att, dq, dk, dv = run_attend(
        nf, ns, normed[:3], ws, wo_low, planes, gg, lens
    )
    y_sum, dx, dw, dwo = run_return(
        nf, att, (dq, dk, dv), wfull, wo_low, wout_low, hidden, gg, xgs
    )
    layer_out = (stream[3] + y_sum).astype(BF)[None]
    backs = [norm_back(stream[c], gains[c], dx[c] if c < 3 else dx_r) for c in range(STREAMS)]
    grad_stream = jnp.stack(
        [backs[0][0], backs[1][0], backs[2][0], backs[3][0] + grad_out.astype(F32)], axis=0
    )
    grad_coef = (
        jnp.einsum("cnd,jnd->ncj", grad_stream, entries, precision=lax.Precision.HIGHEST)
        .reshape(tok_rows, STREAMS * HIST)
        .astype(BF)
    )
    grad_entries = jnp.einsum(
        "ncj,cnd->jnd", mix_coef, grad_stream, precision=lax.Precision.HIGHEST
    )
    grad_pre = gelu_back(mix_pre, dot(grad_coef, mix_out_low, 1, 1)).astype(BF)
    grad_last, gain_mix = norm_back(last_entry, mix_gain, dot(grad_pre, mix_in_low, 1, 1))
    history_grad = jnp.concatenate(
        [grad_entries[: HIST - 1], (grad_entries[HIST - 1] + grad_last)[None]], axis=0
    ).astype(BF)[:, None]
    small = lax.psum(
        (
            dot(mixed_low, grad_pre, 0, 0),
            dot(act_low, grad_coef, 0, 0),
            backs[0][1] + backs[1][1] + backs[2][1],
            backs[3][1],
            gain_mix,
        ),
        ("seq", "fsdp"),
    )
    dw_in = turn_back(nf, ns, dwin).astype(F32)
    dw_qkv = [turn_back(nf, ns, dw[i]).astype(F32) for i in range(3)]
    dwout = lax.psum(dwout, "seq").astype(F32)
    dwo = lax.psum(dwo, "seq").astype(F32)
    return (layer_out, history_grad, *dw_qkv, dwo, dw_in, dwout, *small)


def solution(mesh):
    rows, rep = P("fsdp", None), P()
    in_specs = (
        P(None, "fsdp", "seq", None),
        P("fsdp", "seq", None),
    ) + (rows,) * 7 + (rep,) * 5
    out_specs = (
        P("fsdp", "seq", None),
        P(None, "fsdp", "seq", None),
    ) + (rows,) * 6 + (rep,) * 5
    body = partial(local, mesh.shape["fsdp"], mesh.shape["seq"])
    return jax.shard_map(body, mesh=mesh, in_specs=in_specs, out_specs=out_specs, check_vma=False)
```

time: 1930 us -> 1220 us (0.63)
  waiting for transfers between devices: 1350 us -> 500 us
  Pallas kernels: 0 us -> 433 us
  matrix products: 264 us -> 53.9 us
  local copies, waits for them, and re-layouts: 182 us -> 55.3 us
  blocking collectives: 46.7 us -> 103 us
    reduce_scatter x2 -> x0, waiting for transfers between devices: 549 us -> none  [the longest x1 388 us: local(): lax.psum_scatter(jnp.concatenate([contract_rows(left_op, right_op) for le...]
    all_gather x8 -> x4, waiting for transfers between devices: 443 us -> 0.01 us  [turn_back(): whole = lax.all_gather(split, 'seq', axis=1, tiled=True)]
    pallas_call x0 -> x3, Pallas kernels: none -> 433 us  [the longest x1 175 us: run_attend(): pl.pallas_call(kernel, out_shape=(shape((nf, tok, D)),) * 3 + (shape((3,...]
    unnamed x15 -> x7, waiting for transfers between devices: 0.25 us -> 433 us
    psum x2 -> x1, waiting for transfers between devices: 358 us -> 67.1 us  [local(): lax.psum((dot(mixed_low, grad_pre, 0, 0), dot(act_low, grad_coef, 0, 0),...]
    dot_general x30 -> x6, matrix products: 228 us -> 8.35 us  [dot(): lax.dot_general(left_op, right_op, (((left_dim,), (right_dim,)), ((), ())...]
    another operation x5 -> x2, local copies, waits for them, and re-layouts: 50.7 us -> 0.04 us  [the longest x1 0.04 us: rope_planes(): jnp.stack([jnp.concatenate([cosine, cosine, ones], axis=1), jnp.concatena...]
    all_to_all x0 -> x4, blocking collectives: none -> 49 us  [turn_back(): lax.all_to_all(split, 'fsdp', split_axis=0, concat_axis=0, tiled=True)]
  transfers between devices with their start and end apart: 14 -> 6, of which waited for: 12 -> 2; matrix products, arithmetic and copies ran while one was open for 25% -> 9% of each run, Pallas kernels for 0% -> 0%
where the time goes in v1:
time: 1220 us; the launch traced here: 1210 us
  waiting for transfers between devices  500 us (41%)
  Pallas kernels  433 us (35%)
  blocking collectives  103 us (8%)
  local copies, waits for them, and re-layouts  55.3 us (5%)
  matrix products  53.9 us (4%)
  other arithmetic  50.5 us (4%)
  between operations  16 us (1%)
    unnamed x7, waiting for transfers between devices  433 us
    pallas_call x1, Pallas kernels, run_attend(): pl.pallas_call(kernel, out_shape=(shape((nf, tok, D)),) * 3 + (shape((3,...  175 us
    pallas_call x1, Pallas kernels, run_mlp(): pl.pallas_call(partial(mlp_kernel, nf), out_shape=(shape((nf, tok, D)), s...  137 us
    pallas_call x1, Pallas kernels, run_return(): pl.pallas_call(kernel, out_shape=(shape((tok, D), F32), shape((3, tok, D)...  121 us
    psum x1, waiting for transfers between devices, local(): lax.psum((dot(mixed_low, grad_pre, 0, 0), dot(act_low, grad_coef, 0, 0),...  67.1 us
    all_to_all x4, blocking collectives, turn_back(): lax.all_to_all(split, 'fsdp', split_axis=0, concat_axis=0, tiled=True)  49 us
    psum x1, blocking collectives, local(): lax.psum((dot(mixed_low, grad_pre, 0, 0), dot(act_low, grad_coef, 0, 0),...  43.9 us
    unnamed x64, local copies, waits for them, and re-layouts  36.8 us
  transfers between devices with their start and end apart: 6, of which 2 were waited for; matrix products, arithmetic and copies ran while one was open for 9% of the time, Pallas kernels for 0%

profile of v1, /device:TPU:0, one launch (start us, length us, event | category | flops | bytes accessed | tf_op | source)
XLA Modules:
  0.0 1212.6 jit_solution(4153324576699094664)
XLA Ops:
  8.1 10.4 all-gather
  18.6 0.7 copy.91.refs_9_
  19.4 1.2 fusion.20
  20.8 2.4 multiply_convert_fusion.4
  23.2 0.8 fusion.51
  24.3 1.2 convert_element_type.130.refs_6_.refs_5_
  25.5 3.5 convert_element_type.127.refs_3_
  29.0 1.1 convert_element_type.128.refs_4_
  30.1 1.1 convert_element_type.129.refs_5_
  31.2 1.9 multiply_cosine_fusion
  33.2 2.8 convert_element_type.136.wout_ref.refs_6_
  36.0 0.5 slice-done
  37.0 12.4 %fusion.2 = f32[128,4,2048]{2,1,0:T(4,128)S(1)} fusion(f32[128,4,9]{2,1,0:T(4,128)S(1)} %copy.86, bf16[9,128,2048]{2,1,0:T(8,128)(2,1)S(1)} %bitcast.190), kind=kOutput, calls=%fused_computation.2 | convolution fusion | flops 113246208 | bytes 8931328 | tf_op jit(solution)/shard_map/ncj,jnd->cnd/dot_general | solution.py:821
  49.4 2.4 copy.134
  52.0 3.0 convert_element_type.135.win_ref
  55.1 0.9 multiply_convert_fusion.x_ref
  56.0 137.1 %mlp.1 = (bf16[8,128,2048]{2,1,0:T(8,128)(2,1)}, bf16[1024,1024]{1,0:T(8,128)(2,1)}, bf16[2048,1024]{1,0:T(8,128)(2,1)}, bf16[1024,2048]{1,0:T(8,128)(2,1)}, f32[128,2048]{1,0:T(8,128)}) custom-call(bf16[128,2048]{1,0:T(8,128)(2,1)} %multiply_convert_fusion.x_ref, bf16[128,2048]{1,0:T(8,128)(2,1)} %bitcast.207, ...), custom_call_target="tpu_custom_call" | custom-call | tf_op jit(solution)/shard_map/mlp/pallas_call | solution.py:682
  193.2 3.2 multiply_reduce_fusion
  196.8 1.2 pad_maximum_fusion.2.refs_7_
  198.0 1.3 multiply_convert_fusion.1
  199.4 175.3 %attend.1 = (bf16[8,128,2048]{2,1,0:T(8,128)(2,1)}, bf16[8,128,2048]{2,1,0:T(8,128)(2,1)}, bf16[8,128,2048]{2,1,0:T(8,128)(2,1)}, bf16[3,2048,256]{2,1,0:T(8,128...) custom-call(bf16[128,2048]{1,0:T(8,128)(2,1)} %get-tuple-element.142, ...), custom_call_target="tpu_custom_call" | custom-call | tf_op jit(solution)/shard_map/attend/pallas_call | solution.py:721
  374.6 120.9 %give_back.1 = (f32[128,2048]{1,0:T(8,128)}, f32[3,128,2048]{2,1,0:T(8,128)}, bf16[3,2048,256]{2,1,0:T(8,128)(2,1)}, bf16[256,2048]{1,0:T(8,128)(2,1)}) custom-call(bf16[1024,256]{1,0:T(8,128)(2,1)} %get-tuple-element.31.refs_0_, bf16[1024,256]{1,0:T(8,128)(2,1)} %get-tuple-element.32.refs_1_, bf16[1024,256]{1,0:T(8,128)(2,1)} %get-tuple-element.33.refs_2_, ...), custom_call_target="tpu_custom_call" | custom-call | tf_op jit(solution)/shard_map/give_back/pallas_call | solution.py:753
  495.6 3.6 fusion.62
  499.2 0.6 copy-done.14
  499.8 0.6 dynamic-slice
  500.4 432.6 %all-reduce.12.cloned.1.call-done = (bf16[8,4,64,256]{3,2,1,0:T(8,128)(2,1)}, bf16[8,4,64,256]{3,2,1,0:T(8,128)(2,1)}, bf16[8,4,64,256]{3,2,1,0:T(8,128)(2,1)}, ...) async-done(((bf16[8,4,64,256]{3,2,1,0:T(8,128)(2,1)}, bf16[8,4,64,256]{3,2,1,0:T(8,128)(2,1)}, ...) | async-done | bytes 12582928
  933.0 1.6 constant_dynamic-slice_fusion.1
  934.6 10.5 all_to_all.20
  945.2 1.9 constant_dynamic-slice_fusion.2
  947.1 10.0 all_to_all.21
  957.1 1.6 constant_dynamic-slice_fusion.3
  958.8 10.0 all_to_all.22
  968.9 2.0 constant_dynamic-slice_fusion
  970.8 18.5 %all_to_all.23 = bf16[8,1,64,1024]{3,2,1,0:T(8,128)(2,1)} all-to-all(bf16[8,1,64,1024]{3,2,1,0:T(8,128)(2,1)S(1)} %constant_dynamic-slice_fusion), channel_id=1, replica_groups=mesh['seq'=4,'fsdp'=8] {'fsdp'}, dimensions={0} | all-to-all | bytes 2097152 | tf_op jit(solution)/shard_map/all_to_all | solution.py:783
  989.6 5.1 fusion.29
  994.8 0.7 add_add_fusion.4
  995.8 2.0 copy-done.3
  997.9 13.6 %fusion.9 = bf16[128,4,9]{2,1,0:T(4,128)(2,1)S(1)} fusion(bf16[9,128,2048]{2,1,0:T(8,128)(2,1)S(1)} %bitcast.193, f32[4,128,2048]{2,1,0:T(8,128)S(1)} %pad_maximum_fusion.1), kind=kOutput, calls=%fused_computation.28 | convolution fusion | flops 113250816 | bytes 8922112 | tf_op jit(solution)/shard_map/cnd,jnd->ncj/dot_general | solution.py:841
  1011.8 2.3 fusion.41
  1014.3 2.4 fusion.15
  1016.7 19.6 %convolution_bitcast_fusion = f32[9,128,2048]{2,0,1:T(8,128)S(1)} fusion(f32[128,4,9]{2,1,0:T(4,128)S(1)} %copy.86, f32[4,128,2048]{2,1,0:T(8,128)} %copy-done.3), kind=kOutput, calls=%fused_computation.7 | convolution fusion | flops 113246208 | bytes 13649920 | tf_op jit(solution)/shard_map/ncj,cnd->jnd/dot_general | solution.py:845
  1036.3 0.7 slice.79
  1037.0 0.6 fusion.4
  1037.7 2.3 fusion.35
  1040.0 1.8 copy.97
  1041.8 3.1 pad_maximum_fusion
  1044.9 5.0 copy.102
  1049.9 43.9 %all-reduce.5 = (f32[100,36]{0,1:T(8,128)}, f32[2048]{0:T(1024)}, f32[2048]{0:T(1024)}, f32[2048]{0:T(1024)}) all-reduce(f32[100,36]{0,1:T(8,128)S(1)} %fusion.63, f32[2048]{0:T(1024)S(1)} %add_add_fusion.5, f32[2048]{0:T(1024)S(1)} %get-tuple-element.120, ...), channel_id=1, replica_groups=mesh['seq'=4,'fsdp'=8] {'seq','fsdp'}, use_global_device_ids=true, to_apply=%region_17.18 | all-reduce | flops 9744 | bytes 77952 | tf_op jit(solution)/shard_map/psum | solution.py:853
  1093.8 1.6 convert_element_type.151
  1095.3 6.7 convert_element_type.155
  1102.0 1.5 convert_bitcast_fusion.1
  1103.5 1.2 copy.100
  1104.7 2.2 copy.115
  1106.9 1.5 convert_bitcast_fusion.2
  1108.4 1.2 copy.99
  1109.6 2.2 copy.114
  1111.8 1.5 convert_bitcast_fusion.3
  1113.3 1.2 copy.98
  1114.5 2.2 copy.113
  1116.7 3.3 convert_bitcast_fusion
  1119.9 5.1 copy.101
  1125.0 11.0 copy.116
  1136.0 67.1 %all-reduce.10.cloned.1.call-done = f32[2048,100]{0,1:T(8,128)} async-done(((f32[2048,100]{0,1:T(8,128)}), f32[2048,100]{0,1:T(8,128)}) %all-reduce.10.cloned.1.call-update) | async-done | bytes 819216 | tf_op jit(solution)/shard_map/psum | solution.py:853
  1203.1 2.1 copy.143
  (101 shorter events, 3.2 us)
Async XLA Ops:
  8.0 16.2 %copy-start.5 = (f32[256,2048]{1,0:T(8,128)S(1)}, f32[256,2048]{1,0:T(8,128)}, u32[]{:S(2)}) copy-start(f32[256,2048]{1,0:T(8,128)} %param.20) | copy-start | bytes 6291460
  8.0 925.0 %all-reduce.12.cloned.1.call-start = ((), (), s32[]{:S(2)}) async-start(), calls=%async_computation.9 | async-start | bytes 25165824
  24.3 4.7 copy-start.6
  24.3 5.8 copy-start.7
  24.3 8.9 slice-start.4
  29.0 4.2 slice-start.5
  33.1 3.4 slice-start
  33.2 3.7 slice-start.1
  36.0 16.0 %slice-start.6 = ((s8[8388608]{0:T(1024)(128)(4,1)}), s8[4194304]{0:T(1024)(128)(4,1)S(1)}, s32[]{:S(2)}) async-start(s8[8388608]{0:T(1024)(128)(4,1)} %bitcast.197), calls=%async_computation.16 | async-start | bytes 8388608
  37.0 15.0 %slice-start.7 = ((s8[8388608]{0:T(1024)(128)(4,1)}), s8[4194304]{0:T(1024)(128)(4,1)S(1)}, s32[]{:S(2)}) async-start(s8[8388608]{0:T(1024)(128)(4,1)} %bitcast.197), calls=%async_computation.17 | async-start | bytes 8388608
  51.8 3.3 copy-start
  52.0 3.1 copy-start.10
  193.1 4.9 copy-start.1
  193.1 4.9 copy-start.11
  499.2 0.7 copy-start.14
  499.2 602.8 %all-gather.10.cloned.1.call-start = ((), (), s32[]{:S(2)}) async-start(), calls=%async_computation.6 | async-start | bytes 1310720 | tf_op jit(solution)/shard_map/all_gather | solution.py:784
  945.1 44.5 %copy-start.4 = (f32[3,128,2048]{2,1,0:T(8,128)S(1)}, f32[3,128,2048]{2,1,0:T(8,128)}, u32[]{:S(2)}) copy-start(f32[3,128,2048]{2,1,0:T(8,128)} %get-tuple-element.41) | copy-start | bytes 9437188
  945.2 161.7 %all-gather.8.cloned.1.call-start = ((), (), s32[]{:S(2)}) async-start(), calls=%async_computation.5 | async-start | bytes 1310720 | tf_op jit(solution)/shard_map/all_gather | solution.py:784
  957.1 154.7 %all-gather.6.cloned.1.call-start = ((), (), s32[]{:S(2)}) async-start(), calls=%async_computation.4 | async-start | bytes 1310720 | tf_op jit(solution)/shard_map/all_gather | solution.py:784
  968.8 147.9 %all-gather.12.cloned.1.call-start = ((), (), s32[]{:S(2)}) async-start(), calls=%async_computation.7 | async-start | bytes 5242880 | tf_op jit(solution)/shard_map/all_gather | solution.py:784
  989.4 213.8 %all-reduce.10.cloned.1.call-start = ((), (), s32[]{:S(2)}) async-start(), calls=%async_computation.8 | async-start | bytes 1703936 | tf_op jit(solution)/shard_map/psum | solution.py:853
  989.6 5.1 copy-start.2
  989.6 8.2 slice-start.2
  994.7 3.1 slice-start.3
  995.8 2.0 copy-start.3
  997.8 13.8 %copy-start.13 = (f32[100,36]{0,1:T(8,128)S(1)}, f32[100,36]{0,1:T(8,128)}, u32[]{:S(2)}) copy-start(f32[100,36]{0,1:T(8,128)} %param.24) | copy-start | bytes 43204
  997.8 13.8 %copy-start.15 = (f32[128,100]{0,1:T(8,128)S(1)}, f32[128,100]{0,1:T(8,128)}, u32[]{:S(2)}) copy-start(f32[128,100]{0,1:T(8,128)} %get-tuple-element.136) | copy-start | bytes 153604
  997.8 13.8 %copy-start.16 = (f32[128,100]{0,1:T(8,128)S(1)}, f32[128,100]{0,1:T(8,128)}, u32[]{:S(2)}) copy-start(f32[128,100]{0,1:T(8,128)} %get-tuple-element.151) | copy-start | bytes 153604
  997.8 14.0 %copy-start.12 = (f32[2048]{0:T(1024)S(1)}, f32[2048]{0:T(1024)}, u32[]{:S(2)}) copy-start(f32[2048]{0:T(1024)} %param.27) | copy-start | bytes 24580
  997.8 16.5 %copy-start.9 = (f32[2048,100]{0,1:T(8,128)S(1)}, f32[2048,100]{0,1:T(8,128)}, u32[]{:S(2)}) copy-start(f32[2048,100]{0,1:T(8,128)} %param.23) | copy-start | bytes 2457604
  1044.9 48.9 %copy-start.8 = (bf16[256,2048]{1,0:T(8,128)(2,1)S(1)}, bf16[256,2048]{1,0:T(8,128)(2,1)}, u32[]{:S(2)}) copy-start(bf16[256,2048]{1,0:T(8,128)(2,1)} %get-tuple-element.132) | copy-start | bytes 3145732
Sparse Core Ops, SparseCore 0:
  499.3 433.6 all-reduce.11
  945.3 25.0 all-gather.9
  972.0 27.4 all-gather.7
  1000.8 28.7 all-gather.5
  1031.0 81.5 all-gather.11
Sparse Core Ops, SparseCore 1:
  1014.3 188.8 all-reduce.9

commit v2 on v1

--- a/solution.py
+++ b/solution.py
@@ -775,14 +775,575 @@
     )(att, *ds, wfull, wo, wout, h, gg, *xgs)
 
 
-def turn_back(nf, ns, grad):
+ROWS = 16
+WIDTH = 512
+
+
+def start_kernel(
+    hist_ref,
+    mix_in_ref,
+    mix_out_ref,
+    again_ref,
+    mgain_ref,
+    xgain_ref,
+    low_ref,
+    st_ref,
+    coef_ref,
+    inv_ref,
+    pre_ref,
+    act_ref,
+    mixed_ref,
+):
+    tok = hist_ref.shape[1]
+
+    def mix_step(i):
+        rows = tile(i, ROWS)
+        value = hist_ref[HIST - 1, rows, :].astype(F32)
+        inv = lax.rsqrt(jnp.mean(value * value, axis=1, keepdims=True) + EPSILON)
+        mixed_ref[rows, :] = (value * inv * xgain_ref[...]).astype(BF)
+        inv_ref[STREAMS, rows, :] = inv
+
+    loop(tok // ROWS, mix_step)
+    pre = dot(mixed_ref[...], mix_in_ref[...].astype(BF))
+    pre_ref[...] = pre
+    act = (0.5 * pre * (1.0 + lax.erf(pre * (0.5**0.5)))).astype(BF)
+    act_ref[...] = act
+    coef_ref[...] = dot(act, mix_out_ref[...].astype(BF))
+
+    def stream_step(i):
+        rows = tile(i, ROWS)
+        coef = coef_ref[rows, :]
+        squares = [jnp.zeros((ROWS, 1), F32)] * STREAMS
+        for begin in range(0, D, WIDTH):
+            cols = slice(begin, begin + WIDTH)
+            total = [jnp.zeros((ROWS, WIDTH), F32)] * STREAMS
+            for j in range(HIST):
+                entry = hist_ref[j, rows, cols].astype(F32)
+                for c in range(STREAMS):
+                    at = c * HIST + j
+                    total[c] = total[c] + coef[:, at : at + 1] * entry
+            for c in range(STREAMS):
+                st_ref[c, rows, cols] = total[c]
+                squares[c] = squares[c] + jnp.sum(total[c] * total[c], axis=1, keepdims=True)
+        for c in range(STREAMS):
+            inv = lax.rsqrt(squares[c] / D + EPSILON)
+            inv_ref[c, rows, :] = inv
+            gain = mgain_ref if c == STREAMS - 1 else again_ref
+            low_ref[c, rows, :] = (st_ref[c, rows, :] * inv * gain[...]).astype(BF)
+
+    loop(tok // ROWS, stream_step)
+
+
+def run_start(hist, mix_in, mix_out, again, mgain, xgain):
+    tok = hist.shape[1]
+    hidden = mix_in.shape[1]
+    return pl.pallas_call(
+        start_kernel,
+        out_shape=(
+            shape((STREAMS, tok, D)),
+            shape((STREAMS, tok, D), F32),
+            shape((tok, STREAMS * HIST), F32),
+            shape((STREAMS + 1, tok, 1), F32),
+            shape((tok, hidden), F32),
+            shape((tok, hidden)),
+            shape((tok, D)),
+        ),
+        in_specs=[vmem()] * 6,
+        out_specs=(vmem(),) * 7,
+        compiler_params=pltpu.CompilerParams(vmem_limit_bytes=62 * MIB),
+        name="streams",
+    )(hist, mix_in, mix_out, again, mgain, xgain)
+
+
+SMALL = 112
+
+
+def end_kernel(
+    hist_ref,
+    st_ref,
+    dx_ref,
+    dxr_ref,
+    g_ref,
+    y_ref,
+    coef_ref,
+    inv_ref,
+    pre_ref,
+    act_ref,
+    mixed_ref,
+    mix_in_ref,
+    mix_out_ref,
+    again_ref,
+    mgain_ref,
+    xgain_ref,
+    hg_ref,
+    lo_ref,
+    sm_ref,
+    ds,
+    last,
+    dmixed,
+    dcoef,
+    gsum,
+):
+    tok = hist_ref.shape[1]
+    gsum[...] = jnp.zeros_like(gsum)
+
+    def back(value, inv, gain, grad):
+        scaled = grad * gain
+        mean = jnp.sum(value * scaled, axis=1, keepdims=True) / D
+        return inv * scaled - value * (inv * inv * inv * mean)
+
+    def row_step(i):
+        rows = tile(i, ROWS)
+        coef = coef_ref[rows, :]
+        lane = lax.broadcasted_iota(jnp.int32, (ROWS, STREAMS * HIST), 1)
+        for c in range(STREAMS):
+            value, inv = st_ref[c, rows, :], inv_ref[c, rows, :]
+            grad = dxr_ref[rows, :] if c == STREAMS - 1 else dx_ref[c, rows, :]
+            gain = mgain_ref if c == STREAMS - 1 else again_ref
+            gsum[c // 3] += grad * (value * inv)
+            d_value = back(value, inv, gain[...], grad)
+            if c == STREAMS - 1:
+                d_value = d_value + g_ref[rows, :].astype(F32)
+                lo_ref[rows, :] = (value + y_ref[rows, :]).astype(BF)
+            ds[c] = d_value
+        found = jnp.zeros((ROWS, STREAMS * HIST), F32)
+        for j in range(HIST):
+            sums = [jnp.zeros((ROWS, 128), F32)] * STREAMS
+            for begin in range(0, D, WIDTH):
+                cols = slice(begin, begin + WIDTH)
+                entry = hist_ref[j, rows, cols].astype(F32)
+                grad = jnp.zeros((ROWS, WIDTH), F32)
+                for c in range(STREAMS):
+                    at = c * HIST + j
+                    value = ds[c, :, cols]
+                    grad = grad + coef[:, at : at + 1] * value
+                    product = value * entry
+                    for k in range(0, WIDTH, 128):
+                        sums[c] = sums[c] + product[:, k : k + 128]
+                if j < HIST - 1:
+                    hg_ref[j, rows, cols] = grad.astype(BF)
+                else:
+                    last[rows, cols] = grad
+            for c in range(STREAMS):
+                value = jnp.sum(sums[c], axis=1, keepdims=True)
+                found = jnp.where(lane == c * HIST + j, value, found)
+        dcoef[rows, :] = found.astype(BF)
+
+    loop(tok // ROWS, row_step)
+    mix_in, mix_out = mix_in_ref[...].astype(BF), mix_out_ref[...].astype(BF)
+    pre, d_coef = pre_ref[...], dcoef[...]
+    slope = 0.5 * (1.0 + lax.erf(pre * (0.5**0.5)))
+    slope = slope + pre * jnp.exp(-0.5 * pre * pre) * 0.3989422804014327
+    d_pre = (dot(d_coef, mix_out, 1, 1) * slope).astype(BF)
+    hidden = pre.shape[1]
+    sm_ref[0:hidden, :] = dot(d_pre, mixed_ref[...], 0, 0)
+    dmixed[...] = dot(d_pre, mix_in, 1, 1)
+
+    def last_step(i):
+        rows = tile(i, ROWS)
+        value, inv, grad = hist_ref[HIST - 1, rows, :].astype(F32), inv_ref[STREAMS, rows, :], dmixed[rows, :]
+        gsum[2] += grad * (value * inv)
+        total = last[rows, :] + back(value, inv, xgain_ref[...], grad)
+        hg_ref[HIST - 1, rows, :] = total.astype(BF)
+
+    loop(tok // ROWS, last_step)
+    for k in range(3):
+        sm_ref[hidden + k : hidden + k + 1, :] = jnp.sum(gsum[k], axis=0, keepdims=True)
+    begin = hidden + 3
+    sm_ref[begin:SMALL, :] = jnp.zeros((SMALL - begin, D), F32)
+    turned = dot(d_coef, act_ref[...], 0, 0)
+    for k in range(STREAMS * HIST):
+        at = begin + k // STREAMS
+        cols = slice(k % STREAMS * 128, k % STREAMS * 128 + hidden)
+        sm_ref[at : at + 1, cols] = turned[k : k + 1, :]
+
+
+def run_end(*args):
+    tok = args[0].shape[1]
+    return pl.pallas_call(
+        end_kernel,
+        out_shape=(shape((HIST, tok, D)), shape((tok, D)), shape((SMALL, D), F32)),
+        in_specs=[vmem()] * 16,
+        out_specs=(vmem(),) * 3,
+        scratch_shapes=[
+            pltpu.VMEM((STREAMS, ROWS, D), F32),
+            pltpu.VMEM((tok, D), F32),
+            pltpu.VMEM((tok, D), F32),
+            pltpu.VMEM((tok, STREAMS * HIST), BF),
+            pltpu.VMEM((3, ROWS, D), F32),
+        ],
+        compiler_params=pltpu.CompilerParams(vmem_limit_bytes=62 * MIB),
+        name="streams_back",
+    )(*args)
+
+
+class Line:
+    def __init__(self, plane, ns, part, inward, swap, res, sems, base, turned):
+        self.plane, self.ns, self.turned = plane, ns, turned
+        self.part, self.inward, self.swap, self.res = part, inward, swap, res
+        self.sems, self.base = sems, base
+        self.me = lax.axis_index("seq")
+        self.side = self.me // (ns // 2)
+        middle = ns // 2 - 1
+        self.depth = (1 - self.side) * (middle - self.me) + self.side * (self.me - middle - 1)
+        self.ends = middle
+        self.in_to = self.me + 1 - 2 * self.side
+        self.out_to = self.me - 1 + 2 * self.side
+        self.other = ns - 1 - self.me
+        self.count = part.shape[0]
+
+    @staticmethod
+    def slots(nf, turned):
+        return 5 + (nf - 1 if turned else 0)
+
+    def sem(self, chunk, kind):
+        return self.base + chunk * self.slots(self.plane.nf, self.turned) + kind
+
+    def half(self, ref, chunk, side):
+        rows = ref.shape[-2] // 2
+        rows = pl.ds(pl.multiple_of(side * rows, rows), rows)
+        return ref.at[chunk, :, rows, :]
+
+    def inner(self, chunk, src):
+        return send(
+            src.at[chunk], self.inward.at[chunk], self.sems, self.sem(chunk, 0), "seq", self.in_to
+        )
+
+    def cross(self, chunk):
+        return send(
+            self.half(self.inward, chunk, 1 - self.side),
+            self.swap.at[chunk],
+            self.sems,
+            self.sem(chunk, 1),
+            "seq",
+            self.other,
+        )
+
+    def result(self):
+        return self.res if self.turned else self.part
+
+    def back_cross(self, chunk):
+        return send(
+            self.half(self.result(), chunk, self.side),
+            self.half(self.res, chunk, self.side),
+            self.sems,
+            self.sem(chunk, 2),
+            "seq",
+            self.other,
+        )
+
+    def outer(self, chunk, side, src):
+        return send(
+            self.half(src, chunk, side),
+            self.half(self.res, chunk, side),
+            self.sems,
+            self.sem(chunk, 3) + side,
+            "seq",
+            self.out_to,
+        )
+
+    def spread(self, chunk, step):
+        rows = self.part.shape[-2] // 2
+        rows = pl.ds(pl.multiple_of(self.side * rows, rows), rows)
+        target = wrap(self.plane.me + step, self.plane.nf)
+        return send(
+            self.part.at[chunk, target, rows, :],
+            self.res.at[chunk, self.plane.me, rows, :],
+            self.sems,
+            self.sem(chunk, 4) + step,
+            "fsdp",
+            target,
+        )
+
+    def keep(self, chunk, sem):
+        if self.turned:
+            rows = self.part.shape[-2] // 2
+            rows = pl.ds(pl.multiple_of(self.side * rows, rows), rows)
+            me = self.plane.me
+            src, dst = self.part.at[chunk, me, rows, :], self.res.at[chunk, me, rows, :]
+        else:
+            src = self.half(self.part, chunk, self.side)
+            dst = self.half(self.res, chunk, self.side)
+        return pltpu.make_async_copy(src, dst, sem.at[chunk])
+
+    def begin(self, chunk):
+        if self.ends:
+
+            @pl.when(self.depth == self.ends)
+            def _():
+                self.inner(chunk, self.part).start()
+
+    def relay(self, chunk, hop):
+        @pl.when(self.depth == self.ends - hop)
+        def _():
+            self.inner(chunk, self.part).wait_recv()
+            total = self.inward[chunk].astype(F32) + self.part[chunk].astype(F32)
+            self.inward[chunk] = total.astype(BF)
+            self.inner(chunk, self.inward).start()
+
+    def meet(self, chunk):
+        @pl.when(self.depth == 0)
+        def _():
+            self.inner(chunk, self.part).wait_recv()
+            theirs = self.half(self.inward, chunk, 1 - self.side)
+            mine = self.half(self.part, chunk, 1 - self.side)
+
+            def step(i):
+                rows = tile(i, 16)
+                total = theirs[:, rows, :].astype(F32) + mine[:, rows, :].astype(F32)
+                theirs[:, rows, :] = total.astype(BF)
+
+            loop(theirs.shape[1] // 16, step)
+            self.cross(chunk).start()
+
+    def settle(self, chunk, sem):
+        @pl.when(self.depth == 0)
+        def _():
+            self.cross(chunk).wait_recv()
+            theirs = self.half(self.inward, chunk, self.side)
+            mine = self.half(self.part, chunk, self.side)
+
+            def step(i):
+                rows = tile(i, 16)
+                total = theirs[:, rows, :].astype(F32) + mine[:, rows, :].astype(F32)
+                total += self.swap[chunk, :, rows, :].astype(F32)
+                mine[:, rows, :] = total.astype(BF)
+
+            loop(theirs.shape[1] // 16, step)
+            self.keep(chunk, sem).start()
+            if self.turned:
+                for k in range(1, self.plane.nf):
+                    self.spread(chunk, k).start()
+            else:
+                self.hand_out(chunk)
+
+    def hand_out(self, chunk):
+        self.back_cross(chunk).start()
+        if self.ends:
+            self.outer(chunk, self.side, self.result()).start()
+
+    def spread_end(self, chunk, sem):
+        @pl.when(self.depth == 0)
+        def _():
+            for k in range(1, self.plane.nf):
+                self.spread(chunk, k).wait_recv()
+            self.keep(chunk, sem).wait()
+            self.hand_out(chunk)
+
+    def pass_on(self, chunk):
+        @pl.when(self.depth == 0)
+        def _():
+            self.back_from(chunk).wait_recv()
+            if self.ends:
+                self.outer(chunk, 1 - self.side, self.res).start()
+
+    def back_from(self, chunk):
+        return send(
+            self.half(self.result(), chunk, 1 - self.side),
+            self.half(self.res, chunk, 1 - self.side),
+            self.sems,
+            self.sem(chunk, 2),
+            "seq",
+            self.other,
+        )
+
+    def outward_hop(self, chunk, hop):
+        @pl.when(self.depth == hop)
+        def _():
+            for side in range(2):
+                self.outer(chunk, side, self.res).wait_recv()
+                if hop < self.ends:
+                    self.outer(chunk, side, self.res).start()
+
+    def phases(self, sem):
+        listed = [self.begin]
+        listed += [partial(self.relay, hop=hop) for hop in range(1, self.ends)]
+        listed += [self.meet, partial(self.settle, sem=sem)]
+        if self.turned:
+            listed += [partial(self.spread_end, sem=sem)]
+        listed += [self.pass_on]
+        listed += [partial(self.outward_hop, hop=hop) for hop in range(1, self.ends + 1)]
+        return listed
+
+    def drain(self, chunk, sem):
+        @pl.when(self.depth == 0)
+        def _():
+            self.cross(chunk).wait_send()
+            self.back_cross(chunk).wait_send()
+            if self.turned:
+                for k in range(1, self.plane.nf):
+                    self.spread(chunk, k).wait_send()
+            else:
+                self.keep(chunk, sem).wait()
+
+        if self.ends:
+
+            @pl.when(self.depth < self.ends)
+            def _():
+                for side in range(2):
+                    self.outer(chunk, side, self.res).wait_send()
+
+            @pl.when(self.depth > 0)
+            def _():
+                self.inner(chunk, self.part).wait_send()
+
+
+class Ticks:
+    def __init__(self, jobs):
+        self.jobs = jobs
+        self.now = 0
+
+    def tick(self, upto=None):
+        upto = len(self.jobs) if upto is None else upto
+        late = [
+            (i, self.now - i)
+            for i in range(len(self.jobs))
+            if 0 <= self.now - i < len(self.jobs[i][0].phases(self.jobs[i][2]))
+        ]
+        for i, phase in late:
+            line, chunk, sem = self.jobs[i]
+            line.phases(sem)[phase](chunk)
+        self.now += 1
+        return bool(late)
+
+    def finish(self):
+        while self.tick():
+            pass
+        for line, chunk, sem in self.jobs:
+            line.drain(chunk, sem)
+
+
+def sum_kernel(nf, ns, counts, turned, *refs):
+    kinds = len(counts)
+    ins, sm_ref, outs = refs[:kinds], refs[kinds], refs[kinds + 1 : 2 * kinds + 1]
+    sm_out = refs[2 * kinds + 1]
+    scratch = refs[2 * kinds + 2 :]
+    inward, swap = scratch[:kinds], scratch[kinds : 2 * kinds]
+    send_sem, recv_sem, copy_sem = scratch[2 * kinds : 2 * kinds + 3]
+    sm_in, sm_z, sm_sem, sm_rsem = scratch[2 * kinds + 3 :]
+    plane = Plane(nf)
+    greet(nf, ns)
+    jobs, base, copies = [], 0, 0
+    for k in range(kinds):
+        line = Line(
+            plane, ns, ins[k], inward[k], swap[k], outs[k], (send_sem, recv_sem), base, turned[k]
+        )
+        base += counts[k] * Line.slots(nf, turned[k])
+        for chunk in range(counts[k]):
+            jobs.append((line, chunk, copy_sem.at[pl.ds(copies, counts[k])]))
+        copies += counts[k]
+    ticks = Ticks(jobs)
+    small = Small(plane, ns, sm_ref, sm_in, sm_z, sm_out, (sm_sem, sm_rsem))
+    ticks.tick()
+    small.start()
+    ticks.tick()
+    ticks.tick()
+    small.across()
+    ticks.tick()
+    ticks.tick()
+    small.finish()
+    ticks.finish()
+    small.drain()
+
+
+class Small:
+    def __init__(self, plane, ns, src, mid, line, out, sems):
+        self.plane, self.ns, self.src, self.mid, self.line, self.out = plane, ns, src, mid, line, out
+        self.sems = sems
+        self.me = lax.axis_index("seq")
+
+    def scatter(self, step):
+        target = wrap(self.plane.me + step, self.plane.nf)
+        return send(
+            self.src.at[target], self.mid.at[self.plane.me], self.sems, step - 1, "fsdp", target
+        )
+
+    def along(self, step):
+        me = self.line.at[self.me]
+        slot = self.plane.nf - 1 + step - 1
+        return send(me, me, self.sems, slot, "seq", wrap(self.me + step, self.ns))
+
+    def spread(self, step):
+        me = self.out.at[self.plane.me]
+        slot = self.plane.nf - 1 + self.ns - 1 + step - 1
+        return send(me, me, self.sems, slot, "fsdp", wrap(self.plane.me + step, self.plane.nf))
+
+    def start(self):
+        self.mid[self.plane.me] = self.src[self.plane.me]
+        for step in range(1, self.plane.nf):
+            self.scatter(step).start()
+
+    def across(self):
+        for step in range(1, self.plane.nf):
+            self.scatter(step).wait_recv()
+        total = self.mid[0]
+        for k in range(1, self.plane.nf):
+            total += self.mid[k]
+        self.line[self.me] = total
+        for step in range(1, self.ns):
+            self.along(step).start()
+
+    def finish(self):
+        for step in range(1, self.ns):
+            self.along(step).wait_recv()
+        total = self.line[0]
+        for k in range(1, self.ns):
+            total += self.line[k]
+        self.out[self.plane.me] = total
+        for step in range(1, self.plane.nf):
+            self.spread(step).start()
+
+    def drain(self):
+        for step in range(1, self.plane.nf):
+            self.spread(step).wait_recv()
+        for step in range(1, self.plane.nf):
+            self.scatter(step).wait_send()
+            self.spread(step).wait_send()
+        for step in range(1, self.ns):
+            self.along(step).wait_send()
+
+
+def run_sums(nf, ns, parts, turned, small):
+    counts = [p.shape[0] for p in parts]
+    total = sum(n * Line.slots(nf, t) for n, t in zip(counts, turned))
+    kinds = len(parts)
+    few = 2 * (nf - 1) + ns - 1
+    halves = [(p.shape[0], p.shape[1], p.shape[2] // 2, p.shape[3]) for p in parts]
+    cols = D // nf
+    split = small.reshape(SMALL, nf, cols).transpose(1, 0, 2)
+    outs = pl.pallas_call(
+        partial(sum_kernel, nf, ns, counts, turned),
+        out_shape=tuple(shape(p.shape) for p in parts) + (shape((nf, SMALL, cols), F32),),
+        in_specs=[vmem()] * (kinds + 1),
+        out_specs=(hbm(),) * kinds + (vmem(),),
+        scratch_shapes=[pltpu.VMEM(p.shape, BF) for p in parts]
+        + [pltpu.VMEM(h, BF) for h in halves]
+        + [pltpu.SemaphoreType.DMA((total,))] * 2
+        + [pltpu.SemaphoreType.DMA((sum(counts),))]
+        + [
+            pltpu.VMEM((nf, SMALL, cols), F32),
+            pltpu.VMEM((ns, SMALL, cols), F32),
+            pltpu.SemaphoreType.DMA((few,)),
+            pltpu.SemaphoreType.DMA((few,)),
+        ],
+        compiler_params=params(4),
+        name="sums",
+    )(*parts, split)
+    return outs[:-1], outs[-1].transpose(1, 0, 2).reshape(SMALL, D)
+
+
+def natural_chunks(grad):
+    return grad.reshape(grad.shape[0] // 128, 1, 128, grad.shape[1])
+
+
+def turned_chunks(nf, grad):
     rows, cols = grad.shape
-    piece = rows // nf // ns
-    split = grad.reshape(nf, ns, piece, cols)
-    split = lax.psum_scatter(split, "seq", scatter_dimension=1, tiled=True)
-    split = lax.all_to_all(split, "fsdp", split_axis=0, concat_axis=0, tiled=True)
-    whole = lax.all_gather(split, "seq", axis=1, tiled=True)
-    return whole.transpose(1, 2, 0, 3).reshape(ns * piece, nf * cols)
+    return grad.reshape(nf, rows // nf, cols // 128, 128).transpose(2, 0, 1, 3)
+
+
+def turned_rows(parts):
+    chunks, nf, rows, cols = parts.shape
+    return parts.transpose(2, 1, 0, 3).reshape(rows, nf * chunks * cols)
 
 
 def local(
@@ -803,68 +1364,51 @@
     mlp_gain,
     mix_gain,
 ):
-    entries = history[:, 0].astype(F32)
-    tok_rows = entries.shape[1]
+    hist = history[:, 0]
+    tok_rows = hist.shape[1]
     lens = lax.all_gather(seq_lengths, "fsdp", axis=0, tiled=True)
     slab_index = lax.axis_index("seq") * tok_rows + jnp.arange(tok_rows, dtype=jnp.int32)
     every_index = jnp.tile(slab_index, nf)
     _, place = token_marks(every_index, jnp.repeat(lens, tok_rows, axis=0))
     planes = rope_planes(place)
-
-    last_entry = entries[HIST - 1]
-    mixed_low = norm_rows(last_entry, mix_gain).astype(BF)
-    mix_in_low = mix_in.astype(BF)
-    mix_out_low = mix_out.astype(BF)
-    mix_pre = dot(mixed_low, mix_in_low)
-    act_low = gelu_exact(mix_pre).astype(BF)
-    mix_coef = dot(act_low, mix_out_low).reshape(tok_rows, STREAMS, HIST)
-    stream = jnp.einsum("ncj,jnd->cnd", mix_coef, entries, precision=lax.Precision.HIGHEST)
-    gains = (attn_gain, attn_gain, attn_gain, mlp_gain)
-    normed = [norm_rows(stream[c], gains[c]).astype(BF) for c in range(STREAMS)]
+    gains = [g[None] for g in (attn_gain, mlp_gain, mix_gain)]
+    low, stream, coef, inv, pre, act, mixed = run_start(hist, mix_in, mix_out, *gains)
     grad_out = cotangent[0]
     ws = [w.astype(BF) for w in (wq, wk, wv)]
     wo_low, win_low, wout_low = wo.astype(BF), w_in.astype(BF), w_out.astype(BF)
 
-    gg, hidden, dwin, dwout, dx_r = run_mlp(nf, normed[3], grad_out, win_low, wout_low)
+    gg, hidden, dwin, dwout, dx_r = run_mlp(nf, low[3], grad_out, win_low, wout_low)
     *xgs, wfull, att, dq, dk, dv = run_attend(
-        nf, ns, normed[:3], ws, wo_low, planes, gg, lens
+        nf, ns, [low[c] for c in range(3)], ws, wo_low, planes, gg, lens
     )
     y_sum, dx, dw, dwo = run_return(
         nf, att, (dq, dk, dv), wfull, wo_low, wout_low, hidden, gg, xgs
     )
-    layer_out = (stream[3] + y_sum).astype(BF)[None]
-    backs = [norm_back(stream[c], gains[c], dx[c] if c < 3 else dx_r) for c in range(STREAMS)]
-    grad_stream = jnp.stack(
-        [backs[0][0], backs[1][0], backs[2][0], backs[3][0] + grad_out.astype(F32)], axis=0
+    history_grad, layer_out, small = run_end(
+        hist, stream, dx, dx_r, grad_out, y_sum, coef, inv, pre, act, mixed, mix_in, mix_out, *gains
     )
-    grad_coef = (
-        jnp.einsum("cnd,jnd->ncj", grad_stream, entries, precision=lax.Precision.HIGHEST)
-        .reshape(tok_rows, STREAMS * HIST)
-        .astype(BF)
+    parts = [natural_chunks(dwout), turned_chunks(nf, dwin)]
+    parts += [turned_chunks(nf, dw[i]) for i in range(3)] + [natural_chunks(dwo)]
+    sums, small = run_sums(nf, ns, parts, (False, True, True, True, True, False), small)
+    dwout = sums[0].reshape(w_out.shape).astype(F32)
+    dwo = sums[5].reshape(wo.shape).astype(F32)
+    dw_in = turned_rows(sums[1]).astype(F32)
+    dw_qkv = [turned_rows(sums[2 + i]).astype(F32) for i in range(3)]
+    units = mix_in.shape[1]
+    mix_out_rows = small[units + 3 :, : STREAMS * 128].reshape(HIST * STREAMS, 128)
+    return (
+        layer_out[None],
+        history_grad[:, None],
+        *dw_qkv,
+        dwo,
+        dw_in,
+        dwout,
+        small[:units].T,
+        mix_out_rows[:, :units].T,
+        small[units],
+        small[units + 1],
+        small[units + 2],
     )
-    grad_entries = jnp.einsum(
-        "ncj,cnd->jnd", mix_coef, grad_stream, precision=lax.Precision.HIGHEST
-    )
-    grad_pre = gelu_back(mix_pre, dot(grad_coef, mix_out_low, 1, 1)).astype(BF)
-    grad_last, gain_mix = norm_back(last_entry, mix_gain, dot(grad_pre, mix_in_low, 1, 1))
-    history_grad = jnp.concatenate(
-        [grad_entries[: HIST - 1], (grad_entries[HIST - 1] + grad_last)[None]], axis=0
-    ).astype(BF)[:, None]
-    small = lax.psum(
-        (
-            dot(mixed_low, grad_pre, 0, 0),
-            dot(act_low, grad_coef, 0, 0),
-            backs[0][1] + backs[1][1] + backs[2][1],
-            backs[3][1],
-            gain_mix,
-        ),
-        ("seq", "fsdp"),
-    )
-    dw_in = turn_back(nf, ns, dwin).astype(F32)
-    dw_qkv = [turn_back(nf, ns, dw[i]).astype(F32) for i in range(3)]
-    dwout = lax.psum(dwout, "seq").astype(F32)
-    dwo = lax.psum(dwo, "seq").astype(F32)
-    return (layer_out, history_grad, *dw_qkv, dwo, dw_in, dwout, *small)
 
 
 def solution(mesh):

time: 1220 us -> 900 us (0.74)
  waiting for transfers between devices: 500 us -> 0 us
  Pallas kernels: 433 us -> 792 us
  blocking collectives: 103 us -> 10.4 us
  matrix products: 53.9 us -> 0 us
  other arithmetic: 50.5 us -> 33.1 us
  between operations: 16 us -> 0.89 us
    unnamed x7 -> x0, waiting for transfers between devices: 433 us -> none
    pallas_call x0 -> x3, Pallas kernels: none -> 359 us  [the longest x1 328 us: run_sums(): pl.pallas_call(partial(sum_kernel, nf, ns, counts, turned), out_shape=tup...]
    psum x1 -> x0, waiting for transfers between devices: 67.1 us -> none  [local(): lax.psum((dot(mixed_low, grad_pre, 0, 0), dot(act_low, grad_coef, 0, 0),...]
    dot_general x9 -> x0, matrix products: 53.9 us -> none  [the longest x1 19.6 us: local(): jnp.einsum('ncj,cnd->jnd', mix_coef, grad_stream, precision=lax.Precision...]
    all_to_all x4 -> x0, blocking collectives: 49 us -> none  [turn_back(): lax.all_to_all(split, 'fsdp', split_axis=0, concat_axis=0, tiled=True)]
    psum x1 -> x0, blocking collectives: 43.9 us -> none  [local(): lax.psum((dot(mixed_low, grad_pre, 0, 0), dot(act_low, grad_coef, 0, 0),...]
    unnamed x64 -> x36, local copies, waits for them, and re-layouts: 36.8 us -> 27.5 us
  transfers between devices with their start and end apart: 6 -> 0, of which waited for: 2 -> 0; matrix products, arithmetic and copies ran while one was open for 9% -> 0% of each run, Pallas kernels for 0% -> 0%
where the time goes in v2:
time: 900 us; the launch traced here: 899 us
  Pallas kernels  792 us (88%)
  local copies, waits for them, and re-layouts  62.9 us (7%)
  other arithmetic  33.1 us (4%)
  blocking collectives  10.4 us (1%)
    pallas_call x1, Pallas kernels, run_sums(): pl.pallas_call(partial(sum_kernel, nf, ns, counts, turned), out_shape=tup...  328 us
    pallas_call x1, Pallas kernels, run_attend(): pl.pallas_call(kernel, out_shape=(shape((nf, tok, D)),) * 3 + (shape((3,...  175 us
    pallas_call x1, Pallas kernels, run_mlp(): pl.pallas_call(partial(mlp_kernel, nf), out_shape=(shape((nf, tok, D)), s...  137 us
    pallas_call x1, Pallas kernels, run_return(): pl.pallas_call(kernel, out_shape=(shape((tok, D), F32), shape((3, tok, D)...  121 us
    unnamed x36, local copies, waits for them, and re-layouts  27.5 us
    pallas_call x1, Pallas kernels, run_end(): pl.pallas_call(end_kernel, out_shape=(shape((HIST, tok, D)), shape((tok,...  19.3 us

profile of v2, /device:TPU:0, one launch (start us, length us, event | category | flops | bytes accessed | tf_op | source)
XLA Modules:
  0.0 899.1 jit_solution(6412741664155864363)
XLA Ops:
  0.6 0.0 copy-start.7
  0.7 0.0 copy-start.1
  0.7 0.1 pad.9.clone
  0.8 0.1 pad.6.clone
  0.9 10.4 %all-gather = s32[8,1,3]{2,1,0:T(1,128)S(1)} all-gather(s32[1,1,3]{2,1,0:T(1,128)} %bitcast.131), channel_id=1, replica_groups=mesh['seq'=4,'fsdp'=8] {'fsdp'}, dimensions={0}, use_global_device_ids=true | all-gather | bytes 108 | tf_op jit(solution)/shard_map/all_gather | solution.py:1369
  11.3 0.1 copy.86
  11.4 0.7 copy.88.refs_9_
  12.1 0.1 broadcast_bitcast_fusion
  12.2 1.4 copy.85.mix_out_ref
  13.6 2.8 convert_element_type.81.refs_6_.refs_5_
  16.4 0.0 copy-done.7
  16.4 1.3 copy.84.mix_in_ref
  17.7 0.0 copy-done.1
  17.7 1.1 convert_element_type.78.refs_3_
  18.8 3.6 convert_element_type.79.refs_4_
  22.4 1.1 convert_element_type.80.refs_5_
  23.6 1.9 multiply_cosine_fusion
  25.5 0.3 maximum_bitcast_fusion
  25.9 0.0 slice-start.2
  25.9 1.2 pad_maximum_fusion.refs_7_
  27.1 2.8 convert_element_type.86.wout_ref.refs_6_
  29.9 0.0 slice-done.2
  29.9 1.7 slice-done.3
  31.6 2.6 convert_element_type.85.win_ref
  34.2 11.2 %streams.1 = (bf16[4,128,2048]{2,1,0:T(8,128)(2,1)}, f32[4,128,2048]{2,1,0:T(8,128)}, f32[128,36]{1,0:T(8,128)}, f32[5,128,1]{2,1,0:T(8,128)}, f32[128,100]{1,0:...) custom-call(bf16[9,128,2048]{2,1,0:T(8,128)(2,1)} %bitcast.90, f32[2048,100]{1,0:T(8,128)} %copy.84.mix_in_ref, ...), custom_call_target="tpu_custom_call" | custom-call | tf_op jit(solution)/shard_map/streams/pallas_call | solution.py:840
  45.4 2.9 slice_bitcast_fusion
  48.2 136.6 %mlp.1 = (bf16[8,128,2048]{2,1,0:T(8,128)(2,1)}, bf16[1024,1024]{1,0:T(8,128)(2,1)}, bf16[2048,1024]{1,0:T(8,128)(2,1)}, bf16[1024,2048]{1,0:T(8,128)(2,1)}, f32[128,2048]{1,0:T(8,128)}) custom-call(bf16[128,2048]{1,0:T(8,128)(2,1)} %get-tuple-element.136.x_ref, bf16[128,2048]{1,0:T(8,128)(2,1)} %bitcast.111, ...), custom_call_target="tpu_custom_call" | custom-call | tf_op jit(solution)/shard_map/mlp/pallas_call | solution.py:682
  184.9 3.3 copy.119
  188.1 3.1 copy.127
  191.2 175.2 %attend.1 = (bf16[8,128,2048]{2,1,0:T(8,128)(2,1)}, bf16[8,128,2048]{2,1,0:T(8,128)(2,1)}, bf16[8,128,2048]{2,1,0:T(8,128)(2,1)}, bf16[3,2048,256]{2,1,0:T(8,128...) custom-call(bf16[128,2048]{1,0:T(8,128)(2,1)} %get-tuple-element.139, ...), custom_call_target="tpu_custom_call" | custom-call | tf_op jit(solution)/shard_map/attend/pallas_call | solution.py:721
  366.4 121.0 %give_back.1 = (f32[128,2048]{1,0:T(8,128)}, f32[3,128,2048]{2,1,0:T(8,128)}, bf16[3,2048,256]{2,1,0:T(8,128)(2,1)}, bf16[256,2048]{1,0:T(8,128)(2,1)}) custom-call(bf16[1024,256]{1,0:T(8,128)(2,1)} %get-tuple-element.50.refs_0_, bf16[1024,256]{1,0:T(8,128)(2,1)} %get-tuple-element.51.refs_1_, bf16[1024,256]{1,0:T(8,128)(2,1)} %get-tuple-element.52.refs_2_, ...), custom_call_target="tpu_custom_call" | custom-call | tf_op jit(solution)/shard_map/give_back/pallas_call | solution.py:753
  487.5 19.3 %streams_back.1 = (bf16[9,128,2048]{2,1,0:T(8,128)(2,1)}, bf16[128,2048]{1,0:T(8,128)(2,1)}, f32[112,2048]{1,0:T(8,128)}) custom-call(bf16[9,128,2048]{2,1,0:T(8,128)(2,1)} %bitcast.91, f32[4,128,2048]{2,1,0:T(8,128)} %get-tuple-element.47.st_ref, f32[3,128,2048]{2,1,0:T(8,128)} %get-tuple-element.59.dx_ref, f32[128,2048]{1,0:T(8,128)} %get-tuple-element.60.dxr_ref, ...), custom_call_target="tpu_custom_call" | custom-call | tf_op jit(solution)/shard_map/streams_back/pallas_call | solution.py:963
  506.8 2.2 copy.131
  509.0 3.0 fusion.4
  512.0 1.3 reshape.101
  513.3 1.2 copy.128
  514.5 0.3 reshape.100
  514.8 1.2 copy.129
  516.0 0.3 reshape.99
  516.3 1.2 copy.130
  517.4 328.4 %sums.1 = (bf16[8,1,128,2048]{3,2,1,0:T(8,128)(2,1)}, bf16[8,8,256,128]{3,2,1,0:T(8,128)(2,1)}, bf16[2,8,256,128]{3,2,1,0:T(8,128)(2,1)}, bf16[2,8,256,128]{3,2,...) custom-call(bf16[8,1,128,2048]{3,2,1,0:T(8,128)(2,1)} %bitcast.101, ...), custom_call_target="tpu_custom_call" | custom-call | tf_op jit(solution)/shard_map/sums/pallas_call | solution.py:1314
  845.9 1.6 fusion.5
  847.4 1.3 slice.73
  848.7 0.3 copy.103
  849.0 0.1 pad.10
  849.1 1.2 copy.120
  850.3 0.1 copy.117
  850.4 0.6 slice_bitcast_fusion.4
  851.0 0.0 copy-done.6
  851.0 0.2 convert_bitcast_fusion.3
  851.2 1.8 copy.99
  853.0 3.0 copy.106
  856.0 0.2 convert_bitcast_fusion.2
  856.2 1.8 copy.100
  858.0 3.0 copy.107
  861.0 0.2 convert_bitcast_fusion.1
  861.2 1.8 copy.101
  863.0 3.0 copy.108
  866.0 0.0 copy-done.3
  866.0 1.6 bitcast_convert_fusion.1
  867.6 6.7 convert_bitcast_fusion
  874.3 9.2 %copy.102 = f32[256,8,8,128]{0,3,2,1:T(8,128)} copy(f32[256,8,8,128]{3,0,1,2:T(8,128)} %convert_bitcast_fusion) | data formatting | bytes 16777216 | tf_op jit(solution)/shard_map/convert_element_type | solution.py:1395
  883.5 8.9 copy.109
  892.4 6.7 bitcast_convert_fusion
  (29 shorter events, 0.1 us)
Async XLA Ops:
  0.6 15.7 %copy-start.7 = (f32[2048,100]{0,1:T(8,128)S(1)}, f32[2048,100]{0,1:T(8,128)}, u32[]{:S(2)}) copy-start(f32[2048,100]{0,1:T(8,128)} %param.23) | copy-start | bytes 2457604
  0.7 17.1 %copy-start.1 = (f32[256,2048]{1,0:T(8,128)S(1)}, f32[256,2048]{1,0:T(8,128)}, u32[]{:S(2)}) copy-start(f32[256,2048]{1,0:T(8,128)} %param.17) | copy-start | bytes 6291460
  17.7 4.7 copy-start.2
  17.7 9.4 %slice-start = ((s8[8388608]{0:T(1024)(128)(4,1)}), s8[4194304]{0:T(1024)(128)(4,1)S(1)}, s32[]{:S(2)}) async-start(s8[8388608]{0:T(1024)(128)(4,1)} %bitcast.94), calls=%async_computation | async-start | bytes 8388608
  22.4 4.7 slice-start.1
  25.9 4.1 slice-start.2
  27.1 4.5 slice-start.3
  847.4 2.8 copy-start
  848.7 2.3 copy-start.6
  853.0 3.0 copy-start.5
  858.0 3.0 copy-start.4
  863.0 3.0 copy-start.3

commit v3 on v1

v3 whole, which is shorter than its diff:
```python
from functools import partial

import jax
import jax.numpy as jnp
from jax import lax
from jax.experimental import pallas as pl
from jax.experimental.pallas import tpu as pltpu
from jax.sharding import PartitionSpec as P

D = 2048
HEADS = 16
HEAD = 128
ROT = 32
HIST = 9
STREAMS = 4
EPSILON = 1e-05
NEGATIVE = -1e30
MESH = pl.DeviceIdType.MESH
BF = jnp.bfloat16
F32 = jnp.float32
MIB = 2**20


CHUNKS = 4
LANES = 128
SLOTS = 4
EARLY = 3


def token_marks(tok_index, lengths):
    first_end = lengths[..., 0]
    second_end = first_end + lengths[..., 1]
    segment = (tok_index >= first_end).astype(jnp.int32) + (tok_index >= second_end).astype(
        jnp.int32
    )
    seq_begin = jnp.where(segment == 0, 0, jnp.where(segment == 1, first_end, second_end))
    return (segment, tok_index - seq_begin)


def rope_planes(tok_place):
    inverse = 10000.0 ** (-jnp.arange(0, ROT, 2, dtype=F32) / ROT)
    angles = tok_place.astype(F32)[:, None] * inverse[None, :]
    cosine, sine = jnp.cos(angles), jnp.sin(angles)
    rows = tok_place.shape[0]
    ones = jnp.ones((rows, HEAD - ROT), F32)
    none = jnp.zeros((rows, HEAD - ROT // 2), F32)
    gap = jnp.zeros((rows, ROT // 2), F32)
    return jnp.stack(
        [
            jnp.concatenate([cosine, cosine, ones], axis=1),
            jnp.concatenate([-sine, none], axis=1),
            jnp.concatenate([gap, sine, none[:, : HEAD - ROT]], axis=1),
        ]
    )


def dot(left_op, right_op, left_dim=1, right_dim=0):
    return lax.dot_general(
        left_op, right_op, (((left_dim,), (right_dim,)), ((), ())), preferred_element_type=F32
    )


def wrap(value, extent):
    return lax.rem(value + extent, extent)


def tile(index, extent):
    return pl.ds(pl.multiple_of(index * extent, extent), extent)


class Plane:
    def __init__(self, nf):
        self.nf = nf
        self.chips = nf // 2
        self.me = lax.axis_index("fsdp")
        self.chip = self.me // 2
        self.core = lax.rem(self.me, 2)

    def on(self, step, other=0):
        core = 1 - self.core if other else self.core
        return wrap(self.chip + step, self.chips) * 2 + core


def greet(nf, ns=1):
    barrier = pltpu.get_barrier_semaphore()
    for axis, extent in (("fsdp", nf), ("seq", ns)):
        for step in range(1, extent):
            pl.semaphore_signal(
                barrier,
                inc=1,
                device_id={axis: wrap(lax.axis_index(axis) + step, extent)},
                device_id_type=MESH,
            )
    pl.semaphore_wait(barrier, nf - 1 + ns - 1)


def send(src, dst, sems, slot, axis, target):
    return pltpu.make_async_remote_copy(
        src_ref=src,
        dst_ref=dst,
        send_sem=sems[0].at[slot],
        recv_sem=sems[1].at[slot],
        device_id={axis: target},
        device_id_type=MESH,
    )


class Gather:
    def __init__(self, plane, own, buf, sems, base):
        self.plane, self.own, self.buf, self.sems, self.base = plane, own, buf, sems, base

    def direct(self, step, slot=None):
        dst = self.buf.at[self.plane.me if slot is None else slot]
        src = self.own if slot is None else dst
        return send(src, dst, self.sems, self.base + step - 1, "fsdp", self.plane.on(step))

    def across(self, step, slot=None):
        slot = self.plane.on(-step) if slot is None else slot
        block = self.buf.at[slot]
        src = block if step else self.own
        base = self.base + self.plane.chips - 1
        return send(src, block, self.sems, base + step, "fsdp", self.plane.on(0, 1))

    def start(self):
        for step in range(1, self.plane.chips):
            self.direct(step).start()
        self.across(0).start()

    def keep(self, sem):
        return pltpu.make_async_copy(self.own, self.buf.at[self.plane.me], sem)

    def forward(self):
        for step in range(1, self.plane.chips):
            self.direct(step, self.plane.on(-step)).wait_recv()
            self.across(step).start()

    def finish(self):
        for step in range(self.plane.chips):
            self.across(step, self.plane.on(-step, 1)).wait_recv()

    def drain(self):
        for step in range(1, self.plane.chips):
            self.direct(step).wait_send()
        for step in range(self.plane.chips):
            self.across(step).wait_send()


class Turn:
    def __init__(self, plane, rows_ref, full_ref, sems, base, chunks):
        self.plane, self.sems, self.base, self.chunks = plane, sems, base, chunks
        self.rows_ref, self.full_ref = rows_ref, full_ref
        self.height = rows_ref.shape[0]
        self.width = full_ref.shape[1]
        self.part = self.width // chunks

    def copy(self, chunk, step, source=None):
        nf = self.plane.nf
        target = wrap(self.plane.me + step, nf)
        source = self.plane.me if source is None else source
        begin = pl.multiple_of(target * self.width + chunk * self.part, self.part)
        return send(
            self.rows_ref.at[:, pl.ds(begin, self.part)],
            self.full_ref.at[tile(source, self.height), tile(chunk, self.part)],
            self.sems,
            self.base + chunk * (nf - 1) + step - 1,
            "fsdp",
            target,
        )

    def start(self, chunk):
        for step in range(1, self.plane.nf):
            self.copy(chunk, step).start()

    def keep(self, sem):
        return pltpu.make_async_copy(
            self.rows_ref.at[:, tile(self.plane.me, self.width)],
            self.full_ref.at[tile(self.plane.me, self.height), :],
            sem,
        )

    def arrive(self, chunk):
        for step in range(1, self.plane.nf):
            self.copy(chunk, step, wrap(self.plane.me - step, self.plane.nf)).wait_recv()

    def drain(self, chunk):
        for step in range(1, self.plane.nf):
            self.copy(chunk, step).wait_send()


class Scatter:
    def __init__(self, plane, part, sib, rec, sems, base, chunks):
        self.plane, self.part, self.sib, self.rec = plane, part, sib, rec
        self.sems, self.base, self.chunks = sems, base, chunks
        self.width = part.shape[-1] // chunks

    def across(self, chunk, step):
        cols = tile(chunk, self.width)
        return send(
            self.part.at[self.plane.on(step, 1), :, cols],
            self.sib.at[wrap(self.plane.chip + step, self.plane.chips), :, cols],
            self.sems,
            self.base + chunk * (self.plane.nf - 1) + step,
            "fsdp",
            self.plane.on(0, 1),
        )

    def direct(self, chunk, step):
        cols = tile(chunk, self.width)
        return send(
            self.part.at[self.plane.on(step), :, cols],
            self.rec.at[step - 1, :, cols],
            self.sems,
            self.base + chunk * (self.plane.nf - 1) + self.plane.chips + step - 1,
            "fsdp",
            self.plane.on(step),
        )

    def start(self, chunk):
        for step in range(self.plane.chips):
            self.across(chunk, step).start()

    def combine(self, chunk):
        cols = tile(chunk, self.width)
        for step in range(1, self.plane.chips):
            chip = wrap(self.plane.chip + step, self.plane.chips)
            mine = self.plane.on(step)
            self.across(chunk, step).wait_recv()
            total = self.part[mine, :, cols].astype(F32) + self.sib[chip, :, cols].astype(F32)
            self.part[mine, :, cols] = total.astype(BF)
            self.direct(chunk, step).start()
        self.across(chunk, 0).wait_recv()

    def total(self, chunk):
        cols = tile(chunk, self.width)
        total = self.part[self.plane.me, :, cols].astype(F32)
        total += self.sib[self.plane.chip, :, cols].astype(F32)
        for step in range(1, self.plane.chips):
            self.direct(chunk, step).wait_recv()
            total += self.rec[step - 1, :, cols].astype(F32)
        return total

    def drain(self, chunk):
        for step in range(self.plane.chips):
            self.across(chunk, step).wait_send()
        for step in range(1, self.plane.chips):
            self.direct(chunk, step).wait_send()


def loop(extent, body):
    lax.fori_loop(0, extent, lambda i, c: (body(i), c)[1], 0)


def rows_of(ref3, begin, count):
    value = ref3[pl.ds(begin, count)]
    return value.reshape(count * value.shape[1], value.shape[2])


def vmem():
    return pl.BlockSpec(memory_space=pltpu.VMEM)


def hbm():
    return pl.BlockSpec(memory_space=pltpu.HBM)


def shape(dims, dtype=BF):
    return jax.ShapeDtypeStruct(tuple(dims), dtype)


def params(ident, limit=62):
    return pltpu.CompilerParams(
        collective_id=ident, has_side_effects=True, vmem_limit_bytes=limit * MIB
    )


ROWS = 16
WIDTH = 512


def start_kernel(
    hist_ref,
    mix_in_ref,
    mix_out_ref,
    again_ref,
    mgain_ref,
    xgain_ref,
    low_ref,
    st_ref,
    coef_ref,
    inv_ref,
    pre_ref,
    act_ref,
    mixed_ref,
):
    tok = hist_ref.shape[1]

    def mix_step(i):
        rows = tile(i, ROWS)
        value = hist_ref[HIST - 1, rows, :].astype(F32)
        inv = lax.rsqrt(jnp.mean(value * value, axis=1, keepdims=True) + EPSILON)
        mixed_ref[rows, :] = (value * inv * xgain_ref[...]).astype(BF)
        inv_ref[STREAMS, rows, :] = inv

    loop(tok // ROWS, mix_step)
    pre = dot(mixed_ref[...], mix_in_ref[...].astype(BF))
    pre_ref[...] = pre
    act = (0.5 * pre * (1.0 + lax.erf(pre * (0.5**0.5)))).astype(BF)
    act_ref[...] = act
    coef_ref[...] = dot(act, mix_out_ref[...].astype(BF))

    def stream_step(i):
        rows = tile(i, ROWS)
        coef = coef_ref[rows, :]
        squares = [jnp.zeros((ROWS, 1), F32)] * STREAMS
        for begin in range(0, D, WIDTH):
            cols = slice(begin, begin + WIDTH)
            total = [jnp.zeros((ROWS, WIDTH), F32)] * STREAMS
            for j in range(HIST):
                entry = hist_ref[j, rows, cols].astype(F32)
                for c in range(STREAMS):
                    at = c * HIST + j
                    total[c] = total[c] + coef[:, at : at + 1] * entry
            for c in range(STREAMS):
                st_ref[c, rows, cols] = total[c]
                squares[c] = squares[c] + jnp.sum(total[c] * total[c], axis=1, keepdims=True)
        for c in range(STREAMS):
            inv = lax.rsqrt(squares[c] / D + EPSILON)
            inv_ref[c, rows, :] = inv
            gain = mgain_ref if c == STREAMS - 1 else again_ref
            low_ref[c, rows, :] = (st_ref[c, rows, :] * inv * gain[...]).astype(BF)

    loop(tok // ROWS, stream_step)


def run_start(hist, mix_in, mix_out, again, mgain, xgain):
    tok = hist.shape[1]
    hidden = mix_in.shape[1]
    return pl.pallas_call(
        start_kernel,
        out_shape=(
            shape((STREAMS, tok, D)),
            shape((STREAMS, tok, D), F32),
            shape((tok, STREAMS * HIST), F32),
            shape((STREAMS + 1, tok, 1), F32),
            shape((tok, hidden), F32),
            shape((tok, hidden)),
            shape((tok, D)),
        ),
        in_specs=[vmem()] * 6,
        out_specs=(vmem(),) * 7,
        compiler_params=pltpu.CompilerParams(vmem_limit_bytes=62 * MIB),
        name="streams",
    )(hist, mix_in, mix_out, again, mgain, xgain)


def rotated(value, planes):
    return value * planes[0] + pltpu.roll(value, HEAD - ROT // 2, 1) * planes[1] + pltpu.roll(
        value, ROT // 2, 1
    ) * planes[2]


def rotated_back(value, planes):
    return value * planes[0] - pltpu.roll(value, HEAD - ROT // 2, 1) * planes[1] - pltpu.roll(
        value, ROT // 2, 1
    ) * planes[2]


class Exchange:
    def __init__(self, ns, sems, base):
        self.ns, self.sems, self.base = ns, sems, base
        self.me = lax.axis_index("seq")

    def copy(self, src, dst, lane, step):
        return send(
            src,
            dst,
            self.sems,
            self.base + lane * (self.ns - 1) + step - 1,
            "seq",
            wrap(self.me + step, self.ns),
        )


class Line:
    def __init__(self, plane, ns, part, inward, swap, res, sems, base, turned, copy_sem, credits):
        self.plane, self.ns, self.turned = plane, ns, turned
        self.part, self.inward, self.swap, self.res = part, inward, swap, res
        self.sems, self.base, self.copy_sem, self.credits = sems, base, copy_sem, credits
        self.me = lax.axis_index("seq")
        self.side = self.me // (ns // 2)
        middle = ns // 2 - 1
        self.depth = (1 - self.side) * (middle - self.me) + self.side * (self.me - middle - 1)
        self.ends = middle
        self.in_to = self.me + 1 - 2 * self.side
        self.out_to = self.me - 1 + 2 * self.side
        self.other = ns - 1 - self.me
        self.count = res.shape[0]
        self.slots = inward.shape[0]
        if self.ends != 1 and self.slots < self.count:
            raise ValueError("slots")

    @staticmethod
    def marks(nf, turned):
        return 5 + (nf - 1 if turned else 0)

    def sem(self, chunk, kind):
        return self.base + chunk * self.marks(self.plane.nf, self.turned) + kind

    def half(self, ref, chunk, side):
        rows = ref.shape[-2] // 2
        rows = pl.ds(pl.multiple_of(side * rows, rows), rows)
        return ref.at[chunk, :, rows, :]

    def inner(self, chunk, relayed=False):
        slot = chunk % self.slots
        src = self.inward.at[slot] if relayed else self.part.at[chunk]
        return send(src, self.inward.at[slot], self.sems, self.sem(chunk, 0), "seq", self.in_to)

    def cross(self, chunk):
        slot = chunk % self.slots
        return send(
            self.half(self.inward, slot, 1 - self.side),
            self.swap.at[slot],
            self.sems,
            self.sem(chunk, 1),
            "seq",
            self.other,
        )

    def result(self):
        return self.res if self.turned else self.part

    def back_cross(self, chunk, side=None):
        side = self.side if side is None else side
        return send(
            self.half(self.result(), chunk, side),
            self.half(self.res, chunk, side),
            self.sems,
            self.sem(chunk, 2),
            "seq",
            self.other,
        )

    def outer(self, chunk, side, src):
        return send(
            self.half(src, chunk, side),
            self.half(self.res, chunk, side),
            self.sems,
            self.sem(chunk, 3) + side,
            "seq",
            self.out_to,
        )

    def spread(self, chunk, step, source=None):
        rows = self.part.shape[-2] // 2
        rows = pl.ds(pl.multiple_of(self.side * rows, rows), rows)
        target = wrap(self.plane.me + step, self.plane.nf)
        source = self.plane.me if source is None else source
        return send(
            self.part.at[chunk, target, rows, :],
            self.res.at[chunk, source, rows, :],
            self.sems,
            self.sem(chunk, 4) + step,
            "fsdp",
            target,
        )

    def keep(self, chunk):
        if self.turned:
            rows = self.part.shape[-2] // 2
            rows = pl.ds(pl.multiple_of(self.side * rows, rows), rows)
            me = self.plane.me
            src, dst = self.part.at[chunk, me, rows, :], self.res.at[chunk, me, rows, :]
        else:
            src = self.half(self.part, chunk, self.side)
            dst = self.half(self.res, chunk, self.side)
        return pltpu.make_async_copy(src, dst, self.copy_sem.at[chunk])

    def begin(self, chunk):
        if self.ends:

            @pl.when(self.depth == self.ends)
            def _():
                if chunk >= self.slots:
                    pl.semaphore_wait(self.credits.at[0], 1)
                self.inner(chunk).start()

    def relay(self, chunk, hop):
        slot = chunk % self.slots

        @pl.when(self.depth == self.ends - hop)
        def _():
            self.inner(chunk).wait_recv()
            total = self.inward[slot].astype(F32) + self.part[chunk].astype(F32)
            self.inward[slot] = total.astype(BF)
            self.inner(chunk, True).start()

    def meet(self, chunk):
        slot = chunk % self.slots

        @pl.when(self.depth == 0)
        def _():
            self.inner(chunk).wait_recv()
            theirs = self.half(self.inward, slot, 1 - self.side)
            mine = self.half(self.part, chunk, 1 - self.side)

            def step(i):
                rows = tile(i, 16)
                total = theirs[:, rows, :].astype(F32) + mine[:, rows, :].astype(F32)
                theirs[:, rows, :] = total.astype(BF)

            loop(theirs.shape[1] // 16, step)
            if chunk >= self.slots:
                pl.semaphore_wait(self.credits.at[1], 1)
            self.cross(chunk).start()

    def settle(self, chunk):
        slot = chunk % self.slots

        @pl.when(self.depth == 0)
        def _():
            self.cross(chunk).wait_recv()
            theirs = self.half(self.inward, slot, self.side)
            mine = self.half(self.part, chunk, self.side)

            def step(i):
                rows = tile(i, 16)
                total = theirs[:, rows, :].astype(F32) + mine[:, rows, :].astype(F32)
                total += self.swap[slot, :, rows, :].astype(F32)
                mine[:, rows, :] = total.astype(BF)

            loop(theirs.shape[1] // 16, step)
            self.keep(chunk).start()
            if self.turned:
                for k in range(1, self.plane.nf):
                    self.spread(chunk, k).start()
            else:
                self.hand_out(chunk)
            self.cross(chunk).wait_send()
            if chunk + self.slots < self.count:
                pl.semaphore_signal(
                    self.credits.at[0], inc=1, device_id={"seq": self.out_to}, device_id_type=MESH
                )
                pl.semaphore_signal(
                    self.credits.at[1], inc=1, device_id={"seq": self.other}, device_id_type=MESH
                )

    def hand_out(self, chunk):
        self.back_cross(chunk).start()
        if self.ends:
            self.outer(chunk, self.side, self.result()).start()

    def spread_end(self, chunk):
        @pl.when(self.depth == 0)
        def _():
            for k in range(1, self.plane.nf):
                self.spread(chunk, k, wrap(self.plane.me - k, self.plane.nf)).wait_recv()
            self.keep(chunk).wait()
            self.hand_out(chunk)

    def pass_on(self, chunk):
        @pl.when(self.depth == 0)
        def _():
            self.back_cross(chunk, 1 - self.side).wait_recv()
            if self.ends:
                self.outer(chunk, 1 - self.side, self.res).start()

    def outward_hop(self, chunk, hop):
        @pl.when(self.depth == hop)
        def _():
            for side in range(2):
                self.outer(chunk, side, self.res).wait_recv()
                self.outer(chunk, side, self.res).start()

    def pause(self, chunk):
        pass

    def phases(self):
        listed = [self.begin, self.pause]
        listed += [partial(self.relay, hop=hop) for hop in range(1, self.ends)]
        listed += [self.meet, self.settle]
        if self.turned:
            listed += [self.spread_end]
        listed += [self.pass_on]
        listed += [partial(self.outward_hop, hop=hop) for hop in range(1, self.ends)]
        return listed

    def drain(self, chunk):
        @pl.when(self.depth == 0)
        def _():
            self.back_cross(chunk).wait_send()
            if self.turned:
                for k in range(1, self.plane.nf):
                    self.spread(chunk, k).wait_send()
            else:
                self.keep(chunk).wait()

        if self.ends:

            @pl.when(self.depth == self.ends)
            def _():
                for side in range(2):
                    self.outer(chunk, side, self.res).wait_recv()

            @pl.when(self.depth < self.ends)
            def _():
                for side in range(2):
                    self.outer(chunk, side, self.res).wait_send()

            @pl.when(self.depth > 0)
            def _():
                self.inner(chunk).wait_send()


class Ticks:
    def __init__(self, jobs):
        self.jobs = jobs
        self.now = 0

    def tick(self, times=1):
        for _ in range(times):
            if self.now < len(self.jobs):
                line, chunk = self.jobs[self.now]
                line.begin(chunk)
            for i, (line, chunk) in enumerate(self.jobs):
                phase = self.now - i
                if 0 < phase < len(line.phases()):
                    line.phases()[phase](chunk)
            self.now += 1

    def finish(self):
        depth = max(len(line.phases()) for line, _ in self.jobs)
        while self.now < len(self.jobs) + depth:
            self.tick()
        for line, chunk in self.jobs:
            line.drain(chunk)


class Lines:
    def __init__(self, nf, kinds):
        self.nf, self.kinds = nf, kinds

    def scratch(self):
        listed = []
        for (blocks, rows, cols), count, _ in self.kinds:
            slots = min(count, SLOTS)
            listed.append(pltpu.VMEM((slots, blocks, rows, cols), BF))
            listed.append(pltpu.VMEM((slots, blocks, rows // 2, cols), BF))
            listed.append(pltpu.SemaphoreType.DMA((count,)))
            listed.append(pltpu.SemaphoreType.REGULAR((2,)))
        marks = sum(count * Line.marks(self.nf, turned) for _, count, turned in self.kinds)
        return listed + [pltpu.SemaphoreType.DMA((marks,))] * 2

    def count(self):
        return 4 * len(self.kinds) + 2

    def outs(self):
        return [shape((count,) + dims) for dims, count, _ in self.kinds]

    def build(self, plane, ns, parts, results, scratch):
        lines, base = [], 0
        sems = tuple(scratch[-2:])
        for k, (_, count, turned) in enumerate(self.kinds):
            inward, swap, copy_sem, credits = scratch[4 * k : 4 * k + 4]
            lines.append(
                Line(
                    plane,
                    ns,
                    parts[k],
                    inward,
                    swap,
                    results[k],
                    sems,
                    base,
                    turned,
                    copy_sem,
                    credits,
                )
            )
            base += count * Line.marks(self.nf, turned)
        return lines


def forward_lines(nf, wide, hidden):
    count = EARLY * (hidden // CHUNKS // LANES)
    return Lines(nf, [((1, LANES, D), count, False), ((nf, D // nf, LANES), count, True)])


def forward_kernel(nf, ns, lines, *refs):
    (low, g_ref, win_ref, wout_ref, wq_ref, wk_ref, wv_ref, wo_ref, planes_ref, lens_ref) = refs[:10]
    refs = refs[10:]
    (xq_out, xk_out, xv_out, gg_out, win_out, h_out, dup_out, w_out, rest_out, rest_in) = refs[:10]
    refs = refs[10:]
    sum_out, sum_in, att_ref, dq_ref, dk_ref, dv_ref = refs[:6]
    refs = refs[6:]
    (xr, gg, wfull, hid, dup, p_out, p_in, stage, wqkv, qkva, zin, zout, zback, dkv) = refs[:14]
    send_sem, recv_sem, copy_sem = refs[14:17]
    line_refs = refs[17:]
    plane = Plane(nf)
    sems = (send_sem, recv_sem)
    tok = g_ref.shape[0]
    wide = wo_ref.shape[0]
    heads = wide // HEAD
    per = nf // ns
    slab = per * tok
    group_tok = ns * tok
    sq = lax.axis_index("seq")
    width = wfull.shape[1] // CHUNKS
    blocks = min(4, nf)
    pieces = width // LANES
    step_sems = nf - 1
    greet(nf, ns)
    l_out, l_in = lines.build(plane, ns, (p_out, p_in), (sum_out, sum_in), line_refs)
    jobs = []
    for n in range(EARLY):
        jobs += [(l_out, n * pieces + k) for k in range(pieces)]
        jobs += [(l_in, n * pieces + k) for k in range(pieces)]
    ticks = Ticks(jobs)
    ag_r = Gather(plane, low.at[3], xr, sems, 0)
    ag_g = Gather(plane, g_ref, gg, sems, step_sems)
    ag_x = [
        Gather(plane, low.at[i], out, sems, (2 + i) * step_sems)
        for i, out in enumerate((xq_out, xk_out, xv_out))
    ]
    turn = Turn(plane, win_ref, wfull, sems, 5 * step_sems, CHUNKS)
    turns = [
        Turn(plane, w, wqkv.at[i], sems, (5 + CHUNKS + i) * step_sems, 1)
        for i, w in enumerate((wq_ref, wk_ref, wv_ref))
    ]
    base = (8 + CHUNKS) * step_sems
    there = Exchange(ns, sems, base)
    home = Exchange(ns, sems, base + 4 * (ns - 1))
    ag_r.start()
    turn.start(0)
    ag_g.start()
    for chunk in range(1, CHUNKS):
        turn.start(chunk)
    for i in range(3):
        ag_x[i].start()
        turns[i].start(0)
    keeps = [ag_r.keep(copy_sem.at[0]), ag_g.keep(copy_sem.at[1]), turn.keep(copy_sem.at[2])]
    keeps += [ag_x[i].keep(copy_sem.at[3 + i]) for i in range(3)]
    keeps += [turns[i].keep(copy_sem.at[6 + i]) for i in range(3)]
    for keep in keeps:
        keep.start()
    ag_r.forward()
    ag_g.forward()
    ag_r.finish()
    ag_g.finish()
    for keep in keeps:
        keep.wait()
    saves = []

    def save(src, dst):
        saves.append(pltpu.make_async_copy(src, dst, copy_sem.at[9 + len(saves)]))
        saves[-1].start()

    save(gg, gg_out)

    for chunk in range(CHUNKS):
        turn.arrive(chunk)
        cols = slice(chunk * width, chunk * width + width)

        def rows_step(i, cols=cols):
            rows = tile(i, blocks * tok)
            up = dot(rows_of(xr, i * blocks, blocks), wfull[:, cols])
            dh = dot(rows_of(gg, i * blocks, blocks), wout_ref[cols, :], 1, 1)
            cdf = 0.5 * (1.0 + lax.erf(up * (0.5**0.5)))
            slope = cdf + up * jnp.exp(-0.5 * up * up) * 0.3989422804014327
            hid[rows, cols] = (up * cdf).astype(BF)
            dup[rows, cols] = (dh * slope).astype(BF)

        loop(nf // blocks, rows_step)

        def grad_step(i, cols=cols, chunk=chunk):
            feats = tile(i, WIDTH)
            every = gg[:, :, feats].reshape(nf * tok, WIDTH)
            grad = dot(hid[:, cols], every, 0, 0).astype(BF)
            for k in range(pieces):
                p_out[chunk * pieces + k, 0, :, feats] = grad[k * LANES : k * LANES + LANES]
            every = xr[:, :, feats].reshape(nf * tok, WIDTH)
            grad = dot(every, dup[:, cols], 0, 0).astype(BF)
            count = WIDTH * nf // D
            for k in range(pieces):
                piece = grad[:, k * LANES : k * LANES + LANES].reshape(count, D // nf, LANES)
                p_in[chunk * pieces + k, pl.ds(i * count, count)] = piece

        loop(D // WIDTH, grad_step)
        ticks.tick()

    early = EARLY * pieces
    save(wfull, win_out)
    save(hid, h_out)
    save(dup, dup_out)
    save(p_out.at[pl.ds(early, CHUNKS * pieces - early)], rest_out)
    save(p_in.at[pl.ds(early, CHUNKS * pieces - early)], rest_in)

    def ship(i):
        for step in range(1, ns):
            target = wrap(sq + step, ns)
            there.copy(qkva.at[i, tile(target, slab), :], zin.at[i, sq], i, step).start()
        zin[i, sq] = qkva[i, tile(sq, slab), :]

    def da_step(i):
        rows = tile(i, blocks * tok)
        qkva[3, rows, :] = dot(rows_of(gg, i * blocks, blocks), wo_ref[...], 1, 1).astype(BF)

    loop(nf // blocks, da_step)
    ship(3)
    ticks.tick()
    for i in range(3):
        ag_x[i].forward()
        turns[i].arrive(0)
        ag_x[i].finish()
        load = pltpu.make_async_copy(ag_x[i].buf, stage, copy_sem.at[15])
        load.start()
        load.wait()

        def lin_step(r, i=i):
            rows = tile(r, blocks * tok)
            lin = dot(rows_of(stage, r * blocks, blocks), wqkv[i])
            for head in range(heads):
                cols = slice(head * HEAD, head * HEAD + HEAD)
                piece = lin[:, cols]
                if i < 2:
                    piece = rotated(piece, [planes_ref[k, rows, :] for k in range(3)])
                qkva[i, rows, cols] = piece.astype(BF)

        loop(nf // blocks, lin_step)
        ship(i)
        ticks.tick(2 if i < 2 else 1)
    save(wqkv, w_out)
    for i in range(4):
        for step in range(1, ns):
            there.copy(zin.at[i, 0], zin.at[i, wrap(sq - step, ns)], i, step).wait_recv()

    scale = HEAD ** (-0.5)
    queries = min(256, group_tok)
    q_slabs = queries // tok

    def pair_step(pair):
        grp = pair // heads
        head = lax.rem(pair, heads)
        cols = tile(head, HEAD)
        toks = tile(grp, tok)
        first_end = lens_ref[sq * per + grp, 0]
        second_end = first_end + lens_ref[sq * per + grp, 1]

        def part_of(i, begin, count):
            return zin[i, pl.ds(begin, count), toks, cols].reshape(count * tok, HEAD)

        keys, values = part_of(1, 0, ns), part_of(2, 0, ns)
        dkv[...] = jnp.zeros_like(dkv)

        def query_step(j):
            begin = j * q_slabs
            query, d_att = part_of(0, begin, q_slabs), part_of(3, begin, q_slabs)
            qi = j * queries + lax.broadcasted_iota(jnp.int32, (queries, group_tok), 0)
            ki = lax.broadcasted_iota(jnp.int32, (queries, group_tok), 1)
            seg_q = (qi >= first_end).astype(jnp.int32) + (qi >= second_end).astype(jnp.int32)
            seg_k = (ki >= first_end).astype(jnp.int32) + (ki >= second_end).astype(jnp.int32)
            allowed = (seg_q == seg_k) & (qi >= ki)
            scores = jnp.where(allowed, dot(query, keys, 1, 1) * scale, NEGATIVE)
            top = jnp.max(scores, axis=1, keepdims=True)
            expo = jnp.where(allowed, jnp.exp(scores - top), 0.0)
            prob = expo / jnp.sum(expo, axis=1, keepdims=True)
            prob_low = prob.astype(BF)
            attended = dot(prob_low, values)
            delta = jnp.sum(d_att.astype(F32) * attended, axis=1, keepdims=True)
            d_score = (prob * (dot(d_att, values, 1, 1) - delta)).astype(BF)
            d_query = dot(d_score, keys) * scale
            dkv[0] += dot(d_score, query, 0, 0)
            dkv[1] += dot(prob_low, d_att, 0, 0)
            where = pl.ds(begin, q_slabs)
            zout[0, where, toks, cols] = attended.astype(BF).reshape(q_slabs, tok, HEAD)
            zout[1, where, toks, cols] = d_query.astype(BF).reshape(q_slabs, tok, HEAD)

        loop(group_tok // queries, query_step)
        zout[2, :, toks, cols] = (dkv[0] * scale).astype(BF).reshape(ns, tok, HEAD)
        zout[3, :, toks, cols] = dkv[1].astype(BF).reshape(ns, tok, HEAD)

    loop(per * heads, pair_step)

    for i in (1, 2, 3, 0):
        for step in range(1, ns):
            target = wrap(sq + step, ns)
            home.copy(zout.at[i, target], zback.at[i, tile(sq, slab), :], i, step).start()
        zback[i, tile(sq, slab), :] = zout[i, sq]
    ticks.tick()
    outs = (att_ref, dq_ref, dk_ref, dv_ref)
    for i in (1, 2, 3, 0):
        for step in range(1, ns):
            source = wrap(sq - step, ns)
            home.copy(zout.at[i, 0], zback.at[i, tile(source, slab), :], i, step).wait_recv()
        if i in (0, 3):
            outs[i][...] = zback[i]
        else:

            def back_step(r, i=i):
                rows = tile(r, tok)
                for head in range(heads):
                    cols = slice(head * HEAD, head * HEAD + HEAD)
                    piece = zback[i, rows, cols].astype(F32)
                    piece = rotated_back(piece, [planes_ref[k, rows, :] for k in range(3)])
                    outs[i][rows, cols] = piece.astype(BF)

            loop(nf, back_step)
        ticks.tick()
    ticks.finish()
    for gather in (ag_r, ag_g, *ag_x):
        gather.drain()
    for chunk in range(CHUNKS):
        turn.drain(chunk)
    for i in range(3):
        turns[i].drain(0)
    for copy in saves:
        copy.wait()
    for i in range(4):
        for step in range(1, ns):
            there.copy(zin.at[i, 0], zin.at[i, 0], i, step).wait_send()
            home.copy(zout.at[i, 0], zout.at[i, 0], i, step).wait_send()


def run_forward(nf, ns, low, g_own, win, wout, ws, wo, planes, lens):
    tok = g_own.shape[0]
    hidden = wout.shape[0]
    wide = wo.shape[0]
    lines = forward_lines(nf, wide, hidden)
    count = (8 + CHUNKS) * (nf - 1) + 8 * (ns - 1)
    flat = shape((nf * tok, wide))
    block = shape((nf, tok, D))
    total = CHUNKS * (hidden // CHUNKS // LANES)
    rest = total - lines.kinds[0][1]
    outs = [block] * 4 + [shape((D, hidden))] + [shape((nf * tok, hidden))] * 2
    outs += [shape((3, D, wide)), shape((rest, 1, LANES, D)), shape((rest, nf, D // nf, LANES))]
    outs += lines.outs() + [flat] * 4
    exchange = pltpu.VMEM((4, ns, nf // ns * tok, wide), BF)
    return pl.pallas_call(
        partial(forward_kernel, nf, ns, lines),
        out_shape=tuple(outs),
        in_specs=[hbm()] * 3
        + [vmem()]
        + [hbm()] * 3
        + [vmem()] * 2
        + [pl.BlockSpec(memory_space=pltpu.SMEM)],
        out_specs=(hbm(),) * 12 + (vmem(),) * 4,
        scratch_shapes=[
            pltpu.VMEM((nf, tok, D), BF),
            pltpu.VMEM((nf, tok, D), BF),
            pltpu.VMEM((D, hidden), BF),
            pltpu.VMEM((nf * tok, hidden), BF),
            pltpu.VMEM((nf * tok, hidden), BF),
            pltpu.VMEM((total, 1, LANES, D), BF),
            pltpu.VMEM((total, nf, D // nf, LANES), BF),
            pltpu.VMEM((nf, tok, D), BF),
            pltpu.VMEM((3, D, wide), BF),
            pltpu.VMEM((4, nf * tok, wide), BF),
            exchange,
            exchange,
            pltpu.VMEM((4, nf * tok, wide), BF),
            pltpu.VMEM((2, ns * tok, HEAD), F32),
            pltpu.SemaphoreType.DMA((count,)),
            pltpu.SemaphoreType.DMA((count,)),
            pltpu.SemaphoreType.DMA((16,)),
        ]
        + lines.scratch(),
        compiler_params=params(1),
        name="forward",
    )(low, g_own, win, wout, *ws, wo, planes, lens)


TENSORS = 5


def return_lines(nf, wide, rest):
    count = wide // LANES
    kinds = [((1, LANES, D), rest, False), ((nf, D // nf, LANES), rest, True)]
    return Lines(nf, kinds + [((nf, D // nf, LANES), count, True)] * 2)


def return_kernel(nf, ns, lines, *refs):
    att_ref, dq_ref, dk_ref, dv_ref, dup_ref, wqkv, win_ref, wo_ref, wout_ref, h_ref = refs[:10]
    p_out, p_in = refs[10:12]
    sources = refs[12:16]
    refs = refs[16:]
    y_ref, dx_ref, dwv_ref, dwo_ref = refs[:4]
    results = refs[4:8]
    refs = refs[8:]
    stage, part, sib, rec, p_q, p_k, send_sem, recv_sem, copy_sem, credit = refs[:10]
    line_refs = refs[10:]
    plane = Plane(nf)
    sems = (send_sem, recv_sem)
    tok = y_ref.shape[0]
    wide = wo_ref.shape[0]
    parts, sibs = part.shape[0], sib.shape[0]
    greet(nf, ns)
    built = lines.build(plane, ns, (p_out, p_in, p_q, p_k), results, line_refs)
    jobs = []
    for line in built:
        jobs += [(line, chunk) for chunk in range(line.count)]
    ticks = Ticks(jobs)
    load = pltpu.make_async_copy(sources[0], stage, copy_sem)
    load.start()
    scats = [
        Scatter(
            plane,
            part.at[t % parts],
            sib.at[t % sibs],
            rec.at[t % sibs],
            sems,
            t * CHUNKS * (nf - 1),
            CHUNKS,
        )
        for t in range(TENSORS)
    ]
    firsts = (dq_ref, dk_ref, dv_ref, dup_ref)

    def total(t):
        def total_step(chunk):
            feats = tile(chunk, D // CHUNKS)
            if t < 4:
                dx_ref[t, :, feats] = scats[t].total(chunk)
            else:
                y_ref[:, feats] = scats[t].total(chunk)

        loop(CHUNKS, total_step)
        if t + sibs < TENSORS:
            for target in [plane.on(0, 1)] + [plane.on(k) for k in range(1, plane.chips)]:
                pl.semaphore_signal(
                    credit.at[t], inc=1, device_id={"fsdp": target}, device_id_type=MESH
                )

    ticks.tick()
    for t in range(TENSORS):
        if t >= sibs:
            pl.semaphore_wait(credit.at[t - sibs], plane.chips)
        for chunk in range(CHUNKS):
            feats = slice(chunk * (D // CHUNKS), (chunk + 1) * (D // CHUNKS))
            if t >= parts:
                scats[t - parts].drain(chunk)
            if t < 3:
                value = dot(firsts[t][...], wqkv[t, feats, :], 1, 1)
            elif t == 3:
                value = dot(dup_ref[...], win_ref[feats, :], 1, 1)
            else:
                value = dot(att_ref[...], wo_ref[:, feats]) + dot(h_ref[...], wout_ref[:, feats])
            scats[t].part[:, :, feats] = value.astype(BF).reshape(nf, tok, D // CHUNKS)
            scats[t].start(chunk)
            if chunk > 0:
                scats[t].combine(chunk - 1)
            if chunk % 2:
                ticks.tick()
        scats[t].combine(CHUNKS - 1)
        if t < 4:
            pltpu.make_async_copy(sources[t], stage, copy_sem).wait()

            def grad_step(i, t=t):
                feats = tile(i, WIDTH)
                every = stage[:, :, feats].reshape(nf * tok, WIDTH)
                if t < 3:
                    grad = dot(every, firsts[t][...], 0, 0).astype(BF)
                    count = WIDTH * nf // D
                    for k in range(wide // LANES):
                        piece = grad[:, k * LANES : k * LANES + LANES]
                        piece = piece.reshape(count, D // nf, LANES)
                        (p_q, p_k, dwv_ref)[t][k, pl.ds(i * count, count)] = piece
                else:
                    grad = dot(att_ref[...], every, 0, 0).astype(BF)
                    for k in range(wide // LANES):
                        dwo_ref[k, 0, :, feats] = grad[k * LANES : k * LANES + LANES]

            loop(D // WIDTH, grad_step)
            if t < 3:
                pltpu.make_async_copy(sources[t + 1], stage, copy_sem).start()
        if t:
            total(t - 1)
    total(TENSORS - 1)
    ticks.finish()
    for t in range(TENSORS - parts, TENSORS):
        loop(CHUNKS, scats[t].drain)


def run_return(nf, ns, att, ds, dup, wqkv, win, wo, wout, h, p_out, p_in, gg, xgs):
    tok = gg.shape[1]
    wide = wo.shape[0]
    chips = nf // 2
    count = TENSORS * CHUNKS * (nf - 1)
    parts = 2 if nf <= 8 else 1
    lines = return_lines(nf, wide, p_out.shape[0])
    turned = (wide // LANES, nf, D // nf, LANES)
    outs = [shape((tok, D), F32), shape((4, tok, D), F32), shape(turned)]
    outs += [shape((wide // LANES, 1, LANES, D))] + lines.outs()
    return pl.pallas_call(
        partial(return_kernel, nf, ns, lines),
        out_shape=tuple(outs),
        in_specs=[vmem()] * 12 + [hbm()] * 4,
        out_specs=(vmem(),) * 4 + (hbm(),) * 4,
        scratch_shapes=[
            pltpu.VMEM((nf, tok, D), BF),
            pltpu.VMEM((parts, nf, tok, D), BF),
            pltpu.VMEM((2, chips, tok, D), BF),
            pltpu.VMEM((2, chips - 1, tok, D), BF),
            pltpu.VMEM(turned, BF),
            pltpu.VMEM(turned, BF),
            pltpu.SemaphoreType.DMA((count,)),
            pltpu.SemaphoreType.DMA((count,)),
            pltpu.SemaphoreType.DMA,
            pltpu.SemaphoreType.REGULAR((TENSORS - 2,)),
        ]
        + lines.scratch(),
        compiler_params=params(2),
        name="give_back",
    )(att, *ds, dup, wqkv, win, wo, wout, h, p_out, p_in, *xgs, gg)


SMALL = 112


def end_lines(nf, wide):
    count = wide // LANES
    return Lines(nf, [((nf, D // nf, LANES), count, True), ((1, LANES, D), count, False)])


def end_kernel(
    nf,
    ns,
    lines,
    p_v,
    p_o,
    hist_ref,
    st_ref,
    dx_ref,
    g_ref,
    y_ref,
    coef_ref,
    inv_ref,
    pre_ref,
    act_ref,
    mixed_ref,
    mix_in_ref,
    mix_out_ref,
    again_ref,
    mgain_ref,
    xgain_ref,
    hg_ref,
    lo_ref,
    sm_out,
    sum_v,
    sum_o,
    ds,
    last,
    dmixed,
    dcoef,
    gsum,
    sm_ref,
    sm_src,
    sm_in,
    sm_z,
    sm_sem,
    sm_rsem,
    *line_refs,
):
    tok = hist_ref.shape[1]
    plane = Plane(nf)
    greet(nf, ns)
    built = lines.build(plane, ns, (p_v, p_o), (sum_v, sum_o), line_refs)
    jobs = []
    for line in built:
        jobs += [(line, chunk) for chunk in range(line.count)]
    ticks = Ticks(jobs)
    small = Small(plane, ns, sm_src, sm_in, sm_z, sm_out, (sm_sem, sm_rsem))
    ticks.tick(2)
    gsum[...] = jnp.zeros_like(gsum)

    def back(value, inv, gain, grad):
        scaled = grad * gain
        mean = jnp.sum(value * scaled, axis=1, keepdims=True) / D
        return inv * scaled - value * (inv * inv * inv * mean)

    def row_step(i):
        rows = tile(i, ROWS)
        coef = coef_ref[rows, :]
        lane = lax.broadcasted_iota(jnp.int32, (ROWS, STREAMS * HIST), 1)
        for c in range(STREAMS):
            value, inv = st_ref[c, rows, :], inv_ref[c, rows, :]
            grad = dx_ref[c, rows, :]
            gain = mgain_ref if c == STREAMS - 1 else again_ref
            gsum[c // 3] += grad * (value * inv)
            d_value = back(value, inv, gain[...], grad)
            if c == STREAMS - 1:
                d_value = d_value + g_ref[rows, :].astype(F32)
                lo_ref[rows, :] = (value + y_ref[rows, :]).astype(BF)
            ds[c] = d_value
        found = jnp.zeros((ROWS, STREAMS * HIST), F32)
        for j in range(HIST):
            sums = [jnp.zeros((ROWS, 128), F32)] * STREAMS
            for begin in range(0, D, WIDTH):
                cols = slice(begin, begin + WIDTH)
                entry = hist_ref[j, rows, cols].astype(F32)
                grad = jnp.zeros((ROWS, WIDTH), F32)
                for c in range(STREAMS):
                    at = c * HIST + j
                    value = ds[c, :, cols]
                    grad = grad + coef[:, at : at + 1] * value
                    product = value * entry
                    for k in range(0, WIDTH, 128):
                        sums[c] = sums[c] + product[:, k : k + 128]
                if j < HIST - 1:
                    hg_ref[j, rows, cols] = grad.astype(BF)
                else:
                    last[rows, cols] = grad
            for c in range(STREAMS):
                value = jnp.sum(sums[c], axis=1, keepdims=True)
                found = jnp.where(lane == c * HIST + j, value, found)
        dcoef[rows, :] = found.astype(BF)

    loop(tok // ROWS // 2, row_step)
    ticks.tick()
    loop(tok // ROWS // 2, lambda i: row_step(i + tok // ROWS // 2))
    ticks.tick()
    mix_in, mix_out = mix_in_ref[...].astype(BF), mix_out_ref[...].astype(BF)
    pre, d_coef = pre_ref[...], dcoef[...]
    slope = 0.5 * (1.0 + lax.erf(pre * (0.5**0.5)))
    slope = slope + pre * jnp.exp(-0.5 * pre * pre) * 0.3989422804014327
    d_pre = (dot(d_coef, mix_out, 1, 1) * slope).astype(BF)
    hidden = pre.shape[1]
    sm_ref[0:hidden, :] = dot(d_pre, mixed_ref[...], 0, 0)
    dmixed[...] = dot(d_pre, mix_in, 1, 1)

    def last_step(i):
        rows = tile(i, ROWS)
        value, inv, grad = hist_ref[HIST - 1, rows, :].astype(F32), inv_ref[STREAMS, rows, :], dmixed[rows, :]
        gsum[2] += grad * (value * inv)
        total = last[rows, :] + back(value, inv, xgain_ref[...], grad)
        hg_ref[HIST - 1, rows, :] = total.astype(BF)

    loop(tok // ROWS, last_step)
    for k in range(3):
        sm_ref[hidden + k : hidden + k + 1, :] = jnp.sum(gsum[k], axis=0, keepdims=True)
    begin = hidden + 3
    sm_ref[begin:SMALL, :] = jnp.zeros((SMALL - begin, D), F32)
    turned = dot(d_coef, act_ref[...], 0, 0)
    for k in range(STREAMS * HIST):
        at = begin + k // STREAMS
        cols = slice(k % STREAMS * 128, k % STREAMS * 128 + hidden)
        sm_ref[at : at + 1, cols] = turned[k : k + 1, :]
    for k in range(nf):
        sm_src[k] = sm_ref[:, k * (D // nf) : (k + 1) * (D // nf)]
    small.start()
    ticks.tick(2)
    small.across()
    ticks.tick(2)
    small.finish()
    ticks.finish()
    small.drain()


def run_end(nf, ns, p_v, p_o, *args):
    tok = args[0].shape[1]
    wide = p_v.shape[0] * LANES
    lines = end_lines(nf, wide)
    cols = D // nf
    few = 2 * (nf - 1) + ns - 1
    outs = [shape((HIST, tok, D)), shape((tok, D)), shape((nf, SMALL, cols), F32)]
    return pl.pallas_call(
        partial(end_kernel, nf, ns, lines),
        out_shape=tuple(outs + lines.outs()),
        in_specs=[vmem()] * 17,
        out_specs=(vmem(),) * 3 + (hbm(),) * 2,
        scratch_shapes=[
            pltpu.VMEM((STREAMS, ROWS, D), F32),
            pltpu.VMEM((tok, D), F32),
            pltpu.VMEM((tok, D), F32),
            pltpu.VMEM((tok, STREAMS * HIST), BF),
            pltpu.VMEM((3, ROWS, D), F32),
            pltpu.VMEM((SMALL, D), F32),
            pltpu.VMEM((nf, SMALL, cols), F32),
            pltpu.VMEM((nf, SMALL, cols), F32),
            pltpu.VMEM((ns, SMALL, cols), F32),
            pltpu.SemaphoreType.DMA((few,)),
            pltpu.SemaphoreType.DMA((few,)),
        ]
        + lines.scratch(),
        compiler_params=params(3),
        name="streams_back",
    )(p_v, p_o, *args)


class Small:
    def __init__(self, plane, ns, src, mid, line, out, sems):
        self.plane, self.ns, self.src, self.mid, self.line, self.out = plane, ns, src, mid, line, out
        self.sems = sems
        self.me = lax.axis_index("seq")

    def scatter(self, step):
        target = wrap(self.plane.me + step, self.plane.nf)
        return send(
            self.src.at[target], self.mid.at[self.plane.me], self.sems, step - 1, "fsdp", target
        )

    def along(self, step):
        me = self.line.at[self.me]
        slot = self.plane.nf - 1 + step - 1
        return send(me, me, self.sems, slot, "seq", wrap(self.me + step, self.ns))

    def spread(self, step):
        me = self.out.at[self.plane.me]
        slot = self.plane.nf - 1 + self.ns - 1 + step - 1
        return send(me, me, self.sems, slot, "fsdp", wrap(self.plane.me + step, self.plane.nf))

    def start(self):
        self.mid[self.plane.me] = self.src[self.plane.me]
        for step in range(1, self.plane.nf):
            self.scatter(step).start()

    def across(self):
        for step in range(1, self.plane.nf):
            self.scatter(step).wait_recv()
        total = self.mid[0]
        for k in range(1, self.plane.nf):
            total += self.mid[k]
        self.line[self.me] = total
        for step in range(1, self.ns):
            self.along(step).start()

    def finish(self):
        for step in range(1, self.ns):
            self.along(step).wait_recv()
        total = self.line[0]
        for k in range(1, self.ns):
            total += self.line[k]
        self.out[self.plane.me] = total
        for step in range(1, self.plane.nf):
            self.spread(step).start()

    def drain(self):
        for step in range(1, self.plane.nf):
            self.spread(step).wait_recv()
        for step in range(1, self.plane.nf):
            self.scatter(step).wait_send()
            self.spread(step).wait_send()
        for step in range(1, self.ns):
            self.along(step).wait_send()


def turned_kernel(*refs):
    out_ref, at = refs[-1], 0
    for ref in refs[:-1]:
        for k in range(ref.shape[0]):
            out_ref[:, at : at + LANES] = ref[k, 0].astype(F32)
            at += LANES


def turned_rows(*parts):
    _, nf, rows, _ = parts[0].shape
    wide = sum(p.shape[0] for p in parts) * LANES
    return pl.pallas_call(
        turned_kernel,
        grid=(nf,),
        out_shape=shape((rows, nf * wide), F32),
        in_specs=[pl.BlockSpec((p.shape[0], 1, rows, LANES), lambda i: (0, i, 0, 0)) for p in parts],
        out_specs=pl.BlockSpec((rows, wide), lambda i: (0, i)),
        name="turned_rows",
    )(*parts)


def local(
    nf,
    ns,
    history,
    cotangent,
    seq_lengths,
    wq,
    wk,
    wv,
    wo,
    w_in,
    w_out,
    mix_in,
    mix_out,
    attn_gain,
    mlp_gain,
    mix_gain,
):
    hist = history[:, 0]
    tok_rows = hist.shape[1]
    lens = lax.all_gather(seq_lengths, "fsdp", axis=0, tiled=True)
    slab_index = lax.axis_index("seq") * tok_rows + jnp.arange(tok_rows, dtype=jnp.int32)
    every_index = jnp.tile(slab_index, nf)
    _, place = token_marks(every_index, jnp.repeat(lens, tok_rows, axis=0))
    planes = rope_planes(place)
    gains = [g[None] for g in (attn_gain, mlp_gain, mix_gain)]
    low, stream, coef, inv, pre, act, mixed = run_start(hist, mix_in, mix_out, *gains)
    grad_out = cotangent[0]
    ws = [w.astype(BF) for w in (wq, wk, wv)]
    wo_low, win_low, wout_low = wo.astype(BF), w_in.astype(BF), w_out.astype(BF)
    *xgs, gg, win_full, hidden, dup, wqkv, rest_out, rest_in, out_a, in_a, att, dq, dk, dv = run_forward(
        nf, ns, low, grad_out, win_low, wout_low, ws, wo_low, planes, lens
    )
    y_sum, dx, dwv, dwo, out_b, in_b, sum_q, sum_k = run_return(
        nf,
        ns,
        att,
        (dq, dk, dv),
        dup,
        wqkv,
        win_full,
        wo_low,
        wout_low,
        hidden,
        rest_out,
        rest_in,
        gg,
        xgs,
    )
    history_grad, layer_out, small, sum_v, sum_o = run_end(
        nf, ns, dwv, dwo, hist, stream, dx, grad_out, y_sum, coef, inv, pre, act, mixed, mix_in, mix_out, *gains
    )
    dwout = jnp.concatenate([out_a, out_b], axis=0).reshape(w_out.shape).astype(F32)
    dwo = sum_o.reshape(wo.shape).astype(F32)
    dw_in = turned_rows(in_a, in_b)
    dw_qkv = [turned_rows(s) for s in (sum_q, sum_k, sum_v)]
    small = small.transpose(1, 0, 2).reshape(SMALL, D)
    units = mix_in.shape[1]
    mix_out_rows = small[units + 3 :, : STREAMS * 128].reshape(HIST * STREAMS, 128)
    return (
        layer_out[None],
        history_grad[:, None],
        *dw_qkv,
        dwo,
        dw_in,
        dwout,
        small[:units].T,
        mix_out_rows[:, :units].T,
        small[units],
        small[units + 1],
        small[units + 2],
    )


def solution(mesh):
    rows, rep = P("fsdp", None), P()
    in_specs = (
        P(None, "fsdp", "seq", None),
        P("fsdp", "seq", None),
    ) + (rows,) * 7 + (rep,) * 5
    out_specs = (
        P("fsdp", "seq", None),
        P(None, "fsdp", "seq", None),
    ) + (rows,) * 6 + (rep,) * 5
    body = partial(local, mesh.shape["fsdp"], mesh.shape["seq"])
    return jax.shard_map(body, mesh=mesh, in_specs=in_specs, out_specs=out_specs, check_vma=False)
```

time: 1220 us -> 763 us (0.63)
  waiting for transfers between devices: 500 us -> 0 us
  Pallas kernels: 433 us -> 694 us
  blocking collectives: 103 us -> 10.4 us
  matrix products: 53.9 us -> 0 us
  local copies, waits for them, and re-layouts: 55.3 us -> 17.9 us
  other arithmetic: 50.5 us -> 30.4 us
  between operations: 16 us -> 1.25 us
    unnamed x7 -> x0, waiting for transfers between devices: 433 us -> none
    pallas_call x3 -> x8, Pallas kernels: 433 us -> 694 us  [the longest x1 394 us: run_forward(): pl.pallas_call(partial(forward_kernel, nf, ns, lines), out_shape=tuple(ou...]
    psum x1 -> x0, waiting for transfers between devices: 67.1 us -> none  [local(): lax.psum((dot(mixed_low, grad_pre, 0, 0), dot(act_low, grad_coef, 0, 0),...]
    dot_general x9 -> x0, matrix products: 53.9 us -> none  [the longest x1 19.6 us: local(): jnp.einsum('ncj,cnd->jnd', mix_coef, grad_stream, precision=lax.Precision...]
    all_to_all x4 -> x0, blocking collectives: 49 us -> none  [turn_back(): lax.all_to_all(split, 'fsdp', split_axis=0, concat_axis=0, tiled=True)]
    psum x1 -> x0, blocking collectives: 43.9 us -> none  [local(): lax.psum((dot(mixed_low, grad_pre, 0, 0), dot(act_low, grad_coef, 0, 0),...]
    unnamed x64 -> x27, local copies, waits for them, and re-layouts: 36.8 us -> 13.6 us
  transfers between devices with their start and end apart: 6 -> 0, of which waited for: 2 -> 0; matrix products, arithmetic and copies ran while one was open for 9% -> 0% of each run, Pallas kernels for 0% -> 0%
where the time goes in v3:
time: 763 us; the launch traced here: 754 us
  Pallas kernels  694 us (91%)
  other arithmetic  30.4 us (4%)
  local copies, waits for them, and re-layouts  17.9 us (2%)
  blocking collectives  10.4 us (1%)
    pallas_call x1, Pallas kernels, run_forward(): pl.pallas_call(partial(forward_kernel, nf, ns, lines), out_shape=tuple(ou...  394 us
    pallas_call x1, Pallas kernels, run_return(): pl.pallas_call(partial(return_kernel, nf, ns, lines), out_shape=tuple(out...  169 us
    pallas_call x1, Pallas kernels, run_end(): pl.pallas_call(partial(end_kernel, nf, ns, lines), out_shape=tuple(outs +...  96.7 us
    pallas_call x4, Pallas kernels, turned_rows(): pl.pallas_call(turned_kernel, grid=(nf,), out_shape=shape((rows, nf * wid...  23.7 us

profile of v3, /device:TPU:0, one launch (start us, length us, event | category | flops | bytes accessed | tf_op | source)
XLA Modules:
  0.0 753.9 jit_solution(5597778975630226759)
XLA Ops:
  0.6 0.0 copy-start.2
  0.7 0.1 pad.11.clone
  0.8 0.1 pad.8.clone
  0.9 10.4 %all-gather = s32[8,1,3]{2,1,0:T(1,128)S(1)} all-gather(s32[1,1,3]{2,1,0:T(1,128)} %bitcast.75), channel_id=1, replica_groups=mesh['seq'=4,'fsdp'=8] {'fsdp'}, dimensions={0}, use_global_device_ids=true | all-gather | bytes 108 | tf_op jit(solution)/shard_map/all_gather | solution.py:1387
  11.3 0.1 copy.54
  11.4 0.7 copy.56.refs_9_
  12.1 0.1 broadcast_bitcast_fusion
  12.2 1.4 copy.53.mix_out_ref
  13.6 2.7 convert_element_type.47.refs_7_
  16.3 2.5 copy.52.mix_in_ref
  18.8 0.0 copy-done.2
  18.8 0.0 copy-start.3
  18.8 0.0 slice-start
  18.8 1.1 convert_element_type.44.refs_4_
  19.9 3.5 convert_element_type.45.refs_5_
  23.4 0.0 copy-done.3
  23.4 0.0 slice-start.1
  23.4 1.1 convert_element_type.46.refs_6_
  24.6 1.9 multiply_cosine_fusion
  26.5 0.3 maximum_bitcast_fusion
  26.9 0.0 slice-start.2
  26.9 1.2 pad_maximum_fusion.1.refs_8_
  28.1 0.0 slice-done
  28.2 0.0 slice-done.1
  28.2 0.0 slice-start.3
  28.2 2.8 convert_element_type.43.refs_3_.refs_8_
  31.0 0.0 slice-done.2
  31.0 1.7 slice-done.3
  32.6 2.6 convert_element_type.42.refs_2_
  35.2 11.2 %streams.1 = (bf16[4,128,2048]{2,1,0:T(8,128)(2,1)}, f32[4,128,2048]{2,1,0:T(8,128)}, f32[128,36]{1,0:T(8,128)}, f32[5,128,1]{2,1,0:T(8,128)}, f32[128,100]{1,0:...) custom-call(bf16[9,128,2048]{2,1,0:T(8,128)(2,1)} %bitcast.45, f32[2048,100]{1,0:T(8,128)} %copy.52.mix_in_ref, ...), custom_call_target="tpu_custom_call" | custom-call | tf_op jit(solution)/shard_map/streams/pallas_call | solution.py:338
  46.4 393.6 %forward.1 = (bf16[8,128,2048]{2,1,0:T(8,128)(2,1)}, bf16[8,128,2048]{2,1,0:T(8,128)(2,1)}, bf16[8,128,2048]{2,1,0:T(8,128)(2,1)}, bf16[8,128,2048]{2,1,0:T(8,12...) custom-call(bf16[4,128,2048]{2,1,0:T(8,128)(2,1)} %get-tuple-element, ...), custom_call_target="tpu_custom_call" | custom-call | tf_op jit(solution)/shard_map/forward/pallas_call | solution.py:938
  440.0 168.7 %give_back.1 = (f32[128,2048]{1,0:T(8,128)}, f32[4,128,2048]{2,1,0:T(8,128)}, bf16[2,8,256,128]{3,2,1,0:T(8,128)(2,1)}, bf16[2,1,128,2048]{3,2,1,0:T(8,128)(2,1)...) custom-call(bf16[1024,256]{1,0:T(8,128)(2,1)} %get-tuple-element.50., ...), custom_call_target="tpu_custom_call" | custom-call | tf_op jit(solution)/shard_map/give_back/pallas_call | solution.py:1093
  608.7 96.7 %streams_back.1 = (bf16[9,128,2048]{2,1,0:T(8,128)(2,1)}, bf16[128,2048]{1,0:T(8,128)(2,1)}, f32[8,112,256]{2,1,0:T(8,128)}, bf16[2,8,256,128]{3,2,1,0:T(8,128)(2,1)}, bf16[2,1,128,2048]{3,2,1,0:T(8,128)(2,1)}) custom-call(bf16[2,8,256,128]{3,2,1,0:T(8,128)(2,1)} %get-tuple-element.64.p_v, bf16[2,1,128,2048]{3,2,1,0:T(8,128)(2,1)} %get-tuple-element.65.p_o, ...), custom_call_target="tpu_custom_call" | custom-call | tf_op jit(solution)/shard_map/streams_back/pallas_call | solution.py:1265
  705.4 0.0 copy-start
  705.4 1.6 fusion.4
  707.1 0.0 copy-start.1
  707.1 1.4 slice.45
  708.4 0.3 copy.59
  708.7 0.1 pad.12
  708.8 1.2 copy.64
  709.9 0.0 copy-done
  710.0 0.1 copy.62
  710.1 0.6 slice_bitcast_fusion
  710.7 0.0 copy-done.1
  710.7 3.6 pad_maximum_fusion
  714.3 5.4 turned_rows.6
  719.7 2.8 bitcast_convert_fusion.1
  722.5 5.4 turned_rows.4
  727.9 5.4 turned_rows.5
  733.3 6.7 bitcast_convert_fusion
  740.0 0.0 copy-start.4
  740.0 7.4 turned_rows.7
  747.4 0.0 copy-done.4
  747.4 0.8 copy.69
  748.2 5.2 copy.70
  (14 shorter events, 0.1 us)
Async XLA Ops:
  0.6 18.2 %copy-start.2 = (f32[256,2048]{1,0:T(8,128)S(1)}, f32[256,2048]{1,0:T(8,128)}, u32[]{:S(2)}) copy-start(f32[256,2048]{1,0:T(8,128)} %param.17) | copy-start | bytes 6291460
  18.8 4.6 copy-start.3
  18.8 9.3 %slice-start = ((s8[8388608]{0:T(1024)(128)(4,1)}), s8[4194304]{0:T(1024)(128)(4,1)S(1)}, s32[]{:S(2)}) async-start(s8[8388608]{0:T(1024)(128)(4,1)} %bitcast.47), calls=%async_computation | async-start | bytes 8388608
  23.4 4.7 slice-start.1
  26.9 4.1 slice-start.2
  28.2 4.5 slice-start.3
  705.4 4.5 copy-start
  707.1 3.6 copy-start.1
  740.0 7.5 copy-start.4

commit v4 on v3

--- a/solution.py
+++ b/solution.py
@@ -23,8 +23,7 @@
 
 CHUNKS = 4
 LANES = 128
-SLOTS = 4
-EARLY = 3
+SLOTS = 6
 
 
 def token_marks(tok_index, lengths):
@@ -576,11 +575,10 @@
         pass
 
     def phases(self):
-        listed = [self.begin, self.pause]
-        listed += [partial(self.relay, hop=hop) for hop in range(1, self.ends)]
+        listed = [partial(self.relay, hop=hop) for hop in range(1, self.ends)]
         listed += [self.meet, self.settle]
         if self.turned:
-            listed += [self.spread_end]
+            listed += [self.pause, self.spread_end]
         listed += [self.pass_on]
         listed += [partial(self.outward_hop, hop=hop) for hop in range(1, self.ends)]
         return listed
@@ -613,18 +611,19 @@
 
 
 class Ticks:
-    def __init__(self, jobs):
-        self.jobs = jobs
-        self.now = 0
+    def __init__(self, jobs, lead):
+        self.jobs, self.lead = jobs, lead
+        self.now, self.begun = 0, 0
 
     def tick(self, times=1):
         for _ in range(times):
-            if self.now < len(self.jobs):
-                line, chunk = self.jobs[self.now]
+            while self.begun < min(len(self.jobs), self.now + self.lead + 1):
+                line, chunk = self.jobs[self.begun]
                 line.begin(chunk)
+                self.begun += 1
             for i, (line, chunk) in enumerate(self.jobs):
-                phase = self.now - i
-                if 0 < phase < len(line.phases()):
+                phase = self.now - i - 1
+                if 0 <= phase < len(line.phases()):
                     line.phases()[phase](chunk)
             self.now += 1
 
@@ -682,17 +681,16 @@
 
 
 def forward_lines(nf, wide, hidden):
-    count = EARLY * (hidden // CHUNKS // LANES)
-    return Lines(nf, [((1, LANES, D), count, False), ((nf, D // nf, LANES), count, True)])
+    return Lines(nf, [((1, LANES, D), hidden // LANES, False)])
 
 
 def forward_kernel(nf, ns, lines, *refs):
     (low, g_ref, win_ref, wout_ref, wq_ref, wk_ref, wv_ref, wo_ref, planes_ref, lens_ref) = refs[:10]
     refs = refs[10:]
-    (xq_out, xk_out, xv_out, gg_out, win_out, h_out, dup_out, w_out, rest_out, rest_in) = refs[:10]
-    refs = refs[10:]
-    sum_out, sum_in, att_ref, dq_ref, dk_ref, dv_ref = refs[:6]
-    refs = refs[6:]
+    (xq_out, xk_out, xv_out, gg_out, pr_out, py_out, w_out, rest_in) = refs[:8]
+    refs = refs[8:]
+    sum_out, att_ref, dq_ref, dk_ref, dv_ref = refs[:5]
+    refs = refs[5:]
     (xr, gg, wfull, hid, dup, p_out, p_in, stage, wqkv, qkva, zin, zout, zback, dkv) = refs[:14]
     send_sem, recv_sem, copy_sem = refs[14:17]
     line_refs = refs[17:]
@@ -710,12 +708,8 @@
     pieces = width // LANES
     step_sems = nf - 1
     greet(nf, ns)
-    l_out, l_in = lines.build(plane, ns, (p_out, p_in), (sum_out, sum_in), line_refs)
-    jobs = []
-    for n in range(EARLY):
-        jobs += [(l_out, n * pieces + k) for k in range(pieces)]
-        jobs += [(l_in, n * pieces + k) for k in range(pieces)]
-    ticks = Ticks(jobs)
+    (l_out,) = lines.build(plane, ns, (p_out,), (sum_out,), line_refs)
+    ticks = Ticks([(l_out, chunk) for chunk in range(l_out.count)], 1)
     ag_r = Gather(plane, low.at[3], xr, sems, 0)
     ag_g = Gather(plane, g_ref, gg, sems, step_sems)
     ag_x = [
@@ -749,10 +743,11 @@
     ag_g.finish()
     for keep in keeps:
         keep.wait()
-    saves = []
+    saves, started = [], []
 
     def save(src, dst):
-        saves.append(pltpu.make_async_copy(src, dst, copy_sem.at[9 + len(saves)]))
+        started.append(dst)
+        saves.append(pltpu.make_async_copy(src, dst, copy_sem.at[8 + len(started)]))
         saves[-1].start()
 
     save(gg, gg_out)
@@ -788,12 +783,19 @@
         loop(D // WIDTH, grad_step)
         ticks.tick()
 
-    early = EARLY * pieces
-    save(wfull, win_out)
-    save(hid, h_out)
-    save(dup, dup_out)
-    save(p_out.at[pl.ds(early, CHUNKS * pieces - early)], rest_out)
-    save(p_in.at[pl.ds(early, CHUNKS * pieces - early)], rest_in)
+    save(p_in, rest_in)
+
+    def partial_sums(left, right, right_dim, out):
+        def step(i):
+            feats = tile(i, WIDTH)
+            block = right[feats, :] if right_dim else right[:, feats]
+            value = dot(left[...], block, 1, right_dim).astype(BF)
+            stage[:, :, feats] = value.reshape(nf, tok, WIDTH)
+
+        loop(D // WIDTH, step)
+        save(stage, out)
+
+    partial_sums(dup, wfull, 1, pr_out)
 
     def ship(i):
         for step in range(1, ns):
@@ -812,6 +814,9 @@
         ag_x[i].forward()
         turns[i].arrive(0)
         ag_x[i].finish()
+        if i == 0:
+            saves[-1].wait()
+            saves.pop()
         load = pltpu.make_async_copy(ag_x[i].buf, stage, copy_sem.at[15])
         load.start()
         load.wait()
@@ -830,6 +835,7 @@
         ship(i)
         ticks.tick(2 if i < 2 else 1)
     save(wqkv, w_out)
+    partial_sums(hid, wout_ref, 0, py_out)
     for i in range(4):
         for step in range(1, ns):
             there.copy(zin.at[i, 0], zin.at[i, wrap(sq - step, ns)], i, step).wait_recv()
@@ -930,9 +936,7 @@
     flat = shape((nf * tok, wide))
     block = shape((nf, tok, D))
     total = CHUNKS * (hidden // CHUNKS // LANES)
-    rest = total - lines.kinds[0][1]
-    outs = [block] * 4 + [shape((D, hidden))] + [shape((nf * tok, hidden))] * 2
-    outs += [shape((3, D, wide)), shape((rest, 1, LANES, D)), shape((rest, nf, D // nf, LANES))]
+    outs = [block] * 6 + [shape((3, D, wide)), shape((total, nf, D // nf, LANES))]
     outs += lines.outs() + [flat] * 4
     exchange = pltpu.VMEM((4, ns, nf // ns * tok, wide), BF)
     return pl.pallas_call(
@@ -943,7 +947,7 @@
         + [hbm()] * 3
         + [vmem()] * 2
         + [pl.BlockSpec(memory_space=pltpu.SMEM)],
-        out_specs=(hbm(),) * 12 + (vmem(),) * 4,
+        out_specs=(hbm(),) * 9 + (vmem(),) * 4,
         scratch_shapes=[
             pltpu.VMEM((nf, tok, D), BF),
             pltpu.VMEM((nf, tok, D), BF),
@@ -970,37 +974,44 @@
 
 
 TENSORS = 5
-
-
-def return_lines(nf, wide, rest):
-    count = wide // LANES
-    kinds = [((1, LANES, D), rest, False), ((nf, D // nf, LANES), rest, True)]
-    return Lines(nf, kinds + [((nf, D // nf, LANES), count, True)] * 2)
-
-
-def return_kernel(nf, ns, lines, *refs):
-    att_ref, dq_ref, dk_ref, dv_ref, dup_ref, wqkv, win_ref, wo_ref, wout_ref, h_ref = refs[:10]
-    p_out, p_in = refs[10:12]
-    sources = refs[12:16]
-    refs = refs[16:]
-    y_ref, dx_ref, dwv_ref, dwo_ref = refs[:4]
-    results = refs[4:8]
-    refs = refs[8:]
-    stage, part, sib, rec, p_q, p_k, send_sem, recv_sem, copy_sem, credit = refs[:10]
-    line_refs = refs[10:]
+SMALL = 112
+
+
+def back_lines(nf, wide, rest):
+    counts = [rest] + [wide // LANES] * 3
+    kinds = [((nf, D // nf, LANES), count, True) for count in counts]
+    return Lines(nf, kinds + [((1, LANES, D), wide // LANES, False)])
+
+
+def back_kernel(nf, ns, lines, *refs):
+    att_ref, dq_ref, dk_ref, dv_ref, wqkv, wo_ref, p_in, g_ref = refs[:8]
+    coef_ref, inv_ref, pre_ref, act_ref, mixed_ref, mix_in_ref, mix_out_ref = refs[8:15]
+    again_ref, mgain_ref, xgain_ref = refs[15:18]
+    sources, (pr_ref, py_ref, hist_ref, st_ref) = refs[18:22], refs[22:26]
+    lo_ref, sm_out, hg_ref = refs[26:29]
+    results, refs = refs[29:34], refs[34:]
+    stage, part, sib, rec, grads, p_o, dx_ref, y_ref = refs[:8]
+    hists, sts, hgs, h8, ds, dcoef, gsum = refs[8:15]
+    sm_ref, sm_src, sm_in, sm_z, sm_sem, sm_rsem = refs[15:21]
+    send_sem, recv_sem, copy_sem, tile_sem, credit = refs[21:26]
+    line_refs = refs[26:]
+    dmixed, last = dx_ref.at[0], dx_ref.at[1]
     plane = Plane(nf)
     sems = (send_sem, recv_sem)
-    tok = y_ref.shape[0]
+    tok = lo_ref.shape[0]
     wide = wo_ref.shape[0]
     parts, sibs = part.shape[0], sib.shape[0]
     greet(nf, ns)
-    built = lines.build(plane, ns, (p_out, p_in, p_q, p_k), results, line_refs)
+    built = lines.build(plane, ns, (p_in, *[grads.at[t] for t in range(3)], p_o), results, line_refs)
     jobs = []
     for line in built:
         jobs += [(line, chunk) for chunk in range(line.count)]
-    ticks = Ticks(jobs)
-    load = pltpu.make_async_copy(sources[0], stage, copy_sem)
+    ticks = Ticks(jobs, 1)
+    small = Small(plane, ns, sm_src, sm_in, sm_z, sm_out, (sm_sem, sm_rsem))
+    ticks.tick()
+    load = pltpu.make_async_copy(sources[0], stage, copy_sem.at[0])
     load.start()
+    pltpu.make_async_copy(hist_ref.at[HIST - 1], h8, copy_sem.at[1]).start()
     scats = [
         Scatter(
             plane,
@@ -1013,7 +1024,7 @@
         )
         for t in range(TENSORS)
     ]
-    firsts = (dq_ref, dk_ref, dv_ref, dup_ref)
+    firsts = (dq_ref, dk_ref, dv_ref)
 
     def total(t):
         def total_step(chunk):
@@ -1021,7 +1032,7 @@
             if t < 4:
                 dx_ref[t, :, feats] = scats[t].total(chunk)
             else:
-                y_ref[:, feats] = scats[t].total(chunk)
+                lo_ref[:, feats] = (y_ref[:, feats] + scats[t].total(chunk)).astype(BF)
 
         loop(CHUNKS, total_step)
         if t + sibs < TENSORS:
@@ -1030,21 +1041,31 @@
                     credit.at[t], inc=1, device_id={"fsdp": target}, device_id_type=MESH
                 )
 
-    ticks.tick()
+    def fetch(t, chunk):
+        feats = slice(chunk * (D // CHUNKS), (chunk + 1) * (D // CHUNKS))
+        src = (pr_ref, py_ref)[t - 3].at[:, :, feats]
+        return pltpu.make_async_copy(src, scats[t].part.at[:, :, feats], copy_sem.at[2 + chunk])
+
     for t in range(TENSORS):
         if t >= sibs:
             pl.semaphore_wait(credit.at[t - sibs], plane.chips)
+        if t >= 3:
+            for chunk in range(CHUNKS):
+                scats[t - parts].drain(chunk)
+                fetch(t, chunk).start()
         for chunk in range(CHUNKS):
             feats = slice(chunk * (D // CHUNKS), (chunk + 1) * (D // CHUNKS))
-            if t >= parts:
-                scats[t - parts].drain(chunk)
             if t < 3:
+                if t >= parts:
+                    scats[t - parts].drain(chunk)
                 value = dot(firsts[t][...], wqkv[t, feats, :], 1, 1)
-            elif t == 3:
-                value = dot(dup_ref[...], win_ref[feats, :], 1, 1)
+                scats[t].part[:, :, feats] = value.astype(BF).reshape(nf, tok, D // CHUNKS)
             else:
-                value = dot(att_ref[...], wo_ref[:, feats]) + dot(h_ref[...], wout_ref[:, feats])
-            scats[t].part[:, :, feats] = value.astype(BF).reshape(nf, tok, D // CHUNKS)
+                fetch(t, chunk).wait()
+            if t == 4:
+                value = dot(att_ref[...], wo_ref[:, feats]).reshape(nf, tok, D // CHUNKS)
+                value = value + scats[t].part[:, :, feats].astype(F32)
+                scats[t].part[:, :, feats] = value.astype(BF)
             scats[t].start(chunk)
             if chunk > 0:
                 scats[t].combine(chunk - 1)
@@ -1052,7 +1073,7 @@
                 ticks.tick()
         scats[t].combine(CHUNKS - 1)
         if t < 4:
-            pltpu.make_async_copy(sources[t], stage, copy_sem).wait()
+            pltpu.make_async_copy(sources[t], stage, copy_sem.at[0]).wait()
 
             def grad_step(i, t=t):
                 feats = tile(i, WIDTH)
@@ -1063,140 +1084,64 @@
                     for k in range(wide // LANES):
                         piece = grad[:, k * LANES : k * LANES + LANES]
                         piece = piece.reshape(count, D // nf, LANES)
-                        (p_q, p_k, dwv_ref)[t][k, pl.ds(i * count, count)] = piece
+                        grads[t, k, pl.ds(i * count, count)] = piece
                 else:
                     grad = dot(att_ref[...], every, 0, 0).astype(BF)
                     for k in range(wide // LANES):
-                        dwo_ref[k, 0, :, feats] = grad[k * LANES : k * LANES + LANES]
+                        p_o[k, 0, :, feats] = grad[k * LANES : k * LANES + LANES]
 
             loop(D // WIDTH, grad_step)
             if t < 3:
-                pltpu.make_async_copy(sources[t + 1], stage, copy_sem).start()
+                pltpu.make_async_copy(sources[t + 1], stage, copy_sem.at[0]).start()
         if t:
             total(t - 1)
-    total(TENSORS - 1)
-    ticks.finish()
-    for t in range(TENSORS - parts, TENSORS):
-        loop(CHUNKS, scats[t].drain)
-
-
-def run_return(nf, ns, att, ds, dup, wqkv, win, wo, wout, h, p_out, p_in, gg, xgs):
-    tok = gg.shape[1]
-    wide = wo.shape[0]
-    chips = nf // 2
-    count = TENSORS * CHUNKS * (nf - 1)
-    parts = 2 if nf <= 8 else 1
-    lines = return_lines(nf, wide, p_out.shape[0])
-    turned = (wide // LANES, nf, D // nf, LANES)
-    outs = [shape((tok, D), F32), shape((4, tok, D), F32), shape(turned)]
-    outs += [shape((wide // LANES, 1, LANES, D))] + lines.outs()
-    return pl.pallas_call(
-        partial(return_kernel, nf, ns, lines),
-        out_shape=tuple(outs),
-        in_specs=[vmem()] * 12 + [hbm()] * 4,
-        out_specs=(vmem(),) * 4 + (hbm(),) * 4,
-        scratch_shapes=[
-            pltpu.VMEM((nf, tok, D), BF),
-            pltpu.VMEM((parts, nf, tok, D), BF),
-            pltpu.VMEM((2, chips, tok, D), BF),
-            pltpu.VMEM((2, chips - 1, tok, D), BF),
-            pltpu.VMEM(turned, BF),
-            pltpu.VMEM(turned, BF),
-            pltpu.SemaphoreType.DMA((count,)),
-            pltpu.SemaphoreType.DMA((count,)),
-            pltpu.SemaphoreType.DMA,
-            pltpu.SemaphoreType.REGULAR((TENSORS - 2,)),
-        ]
-        + lines.scratch(),
-        compiler_params=params(2),
-        name="give_back",
-    )(att, *ds, dup, wqkv, win, wo, wout, h, p_out, p_in, *xgs, gg)
-
-
-SMALL = 112
-
-
-def end_lines(nf, wide):
-    count = wide // LANES
-    return Lines(nf, [((nf, D // nf, LANES), count, True), ((1, LANES, D), count, False)])
-
-
-def end_kernel(
-    nf,
-    ns,
-    lines,
-    p_v,
-    p_o,
-    hist_ref,
-    st_ref,
-    dx_ref,
-    g_ref,
-    y_ref,
-    coef_ref,
-    inv_ref,
-    pre_ref,
-    act_ref,
-    mixed_ref,
-    mix_in_ref,
-    mix_out_ref,
-    again_ref,
-    mgain_ref,
-    xgain_ref,
-    hg_ref,
-    lo_ref,
-    sm_out,
-    sum_v,
-    sum_o,
-    ds,
-    last,
-    dmixed,
-    dcoef,
-    gsum,
-    sm_ref,
-    sm_src,
-    sm_in,
-    sm_z,
-    sm_sem,
-    sm_rsem,
-    *line_refs,
-):
-    tok = hist_ref.shape[1]
-    plane = Plane(nf)
-    greet(nf, ns)
-    built = lines.build(plane, ns, (p_v, p_o), (sum_v, sum_o), line_refs)
-    jobs = []
-    for line in built:
-        jobs += [(line, chunk) for chunk in range(line.count)]
-    ticks = Ticks(jobs)
-    small = Small(plane, ns, sm_src, sm_in, sm_z, sm_out, (sm_sem, sm_rsem))
-    ticks.tick(2)
+
     gsum[...] = jnp.zeros_like(gsum)
+    steps = tok // ROWS
+
+    def tiles_in(i, slot):
+        rows = pl.ds(i * ROWS, ROWS)
+        first = pltpu.make_async_copy(hist_ref.at[:, rows, :], hists.at[slot], tile_sem.at[slot])
+        second = pltpu.make_async_copy(st_ref.at[:, rows, :], sts.at[slot], tile_sem.at[2 + slot])
+        return first, second
+
+    def tiles_out(i, slot):
+        rows = pl.ds(i * ROWS, ROWS)
+        dst = hg_ref.at[pl.ds(0, HIST - 1), rows, :]
+        return pltpu.make_async_copy(hgs.at[slot], dst, tile_sem.at[4 + slot])
 
     def back(value, inv, gain, grad):
         scaled = grad * gain
         mean = jnp.sum(value * scaled, axis=1, keepdims=True) / D
         return inv * scaled - value * (inv * inv * inv * mean)
 
-    def row_step(i):
-        rows = tile(i, ROWS)
+    def row_step(i, slot):
+        rows = pl.ds(i * ROWS, ROWS)
+        for copy in tiles_in(i, slot):
+            copy.wait()
+        if i + 1 < steps:
+            for copy in tiles_in(i + 1, 1 - slot):
+                copy.start()
+        if i > 1:
+            tiles_out(i - 2, slot).wait()
         coef = coef_ref[rows, :]
         lane = lax.broadcasted_iota(jnp.int32, (ROWS, STREAMS * HIST), 1)
         for c in range(STREAMS):
-            value, inv = st_ref[c, rows, :], inv_ref[c, rows, :]
+            value, inv = sts[slot, c], inv_ref[c, rows, :]
             grad = dx_ref[c, rows, :]
             gain = mgain_ref if c == STREAMS - 1 else again_ref
             gsum[c // 3] += grad * (value * inv)
             d_value = back(value, inv, gain[...], grad)
             if c == STREAMS - 1:
                 d_value = d_value + g_ref[rows, :].astype(F32)
-                lo_ref[rows, :] = (value + y_ref[rows, :]).astype(BF)
+                y_ref[rows, :] = value
             ds[c] = d_value
         found = jnp.zeros((ROWS, STREAMS * HIST), F32)
         for j in range(HIST):
             sums = [jnp.zeros((ROWS, 128), F32)] * STREAMS
             for begin in range(0, D, WIDTH):
                 cols = slice(begin, begin + WIDTH)
-                entry = hist_ref[j, rows, cols].astype(F32)
+                entry = hists[slot, j, :, cols].astype(F32)
                 grad = jnp.zeros((ROWS, WIDTH), F32)
                 for c in range(STREAMS):
                     at = c * HIST + j
@@ -1206,18 +1151,22 @@
                     for k in range(0, WIDTH, 128):
                         sums[c] = sums[c] + product[:, k : k + 128]
                 if j < HIST - 1:
-                    hg_ref[j, rows, cols] = grad.astype(BF)
+                    hgs[slot, j, :, cols] = grad.astype(BF)
                 else:
                     last[rows, cols] = grad
             for c in range(STREAMS):
                 value = jnp.sum(sums[c], axis=1, keepdims=True)
                 found = jnp.where(lane == c * HIST + j, value, found)
         dcoef[rows, :] = found.astype(BF)
-
-    loop(tok // ROWS // 2, row_step)
-    ticks.tick()
-    loop(tok // ROWS // 2, lambda i: row_step(i + tok // ROWS // 2))
-    ticks.tick()
+        tiles_out(i, slot).start()
+
+    for copy in tiles_in(0, 0):
+        copy.start()
+    for i in range(steps):
+        row_step(i, i % 2)
+        if i % 2:
+            ticks.tick()
+    total(TENSORS - 1)
     mix_in, mix_out = mix_in_ref[...].astype(BF), mix_out_ref[...].astype(BF)
     pre, d_coef = pre_ref[...], dcoef[...]
     slope = 0.5 * (1.0 + lax.erf(pre * (0.5**0.5)))
@@ -1226,15 +1175,17 @@
     hidden = pre.shape[1]
     sm_ref[0:hidden, :] = dot(d_pre, mixed_ref[...], 0, 0)
     dmixed[...] = dot(d_pre, mix_in, 1, 1)
+    pltpu.make_async_copy(hist_ref.at[HIST - 1], h8, copy_sem.at[1]).wait()
 
     def last_step(i):
         rows = tile(i, ROWS)
-        value, inv, grad = hist_ref[HIST - 1, rows, :].astype(F32), inv_ref[STREAMS, rows, :], dmixed[rows, :]
+        value, inv, grad = h8[rows, :].astype(F32), inv_ref[STREAMS, rows, :], dmixed[rows, :]
         gsum[2] += grad * (value * inv)
-        total = last[rows, :] + back(value, inv, xgain_ref[...], grad)
-        hg_ref[HIST - 1, rows, :] = total.astype(BF)
-
-    loop(tok // ROWS, last_step)
+        h8[rows, :] = (last[rows, :] + back(value, inv, xgain_ref[...], grad)).astype(BF)
+
+    loop(steps, last_step)
+    end = pltpu.make_async_copy(h8, hg_ref.at[HIST - 1], copy_sem.at[1])
+    end.start()
     for k in range(3):
         sm_ref[hidden + k : hidden + k + 1, :] = jnp.sum(gsum[k], axis=0, keepdims=True)
     begin = hidden + 3
@@ -1242,7 +1193,7 @@
     turned = dot(d_coef, act_ref[...], 0, 0)
     for k in range(STREAMS * HIST):
         at = begin + k // STREAMS
-        cols = slice(k % STREAMS * 128, k % STREAMS * 128 + hidden)
+        cols = slice(k % STREAMS * (D // nf), k % STREAMS * (D // nf) + hidden)
         sm_ref[at : at + 1, cols] = turned[k : k + 1, :]
     for k in range(nf):
         sm_src[k] = sm_ref[:, k * (D // nf) : (k + 1) * (D // nf)]
@@ -1253,24 +1204,43 @@
     small.finish()
     ticks.finish()
     small.drain()
-
-
-def run_end(nf, ns, p_v, p_o, *args):
-    tok = args[0].shape[1]
-    wide = p_v.shape[0] * LANES
-    lines = end_lines(nf, wide)
+    for t in range(TENSORS - parts, TENSORS):
+        loop(CHUNKS, scats[t].drain)
+    end.wait()
+    for i in (steps - 2, steps - 1):
+        tiles_out(i, i % 2).wait()
+
+
+def run_back(nf, ns, near, far):
+    wo = near[5]
+    tok = near[7].shape[0]
+    wide = wo.shape[0]
+    chips = nf // 2
     cols = D // nf
+    count = TENSORS * CHUNKS * (nf - 1)
     few = 2 * (nf - 1) + ns - 1
-    outs = [shape((HIST, tok, D)), shape((tok, D)), shape((nf, SMALL, cols), F32)]
+    parts = 2 if nf <= 8 else 1
+    lines = back_lines(nf, wide, near[6].shape[0])
+    outs = [shape((tok, D)), shape((nf, SMALL, cols), F32), shape((HIST, tok, D))]
     return pl.pallas_call(
-        partial(end_kernel, nf, ns, lines),
+        partial(back_kernel, nf, ns, lines),
         out_shape=tuple(outs + lines.outs()),
-        in_specs=[vmem()] * 17,
-        out_specs=(vmem(),) * 3 + (hbm(),) * 2,
+        in_specs=[vmem()] * len(near) + [hbm()] * len(far),
+        out_specs=(vmem(),) * 2 + (hbm(),) * 6,
         scratch_shapes=[
+            pltpu.VMEM((nf, tok, D), BF),
+            pltpu.VMEM((parts, nf, tok, D), BF),
+            pltpu.VMEM((2, chips, tok, D), BF),
+            pltpu.VMEM((2, chips - 1, tok, D), BF),
+            pltpu.VMEM((3, wide // LANES, nf, D // nf, LANES), BF),
+            pltpu.VMEM((wide // LANES, 1, LANES, D), BF),
+            pltpu.VMEM((4, tok, D), F32),
+            pltpu.VMEM((tok, D), F32),
+            pltpu.VMEM((2, HIST, ROWS, D), BF),
+            pltpu.VMEM((2, STREAMS, ROWS, D), F32),
+            pltpu.VMEM((2, HIST - 1, ROWS, D), BF),
+            pltpu.VMEM((tok, D), BF),
             pltpu.VMEM((STREAMS, ROWS, D), F32),
-            pltpu.VMEM((tok, D), F32),
-            pltpu.VMEM((tok, D), F32),
             pltpu.VMEM((tok, STREAMS * HIST), BF),
             pltpu.VMEM((3, ROWS, D), F32),
             pltpu.VMEM((SMALL, D), F32),
@@ -1279,11 +1249,16 @@
             pltpu.VMEM((ns, SMALL, cols), F32),
             pltpu.SemaphoreType.DMA((few,)),
             pltpu.SemaphoreType.DMA((few,)),
+            pltpu.SemaphoreType.DMA((count,)),
+            pltpu.SemaphoreType.DMA((count,)),
+            pltpu.SemaphoreType.DMA((2 + CHUNKS,)),
+            pltpu.SemaphoreType.DMA((6,)),
+            pltpu.SemaphoreType.REGULAR((TENSORS - 2,)),
         ]
         + lines.scratch(),
-        compiler_params=params(3),
-        name="streams_back",
-    )(p_v, p_o, *args)
+        compiler_params=params(2, 63),
+        name="back",
+    )(*near, *far)
 
 
 class Small:
@@ -1343,25 +1318,61 @@
             self.along(step).wait_send()
 
 
-def turned_kernel(*refs):
-    out_ref, at = refs[-1], 0
-    for ref in refs[:-1]:
+def finish_kernel(units, *refs):
+    sum_in, sum_q, sum_k, sum_v, out_ref, sm_ref = refs[:6]
+    w_in, wq, wk, wv, w_out, mix_in, mix_out, again, mgain, xgain = refs[6:]
+    for dst, ref in ((w_in, sum_in), (wq, sum_q), (wk, sum_k), (wv, sum_v)):
         for k in range(ref.shape[0]):
-            out_ref[:, at : at + LANES] = ref[k, 0].astype(F32)
-            at += LANES
-
-
-def turned_rows(*parts):
-    _, nf, rows, _ = parts[0].shape
-    wide = sum(p.shape[0] for p in parts) * LANES
+            dst[:, k * LANES : (k + 1) * LANES] = ref[k, 0].astype(F32)
+    w_out[...] = out_ref[...].astype(F32)
+    mix_in[...] = sm_ref[0, 0:units, :]
+    for k, dst in enumerate((again, mgain, xgain)):
+        dst[...] = sm_ref[0, units + k : units + k + 1, :]
+
+    @pl.when(pl.program_id(0) < STREAMS)
+    def _():
+        mix_out[0] = sm_ref[0, units + 3 : units + 3 + HIST, 0:LANES]
+
+
+def run_finish(nf, units, turned, out, small):
+    cols = D // nf
+    hidden = out.shape[0]
+    wide = turned[1].shape[0] * LANES
+    rows = turned[0].shape[2]
+
+    def chunks(part):
+        return pl.BlockSpec((part.shape[0], 1, rows, LANES), lambda i: (0, i, 0, 0))
+
+    def block(height, width):
+        return pl.BlockSpec((height, width), lambda i: (0, i))
+
     return pl.pallas_call(
-        turned_kernel,
+        partial(finish_kernel, units),
         grid=(nf,),
-        out_shape=shape((rows, nf * wide), F32),
-        in_specs=[pl.BlockSpec((p.shape[0], 1, rows, LANES), lambda i: (0, i, 0, 0)) for p in parts],
-        out_specs=pl.BlockSpec((rows, wide), lambda i: (0, i)),
-        name="turned_rows",
-    )(*parts)
+        out_shape=(
+            shape((rows, nf * hidden), F32),
+            *[shape((rows, D), F32)] * 3,
+            shape((hidden, D), F32),
+            shape((units, D), F32),
+            shape((STREAMS, HIST, LANES), F32),
+            *[shape((1, D), F32)] * 3,
+        ),
+        in_specs=[
+            *[chunks(part) for part in turned],
+            pl.BlockSpec((hidden // nf, D), lambda i: (i, 0)),
+            pl.BlockSpec((1, SMALL, cols), lambda i: (i, 0, 0)),
+        ],
+        out_specs=(
+            block(rows, hidden),
+            *[block(rows, wide)] * 3,
+            pl.BlockSpec((hidden // nf, D), lambda i: (i, 0)),
+            block(units, cols),
+            pl.BlockSpec((1, HIST, LANES), lambda i: (jnp.minimum(i, STREAMS - 1), 0, 0)),
+            *[block(1, cols)] * 3,
+        ),
+        compiler_params=pltpu.CompilerParams(vmem_limit_bytes=40 * MIB),
+        name="finish",
+    )(*turned, out, small)
 
 
 def local(
@@ -1394,47 +1405,31 @@
     grad_out = cotangent[0]
     ws = [w.astype(BF) for w in (wq, wk, wv)]
     wo_low, win_low, wout_low = wo.astype(BF), w_in.astype(BF), w_out.astype(BF)
-    *xgs, gg, win_full, hidden, dup, wqkv, rest_out, rest_in, out_a, in_a, att, dq, dk, dv = run_forward(
+    *xgs, gg, pr, py, wqkv, p_in, sum_out, att, dq, dk, dv = run_forward(
         nf, ns, low, grad_out, win_low, wout_low, ws, wo_low, planes, lens
     )
-    y_sum, dx, dwv, dwo, out_b, in_b, sum_q, sum_k = run_return(
-        nf,
-        ns,
-        att,
-        (dq, dk, dv),
-        dup,
-        wqkv,
-        win_full,
-        wo_low,
-        wout_low,
-        hidden,
-        rest_out,
-        rest_in,
-        gg,
-        xgs,
+    near = (att, dq, dk, dv, wqkv, wo_low, p_in, grad_out)
+    near += (coef, inv, pre, act, mixed, mix_in, mix_out, *gains)
+    far = (*xgs, gg, pr, py, hist, stream)
+    layer_out, small, history_grad, sum_in, *sums, sum_o = run_back(nf, ns, near, far)
+    dwo = sum_o.reshape(wo.shape).astype(F32)
+    units = mix_in.shape[1]
+    dw_in, dwq, dwk, dwv, dwout, dmix_in, dmix_out, *dgains = run_finish(
+        nf, units, (sum_in, *sums), sum_out.reshape(w_out.shape), small
     )
-    history_grad, layer_out, small, sum_v, sum_o = run_end(
-        nf, ns, dwv, dwo, hist, stream, dx, grad_out, y_sum, coef, inv, pre, act, mixed, mix_in, mix_out, *gains
-    )
-    dwout = jnp.concatenate([out_a, out_b], axis=0).reshape(w_out.shape).astype(F32)
-    dwo = sum_o.reshape(wo.shape).astype(F32)
-    dw_in = turned_rows(in_a, in_b)
-    dw_qkv = [turned_rows(s) for s in (sum_q, sum_k, sum_v)]
-    small = small.transpose(1, 0, 2).reshape(SMALL, D)
-    units = mix_in.shape[1]
-    mix_out_rows = small[units + 3 :, : STREAMS * 128].reshape(HIST * STREAMS, 128)
+    dmix_out = dmix_out.transpose(2, 1, 0).reshape(LANES, STREAMS * HIST)[:units]
     return (
         layer_out[None],
         history_grad[:, None],
-        *dw_qkv,
+        dwq,
+        dwk,
+        dwv,
         dwo,
         dw_in,
         dwout,
-        small[:units].T,
-        mix_out_rows[:, :units].T,
-        small[units],
-        small[units + 1],
-        small[units + 2],
+        dmix_in.T,
+        dmix_out,
+        *[grad[0] for grad in dgains],
     )
 
 

time: 763 us -> 629 us (0.82)
  Pallas kernels: 694 us -> 566 us
  other arithmetic: 30.4 us -> 20.2 us
    pallas_call x1, Pallas kernels: 394 us -> 280 us  [run_forward(): pl.pallas_call(partial(forward_kernel, nf, ns, lines), out_shape=tuple(ou...]
    pallas_call x6 -> x2, Pallas kernels: 289 us -> 274 us  [the longest x1 266 us: run_back(): pl.pallas_call(partial(back_kernel, nf, ns, lines), out_shape=tuple(outs...]
    unnamed x27 -> x33, local copies, waits for them, and re-layouts: 13.6 us -> 21.7 us
where the time goes in v4:
time: 629 us; the launch traced here: 620 us
  Pallas kernels  566 us (90%)
  local copies, waits for them, and re-layouts  22.6 us (4%)
  other arithmetic  20.2 us (3%)
  blocking collectives  10.4 us (2%)
    pallas_call x1, Pallas kernels, run_forward(): pl.pallas_call(partial(forward_kernel, nf, ns, lines), out_shape=tuple(ou...  280 us
    pallas_call x1, Pallas kernels, run_back(): pl.pallas_call(partial(back_kernel, nf, ns, lines), out_shape=tuple(outs...  266 us
    unnamed x33, local copies, waits for them, and re-layouts  21.7 us

profile of v4, /device:TPU:0, one launch (start us, length us, event | category | flops | bytes accessed | tf_op | source)
XLA Modules:
  0.0 620.2 jit_solution(1726090308733509918)
XLA Ops:
  0.6 0.0 copy-start.6
  0.7 0.1 pad.9.clone
  0.8 0.1 pad.6.clone
  0.9 10.4 %all-gather = s32[8,1,3]{2,1,0:T(1,128)S(1)} all-gather(s32[1,1,3]{2,1,0:T(1,128)} %bitcast.61), channel_id=1, replica_groups=mesh['seq'=4,'fsdp'=8] {'fsdp'}, dimensions={0}, use_global_device_ids=true | all-gather | bytes 108 | tf_op jit(solution)/shard_map/all_gather | solution.py:1398
  11.3 0.1 copy.52
  11.4 0.7 copy.54.refs_9_
  12.1 0.1 broadcast_bitcast_fusion
  12.2 1.4 copy.51.mix_out_ref.refs_14_
  13.6 2.7 convert_element_type.41.refs_7_.refs_5_
  16.3 2.5 copy.50.mix_in_ref.refs_13_
  18.8 0.0 copy-done.6
  18.8 0.0 copy-start.7
  18.8 0.0 slice-start
  18.8 1.1 convert_element_type.38.refs_4_
  20.0 3.5 convert_element_type.39.refs_5_
  23.4 0.0 copy-done.7
  23.4 0.0 slice-start.1
  23.4 1.1 convert_element_type.40.refs_6_
  24.6 1.9 multiply_cosine_fusion
  26.5 0.3 maximum_bitcast_fusion
  26.9 0.0 slice-start.2
  26.9 1.2 pad_maximum_fusion.refs_8_
  28.1 0.0 slice-done
  28.1 0.0 slice-done.1
  28.1 0.0 slice-start.3
  28.1 2.7 convert_element_type.36.refs_2_
  30.9 0.0 slice-done.2
  30.9 1.7 slice-done.3
  32.6 2.7 convert_element_type.37.refs_3_
  35.3 11.2 %streams.1 = (bf16[4,128,2048]{2,1,0:T(8,128)(2,1)}, f32[4,128,2048]{2,1,0:T(8,128)}, f32[128,36]{1,0:T(8,128)}, f32[5,128,1]{2,1,0:T(8,128)}, f32[128,100]{1,0:...) custom-call(bf16[9,128,2048]{2,1,0:T(8,128)(2,1)} %bitcast.40, f32[2048,100]{1,0:T(8,128)} %copy.50.mix_in_ref.refs_13_, ...), custom_call_target="tpu_custom_call" | custom-call | tf_op jit(solution)/shard_map/streams/pallas_call | solution.py:337
  46.5 280.2 %forward.1 = (bf16[8,128,2048]{2,1,0:T(8,128)(2,1)}, bf16[8,128,2048]{2,1,0:T(8,128)(2,1)}, bf16[8,128,2048]{2,1,0:T(8,128)(2,1)}, bf16[8,128,2048]{2,1,0:T(8,12...) custom-call(bf16[4,128,2048]{2,1,0:T(8,128)(2,1)} %get-tuple-element, ...), custom_call_target="tpu_custom_call" | custom-call | tf_op jit(solution)/shard_map/forward/pallas_call | solution.py:942
  326.7 265.7 %back.1 = (bf16[128,2048]{1,0:T(8,128)(2,1)}, f32[8,112,256]{2,1,0:T(8,128)}, bf16[9,128,2048]{2,1,0:T(8,128)(2,1)}, bf16[8,8,256,128]{3,2,1,0:T(8,128)(2,1)}, b...) custom-call(bf16[1024,256]{1,0:T(8,128)(2,1)} %get-tuple-element.52., ...), custom_call_target="tpu_custom_call" | custom-call | tf_op jit(solution)/shard_map/back/pallas_call | solution.py:1225
  592.4 2.8 bitcast_convert_fusion
  595.2 0.0 copy-start
  595.2 2.2 copy-done
  597.4 0.0 copy-start.1
  597.4 2.2 copy-done.1
  599.6 0.0 copy-start.2
  599.6 1.2 copy-done.2
  600.8 0.0 copy-start.3
  600.8 1.2 copy-done.3
  602.0 0.0 copy-start.4
  602.0 1.2 copy-done.4
  603.3 0.0 copy-start.5
  603.3 1.2 copy-done.5
  604.5 0.0 copy-start.8
  604.5 8.6 %finish.1 = (f32[256,8192]{1,0:T(8,128)}, f32[256,2048]{1,0:T(8,128)}, f32[256,2048]{1,0:T(8,128)}, f32[256,2048]{1,0:T(8,128)}, f32[1024,2048]{1,0:T(8,128)}, /...) custom-call(bf16[8,8,256,128]{3,2,1,0:T(8,128)(2,1)S(1)} %copy-done., ...), custom_call_target="tpu_custom_call" | custom-call | tf_op jit(solution)/shard_map/finish/pallas_call | solution.py:1349
  613.1 0.6 slice.19
  613.7 0.0 copy-done.8
  613.7 0.8 copy.64
  614.5 5.2 copy.65
  (13 shorter events, 0.1 us)
Async XLA Ops:
  0.6 18.2 %copy-start.6 = (f32[256,2048]{1,0:T(8,128)S(1)}, f32[256,2048]{1,0:T(8,128)}, u32[]{:S(2)}) copy-start(f32[256,2048]{1,0:T(8,128)} %param.17) | copy-start | bytes 6291460
  18.8 4.6 copy-start.7
  18.8 9.3 %slice-start = ((s8[8388608]{0:T(1024)(128)(4,1)}), s8[4194304]{0:T(1024)(128)(4,1)S(1)}, s32[]{:S(2)}) async-start(s8[8388608]{0:T(1024)(128)(4,1)} %bitcast.42), calls=%async_computation | async-start | bytes 8388608
  23.4 4.7 slice-start.1
  26.9 4.0 slice-start.2
  28.1 4.5 slice-start.3
  595.2 2.2 copy-start
  597.4 2.2 copy-start.1
  599.6 1.2 copy-start.2
  600.8 1.2 copy-start.3
  602.0 1.2 copy-start.4
  603.3 1.2 copy-start.5
  604.5 9.3 %copy-start.8 = (bf16[128,2048]{1,0:T(8,128)(2,1)S(1)}, bf16[128,2048]{1,0:T(8,128)(2,1)}, u32[]{:S(2)}) copy-start(bf16[128,2048]{1,0:T(8,128)(2,1)} %get-tuple-element.70) | copy-start | bytes 1572868

commit v5 on v4

--- a/solution.py
+++ b/solution.py
@@ -23,7 +23,7 @@
 
 CHUNKS = 4
 LANES = 128
-SLOTS = 6
+SLOTS = 4
 
 
 def token_marks(tok_index, lengths):
@@ -36,21 +36,25 @@
     return (segment, tok_index - seq_begin)
 
 
-def rope_planes(tok_place):
+def token_table(tok_index, lengths):
+    _, place = token_marks(tok_index, lengths)
     inverse = 10000.0 ** (-jnp.arange(0, ROT, 2, dtype=F32) / ROT)
-    angles = tok_place.astype(F32)[:, None] * inverse[None, :]
-    cosine, sine = jnp.cos(angles), jnp.sin(angles)
-    rows = tok_place.shape[0]
-    ones = jnp.ones((rows, HEAD - ROT), F32)
-    none = jnp.zeros((rows, HEAD - ROT // 2), F32)
-    gap = jnp.zeros((rows, ROT // 2), F32)
-    return jnp.stack(
-        [
-            jnp.concatenate([cosine, cosine, ones], axis=1),
-            jnp.concatenate([-sine, none], axis=1),
-            jnp.concatenate([gap, sine, none[:, : HEAD - ROT]], axis=1),
-        ]
-    )
+    angles = place.astype(F32)[:, None] * inverse[None, :]
+    rows = place.shape[0]
+    ends = jnp.stack([lengths[0], lengths[0] + lengths[1]]).astype(F32)
+    ends = jnp.broadcast_to(ends[None], (rows, 2))
+    rest = jnp.zeros((rows, LANES - ROT - 2), F32)
+    return jnp.concatenate([jnp.cos(angles), jnp.sin(angles), ends, rest], axis=1)
+
+
+def rope_planes(packed):
+    lane = lax.broadcasted_iota(jnp.int32, packed.shape, 1)
+    half = ROT // 2
+    cosine = jnp.where(lane < ROT, pltpu.roll(packed, half, 1), 1.0)
+    cosine = jnp.where(lane < half, packed, cosine)
+    low = jnp.where(lane < half, -pltpu.roll(packed, HEAD - half, 1), 0.0)
+    high = jnp.where((lane >= half) & (lane < ROT), packed, 0.0)
+    return cosine, low, high
 
 
 def dot(left_op, right_op, left_dim=1, right_dim=0):
@@ -274,82 +278,6 @@
 
 ROWS = 16
 WIDTH = 512
-
-
-def start_kernel(
-    hist_ref,
-    mix_in_ref,
-    mix_out_ref,
-    again_ref,
-    mgain_ref,
-    xgain_ref,
-    low_ref,
-    st_ref,
-    coef_ref,
-    inv_ref,
-    pre_ref,
-    act_ref,
-    mixed_ref,
-):
-    tok = hist_ref.shape[1]
-
-    def mix_step(i):
-        rows = tile(i, ROWS)
-        value = hist_ref[HIST - 1, rows, :].astype(F32)
-        inv = lax.rsqrt(jnp.mean(value * value, axis=1, keepdims=True) + EPSILON)
-        mixed_ref[rows, :] = (value * inv * xgain_ref[...]).astype(BF)
-        inv_ref[STREAMS, rows, :] = inv
-
-    loop(tok // ROWS, mix_step)
-    pre = dot(mixed_ref[...], mix_in_ref[...].astype(BF))
-    pre_ref[...] = pre
-    act = (0.5 * pre * (1.0 + lax.erf(pre * (0.5**0.5)))).astype(BF)
-    act_ref[...] = act
-    coef_ref[...] = dot(act, mix_out_ref[...].astype(BF))
-
-    def stream_step(i):
-        rows = tile(i, ROWS)
-        coef = coef_ref[rows, :]
-        squares = [jnp.zeros((ROWS, 1), F32)] * STREAMS
-        for begin in range(0, D, WIDTH):
-            cols = slice(begin, begin + WIDTH)
-            total = [jnp.zeros((ROWS, WIDTH), F32)] * STREAMS
-            for j in range(HIST):
-                entry = hist_ref[j, rows, cols].astype(F32)
-                for c in range(STREAMS):
-                    at = c * HIST + j
-                    total[c] = total[c] + coef[:, at : at + 1] * entry
-            for c in range(STREAMS):
-                st_ref[c, rows, cols] = total[c]
-                squares[c] = squares[c] + jnp.sum(total[c] * total[c], axis=1, keepdims=True)
-        for c in range(STREAMS):
-            inv = lax.rsqrt(squares[c] / D + EPSILON)
-            inv_ref[c, rows, :] = inv
-            gain = mgain_ref if c == STREAMS - 1 else again_ref
-            low_ref[c, rows, :] = (st_ref[c, rows, :] * inv * gain[...]).astype(BF)
-
-    loop(tok // ROWS, stream_step)
-
-
-def run_start(hist, mix_in, mix_out, again, mgain, xgain):
-    tok = hist.shape[1]
-    hidden = mix_in.shape[1]
-    return pl.pallas_call(
-        start_kernel,
-        out_shape=(
-            shape((STREAMS, tok, D)),
-            shape((STREAMS, tok, D), F32),
-            shape((tok, STREAMS * HIST), F32),
-            shape((STREAMS + 1, tok, 1), F32),
-            shape((tok, hidden), F32),
-            shape((tok, hidden)),
-            shape((tok, D)),
-        ),
-        in_specs=[vmem()] * 6,
-        out_specs=(vmem(),) * 7,
-        compiler_params=pltpu.CompilerParams(vmem_limit_bytes=62 * MIB),
-        name="streams",
-    )(hist, mix_in, mix_out, again, mgain, xgain)
 
 
 def rotated(value, planes):
@@ -614,6 +542,11 @@
     def __init__(self, jobs, lead):
         self.jobs, self.lead = jobs, lead
         self.now, self.begun = 0, 0
+
+    def open(self):
+        line, chunk = self.jobs[self.begun]
+        line.begin(chunk)
+        self.begun += 1
 
     def tick(self, times=1):
         for _ in range(times):
@@ -681,19 +614,23 @@
 
 
 def forward_lines(nf, wide, hidden):
-    return Lines(nf, [((1, LANES, D), hidden // LANES, False)])
+    width = hidden // CHUNKS
+    return Lines(nf, [((1, width, D * LANES // width), hidden // LANES, False)])
 
 
 def forward_kernel(nf, ns, lines, *refs):
-    (low, g_ref, win_ref, wout_ref, wq_ref, wk_ref, wv_ref, wo_ref, planes_ref, lens_ref) = refs[:10]
-    refs = refs[10:]
-    (xq_out, xk_out, xv_out, gg_out, pr_out, py_out, w_out, rest_in) = refs[:8]
-    refs = refs[8:]
-    sum_out, att_ref, dq_ref, dk_ref, dv_ref = refs[:5]
-    refs = refs[5:]
-    (xr, gg, wfull, hid, dup, p_out, p_in, stage, wqkv, qkva, zin, zout, zback, dkv) = refs[:14]
-    send_sem, recv_sem, copy_sem = refs[14:17]
-    line_refs = refs[17:]
+    hist_ref, g_ref, win_ref, wq_ref, wk_ref, wv_ref, wo_f32, wout_f32 = refs[:8]
+    tab_ref, mix_in_ref, mix_out_ref, again_ref, mgain_ref, xgain_ref = refs[8:14]
+    refs = refs[14:]
+    (xq_out, xk_out, xv_out, gg_out, py_out, w_out, rest_in) = refs[:7]
+    wo_out, wrow_out, win_out, st_out, sum_out = refs[7:12]
+    att_ref, dq_ref, dk_ref, dv_ref, dxr_ref = refs[12:17]
+    coef_ref, inv_ref, pre_ref, act_ref, mixed_ref = refs[17:22]
+    refs = refs[22:]
+    (xr, gg, wfull, hid, dup, p_out, p_in, stage, wqkv, zin, zback, dkv) = refs[:12]
+    wout_ref, wo_ref, wtile, sts, lows, h8, tab, sib, rec = refs[12:21]
+    send_sem, recv_sem, copy_sem = refs[21:24]
+    line_refs = refs[24:]
     plane = Plane(nf)
     sems = (send_sem, recv_sem)
     tok = g_ref.shape[0]
@@ -710,69 +647,225 @@
     greet(nf, ns)
     (l_out,) = lines.build(plane, ns, (p_out,), (sum_out,), line_refs)
     ticks = Ticks([(l_out, chunk) for chunk in range(l_out.count)], 1)
-    ag_r = Gather(plane, low.at[3], xr, sems, 0)
-    ag_g = Gather(plane, g_ref, gg, sems, step_sems)
+    ag_r = Gather(plane, xr.at[plane.me], xr, sems, 0)
     ag_x = [
-        Gather(plane, low.at[i], out, sems, (2 + i) * step_sems)
+        Gather(plane, out.at[plane.me], out, sems, (2 + i) * step_sems)
         for i, out in enumerate((xq_out, xk_out, xv_out))
     ]
-    turn = Turn(plane, win_ref, wfull, sems, 5 * step_sems, CHUNKS)
+    turn = Turn(plane, win_out, wfull, sems, 5 * step_sems, CHUNKS)
     turns = [
-        Turn(plane, w, wqkv.at[i], sems, (5 + CHUNKS + i) * step_sems, 1)
-        for i, w in enumerate((wq_ref, wk_ref, wv_ref))
+        Turn(plane, wrow_out.at[i], wqkv.at[i], sems, (5 + CHUNKS + i) * step_sems, 1)
+        for i in range(3)
     ]
-    base = (8 + CHUNKS) * step_sems
+    ag_t = Gather(plane, tab_ref, tab, sems, (8 + CHUNKS) * step_sems)
+    scat = Scatter(plane, xr, sib, rec, sems, (9 + CHUNKS) * step_sems, CHUNKS)
+    base = (9 + 2 * CHUNKS) * step_sems
+    part_cols = D // pieces
+    ag_gs = []
+    for p in range(pieces):
+        cols = slice(p * part_cols, (p + 1) * part_cols)
+        at = base + (p - 1) * step_sems if p else step_sems
+        ag_gs.append(Gather(plane, g_ref.at[:, cols], gg.at[:, :, cols], sems, at))
+    base += (pieces - 1) * step_sems
     there = Exchange(ns, sems, base)
     home = Exchange(ns, sems, base + 4 * (ns - 1))
+    late = HIST - 1
+    entries = pltpu.make_async_copy(hist_ref.at[pl.ds(0, late)], stage.at[pl.ds(0, late)], copy_sem.at[5])
+    newest = pltpu.make_async_copy(hist_ref.at[late], h8, copy_sem.at[6])
+    newest.start()
+    entries.start()
+    ag_gs[0].start()
+    keeps = [ag_gs[p].keep(copy_sem.at[8 + p]) for p in range(pieces)]
+    keeps.append(ag_t.keep(copy_sem.at[7]))
+    for keep in keeps:
+        keep.start()
+    high, broad = width, part_cols
+
+    def tiles_of(src, dst, store):
+        for r in range(0, src.shape[0], high):
+            for c in range(0, src.shape[1], broad):
+                where = (pl.ds(r, high), pl.ds(c, broad))
+                casts.append((src.at[where], dst.at[where], store))
+
+    def fetch(n):
+        return pltpu.make_async_copy(casts[n][0], wtile.at[n % 2], copy_sem.at[16 + n % 2])
+
+    def cast_all():
+        stores = []
+        fetch(0).start()
+        fetch(1).start()
+        for n, (_, dst, store) in enumerate(casts):
+            fetch(n).wait()
+            low = p_out.at[len(stores), 0] if store else dst
+
+            def cast_step(i, n=n, low=low):
+                rows = tile(i, ROWS)
+                low[rows, :] = wtile[n % 2, rows, :].astype(BF)
+
+            loop(high // ROWS, cast_step)
+            if n + 2 < len(casts):
+                fetch(n + 2).start()
+            if store:
+                stores.append(pltpu.make_async_copy(low, dst, copy_sem.at[18 + len(stores)]))
+                stores[-1].start()
+        for copy in stores:
+            copy.wait()
+
+    casts = []
+    tiles_of(win_ref, win_out, True)
+    cast_all()
+    turn.start(0)
+    keeps.append(turn.keep(copy_sem.at[1]))
+    keeps[-1].start()
+    newest.wait()
+
+    def mix_step(i):
+        rows = tile(i, ROWS)
+        value = h8[rows, :].astype(F32)
+        inv = lax.rsqrt(jnp.mean(value * value, axis=1, keepdims=True) + EPSILON)
+        mixed_ref[rows, :] = (value * inv * xgain_ref[...]).astype(BF)
+        inv_ref[STREAMS, rows, :] = inv
+
+    loop(tok // ROWS, mix_step)
+    pre = dot(mixed_ref[...], mix_in_ref[...].astype(BF), 1, 1)
+    pre_ref[...] = pre
+    act = (0.5 * pre * (1.0 + lax.erf(pre * (0.5**0.5)))).astype(BF)
+    act_ref[...] = act
+    coef_ref[...] = dot(act, mix_out_ref[...].astype(BF), 1, 1)
+    entries.wait()
+
+    def tiles_out(i, slot):
+        rows = tile(i, ROWS)
+        listed = [pltpu.make_async_copy(sts.at[slot], st_out.at[:, rows, :], copy_sem.at[26 + slot])]
+        for c, out in enumerate((xq_out, xk_out, xv_out)):
+            dst = out.at[plane.me, rows, :]
+            sem = copy_sem.at[28 + c * 2 + slot]
+            listed.append(pltpu.make_async_copy(lows.at[slot, c], dst, sem))
+        return listed
+
+    def stream_step(i):
+        slot = lax.rem(i, 2)
+        rows = tile(i, ROWS)
+
+        @pl.when(i > 1)
+        def _():
+            for copy in tiles_out(i - 2, slot):
+                copy.wait()
+
+        coef = coef_ref[rows, :]
+        squares = [jnp.zeros((ROWS, 1), F32)] * STREAMS
+        for begin in range(0, D, WIDTH):
+            cols = slice(begin, begin + WIDTH)
+            total = [jnp.zeros((ROWS, WIDTH), F32)] * STREAMS
+            for j in range(HIST):
+                entry = (stage[j, rows, cols] if j < late else h8[rows, cols]).astype(F32)
+                for c in range(STREAMS):
+                    at = c * HIST + j
+                    total[c] = total[c] + coef[:, at : at + 1] * entry
+            for c in range(STREAMS):
+                sts[slot, c, :, cols] = total[c]
+                squares[c] = squares[c] + jnp.sum(total[c] * total[c], axis=1, keepdims=True)
+        for c in range(STREAMS):
+            inv = lax.rsqrt(squares[c] / D + EPSILON)
+            inv_ref[c, rows, :] = inv
+            gain = mgain_ref if c == STREAMS - 1 else again_ref
+            normed = (sts[slot, c] * inv * gain[...]).astype(BF)
+            if c < STREAMS - 1:
+                lows[slot, c] = normed
+            else:
+                xr[plane.me, rows, :] = normed
+        for copy in tiles_out(i, slot):
+            copy.start()
+
+    steps = tok // ROWS
+    loop(steps, stream_step)
     ag_r.start()
-    turn.start(0)
-    ag_g.start()
+    for p in range(1, pieces):
+        ag_gs[p].start()
     for chunk in range(1, CHUNKS):
         turn.start(chunk)
+    ag_t.start()
+    for i in (steps - 2, steps - 1):
+        for copy in tiles_out(i, i % 2):
+            copy.wait()
+    ag_x[0].start()
+    casts = []
+    tiles_of(wout_f32, wout_ref, False)
+    tiles_of(wo_f32, wo_ref, False)
+    for i, w in enumerate((wq_ref, wk_ref, wv_ref)):
+        tiles_of(w, wrow_out.at[i], True)
+    cast_all()
     for i in range(3):
-        ag_x[i].start()
+        if i:
+            ag_x[i].start()
         turns[i].start(0)
-    keeps = [ag_r.keep(copy_sem.at[0]), ag_g.keep(copy_sem.at[1]), turn.keep(copy_sem.at[2])]
-    keeps += [ag_x[i].keep(copy_sem.at[3 + i]) for i in range(3)]
-    keeps += [turns[i].keep(copy_sem.at[6 + i]) for i in range(3)]
-    for keep in keeps:
-        keep.start()
+        keeps.append(turns[i].keep(copy_sem.at[2 + i]))
+        keeps[-1].start()
+    ag_gs[0].forward()
     ag_r.forward()
-    ag_g.forward()
+    ag_gs[0].finish()
     ag_r.finish()
-    ag_g.finish()
     for keep in keeps:
         keep.wait()
     saves, started = [], []
 
     def save(src, dst):
         started.append(dst)
-        saves.append(pltpu.make_async_copy(src, dst, copy_sem.at[8 + len(started)]))
+        saves.append(pltpu.make_async_copy(src, dst, copy_sem.at[36 + len(started)]))
         saves[-1].start()
 
+    save(wo_ref, wo_out)
+
+    def act(up):
+        return 0.5 * (1.0 + lax.erf(up * (0.5**0.5)))
+
+    def out_grad(chunk, p):
+        cols = slice(chunk * width, chunk * width + width)
+
+        def step(i):
+            feats = pl.ds(pl.multiple_of(p * part_cols + i * WIDTH, WIDTH), WIDTH)
+            every = gg[:, :, feats].reshape(nf * tok, WIDTH)
+            grad = dot(hid[:, cols], every, 0, 0).astype(BF)
+            p_out[chunk * pieces + p, 0, :, tile(i, WIDTH)] = grad
+
+        loop(part_cols // WIDTH, step)
+
+    def first_step(i):
+        rows = tile(i, blocks * tok)
+        up = dot(rows_of(xr, i * blocks, blocks), wfull[:, 0:width])
+        hid[rows, 0:width] = (up * act(up)).astype(BF)
+
+    turn.arrive(0)
+    loop(nf // blocks, first_step)
+    out_grad(0, 0)
+    ticks.open()
+    for p in range(1, pieces):
+        ag_gs[p].forward()
+        ag_gs[p].finish()
     save(gg, gg_out)
 
     for chunk in range(CHUNKS):
-        turn.arrive(chunk)
+        if chunk:
+            turn.arrive(chunk)
         cols = slice(chunk * width, chunk * width + width)
 
         def rows_step(i, cols=cols):
             rows = tile(i, blocks * tok)
             up = dot(rows_of(xr, i * blocks, blocks), wfull[:, cols])
             dh = dot(rows_of(gg, i * blocks, blocks), wout_ref[cols, :], 1, 1)
-            cdf = 0.5 * (1.0 + lax.erf(up * (0.5**0.5)))
+            cdf = act(up)
             slope = cdf + up * jnp.exp(-0.5 * up * up) * 0.3989422804014327
             hid[rows, cols] = (up * cdf).astype(BF)
             dup[rows, cols] = (dh * slope).astype(BF)
 
         loop(nf // blocks, rows_step)
 
+        for p in range(1 if chunk == 0 else 0, pieces):
+            out_grad(chunk, p)
+        ticks.tick()
+
         def grad_step(i, cols=cols, chunk=chunk):
             feats = tile(i, WIDTH)
-            every = gg[:, :, feats].reshape(nf * tok, WIDTH)
-            grad = dot(hid[:, cols], every, 0, 0).astype(BF)
-            for k in range(pieces):
-                p_out[chunk * pieces + k, 0, :, feats] = grad[k * LANES : k * LANES + LANES]
             every = xr[:, :, feats].reshape(nf * tok, WIDTH)
             grad = dot(every, dup[:, cols], 0, 0).astype(BF)
             count = WIDTH * nf // D
@@ -781,42 +874,41 @@
                 p_in[chunk * pieces + k, pl.ds(i * count, count)] = piece
 
         loop(D // WIDTH, grad_step)
-        ticks.tick()
 
     save(p_in, rest_in)
 
-    def partial_sums(left, right, right_dim, out):
-        def step(i):
-            feats = tile(i, WIDTH)
-            block = right[feats, :] if right_dim else right[:, feats]
-            value = dot(left[...], block, 1, right_dim).astype(BF)
-            stage[:, :, feats] = value.reshape(nf, tok, WIDTH)
-
-        loop(D // WIDTH, step)
-        save(stage, out)
-
-    partial_sums(dup, wfull, 1, pr_out)
+    def scatter_step(chunk):
+        feats = tile(chunk, D // CHUNKS)
+        value = dot(dup[...], wfull[feats, :], 1, 1).astype(BF)
+        xr[:, :, feats] = value.reshape(nf, tok, D // CHUNKS)
+        scat.start(chunk)
+
+    ag_r.drain()
+    loop(CHUNKS, scatter_step)
+
+    def lane(i):
+        return slice(i * wide, (i + 1) * wide)
 
     def ship(i):
         for step in range(1, ns):
             target = wrap(sq + step, ns)
-            there.copy(qkva.at[i, tile(target, slab), :], zin.at[i, sq], i, step).start()
-        zin[i, sq] = qkva[i, tile(sq, slab), :]
+            there.copy(dup.at[tile(target, slab), lane(i)], zin.at[i, sq], i, step).start()
+        zin[i, sq] = dup[tile(sq, slab), lane(i)]
 
     def da_step(i):
         rows = tile(i, blocks * tok)
-        qkva[3, rows, :] = dot(rows_of(gg, i * blocks, blocks), wo_ref[...], 1, 1).astype(BF)
+        dup[rows, lane(3)] = dot(rows_of(gg, i * blocks, blocks), wo_ref[...], 1, 1).astype(BF)
 
     loop(nf // blocks, da_step)
     ship(3)
+    loop(CHUNKS, scat.combine)
     ticks.tick()
+    ag_t.forward()
+    ag_t.finish()
     for i in range(3):
         ag_x[i].forward()
         turns[i].arrive(0)
         ag_x[i].finish()
-        if i == 0:
-            saves[-1].wait()
-            saves.pop()
         load = pltpu.make_async_copy(ag_x[i].buf, stage, copy_sem.at[15])
         load.start()
         load.wait()
@@ -824,18 +916,27 @@
         def lin_step(r, i=i):
             rows = tile(r, blocks * tok)
             lin = dot(rows_of(stage, r * blocks, blocks), wqkv[i])
+            if i < 2:
+                planes = rope_planes(rows_of(tab, r * blocks, blocks))
             for head in range(heads):
-                cols = slice(head * HEAD, head * HEAD + HEAD)
-                piece = lin[:, cols]
+                piece = lin[:, head * HEAD : head * HEAD + HEAD]
                 if i < 2:
-                    piece = rotated(piece, [planes_ref[k, rows, :] for k in range(3)])
-                qkva[i, rows, cols] = piece.astype(BF)
+                    piece = rotated(piece, planes)
+                at = i * wide + head * HEAD
+                dup[rows, at : at + HEAD] = piece.astype(BF)
 
         loop(nf // blocks, lin_step)
         ship(i)
         ticks.tick(2 if i < 2 else 1)
     save(wqkv, w_out)
-    partial_sums(hid, wout_ref, 0, py_out)
+
+    def out_step(i):
+        feats = tile(i, WIDTH)
+        value = dot(hid[...], wout_ref[:, feats]).astype(BF)
+        stage[:, :, feats] = value.reshape(nf, tok, WIDTH)
+
+    loop(D // WIDTH, out_step)
+    save(stage, py_out)
     for i in range(4):
         for step in range(1, ns):
             there.copy(zin.at[i, 0], zin.at[i, wrap(sq - step, ns)], i, step).wait_recv()
@@ -849,11 +950,17 @@
         head = lax.rem(pair, heads)
         cols = tile(head, HEAD)
         toks = tile(grp, tok)
-        first_end = lens_ref[sq * per + grp, 0]
-        second_end = first_end + lens_ref[sq * per + grp, 1]
+        marks = tab[sq * per + grp, 0:1, :]
+        first_end, second_end = marks[:, ROT : ROT + 1], marks[:, ROT + 1 : ROT + 2]
 
         def part_of(i, begin, count):
             return zin[i, pl.ds(begin, count), toks, cols].reshape(count * tok, HEAD)
+
+        def keep_rows(i, begin, count, value):
+            at = pl.ds(pl.multiple_of(i * wide + head * HEAD, HEAD), HEAD)
+            for k in range(count):
+                rows = pl.ds(pl.multiple_of((begin + k) * slab + grp * tok, tok), tok)
+                hid[rows, at] = value[k * tok : (k + 1) * tok].astype(BF)
 
         keys, values = part_of(1, 0, ns), part_of(2, 0, ns)
         dkv[...] = jnp.zeros_like(dkv)
@@ -863,8 +970,9 @@
             query, d_att = part_of(0, begin, q_slabs), part_of(3, begin, q_slabs)
             qi = j * queries + lax.broadcasted_iota(jnp.int32, (queries, group_tok), 0)
             ki = lax.broadcasted_iota(jnp.int32, (queries, group_tok), 1)
-            seg_q = (qi >= first_end).astype(jnp.int32) + (qi >= second_end).astype(jnp.int32)
-            seg_k = (ki >= first_end).astype(jnp.int32) + (ki >= second_end).astype(jnp.int32)
+            qf, kf = qi.astype(F32), ki.astype(F32)
+            seg_q = (qf >= first_end).astype(jnp.int32) + (qf >= second_end).astype(jnp.int32)
+            seg_k = (kf >= first_end).astype(jnp.int32) + (kf >= second_end).astype(jnp.int32)
             allowed = (seg_q == seg_k) & (qi >= ki)
             scores = jnp.where(allowed, dot(query, keys, 1, 1) * scale, NEGATIVE)
             top = jnp.max(scores, axis=1, keepdims=True)
@@ -877,43 +985,52 @@
             d_query = dot(d_score, keys) * scale
             dkv[0] += dot(d_score, query, 0, 0)
             dkv[1] += dot(prob_low, d_att, 0, 0)
-            where = pl.ds(begin, q_slabs)
-            zout[0, where, toks, cols] = attended.astype(BF).reshape(q_slabs, tok, HEAD)
-            zout[1, where, toks, cols] = d_query.astype(BF).reshape(q_slabs, tok, HEAD)
+            keep_rows(0, begin, q_slabs, attended)
+            keep_rows(1, begin, q_slabs, d_query)
 
         loop(group_tok // queries, query_step)
-        zout[2, :, toks, cols] = (dkv[0] * scale).astype(BF).reshape(ns, tok, HEAD)
-        zout[3, :, toks, cols] = dkv[1].astype(BF).reshape(ns, tok, HEAD)
+        keep_rows(2, 0, ns, dkv[0] * scale)
+        keep_rows(3, 0, ns, dkv[1])
 
     loop(per * heads, pair_step)
 
     for i in (1, 2, 3, 0):
         for step in range(1, ns):
             target = wrap(sq + step, ns)
-            home.copy(zout.at[i, target], zback.at[i, tile(sq, slab), :], i, step).start()
-        zback[i, tile(sq, slab), :] = zout[i, sq]
+            src = hid.at[tile(target, slab), lane(i)]
+            home.copy(src, zback.at[i, tile(sq, slab), :], i, step).start()
+        zback[i, tile(sq, slab), :] = hid[tile(sq, slab), lane(i)]
     ticks.tick()
     outs = (att_ref, dq_ref, dk_ref, dv_ref)
     for i in (1, 2, 3, 0):
         for step in range(1, ns):
             source = wrap(sq - step, ns)
-            home.copy(zout.at[i, 0], zback.at[i, tile(source, slab), :], i, step).wait_recv()
-        if i in (0, 3):
-            outs[i][...] = zback[i]
-        else:
+            dst = zback.at[i, tile(source, slab), :]
+            home.copy(dst, dst, i, step).wait_recv()
+        if i in (1, 2):
 
             def back_step(r, i=i):
                 rows = tile(r, tok)
+                planes = rope_planes(tab[r])
                 for head in range(heads):
                     cols = slice(head * HEAD, head * HEAD + HEAD)
                     piece = zback[i, rows, cols].astype(F32)
-                    piece = rotated_back(piece, [planes_ref[k, rows, :] for k in range(3)])
-                    outs[i][rows, cols] = piece.astype(BF)
+                    piece = rotated_back(piece, planes)
+                    zback[i, rows, cols] = piece.astype(BF)
 
             loop(nf, back_step)
+        save(zback.at[i], outs[i])
         ticks.tick()
+
+    def total_step(chunk):
+        value = scat.total(chunk)
+        sts[:, :, :, tile(chunk, D // CHUNKS)] = value.reshape(*sts.shape[:3], D // CHUNKS)
+        scat.drain(chunk)
+
+    loop(CHUNKS, total_step)
+    save(sts, dxr_ref)
     ticks.finish()
-    for gather in (ag_r, ag_g, *ag_x):
+    for gather in (*ag_gs, ag_t, *ag_x):
         gather.drain()
     for chunk in range(CHUNKS):
         turn.drain(chunk)
@@ -924,56 +1041,65 @@
     for i in range(4):
         for step in range(1, ns):
             there.copy(zin.at[i, 0], zin.at[i, 0], i, step).wait_send()
-            home.copy(zout.at[i, 0], zout.at[i, 0], i, step).wait_send()
-
-
-def run_forward(nf, ns, low, g_own, win, wout, ws, wo, planes, lens):
+            home.copy(zin.at[i, 0], zin.at[i, 0], i, step).wait_send()
+
+
+def run_forward(nf, ns, hist, g_own, win, ws, wo, wout, table, mixing):
     tok = g_own.shape[0]
     hidden = wout.shape[0]
     wide = wo.shape[0]
+    units = mixing[0].shape[0]
     lines = forward_lines(nf, wide, hidden)
-    count = (8 + CHUNKS) * (nf - 1) + 8 * (ns - 1)
+    count = (8 + 2 * CHUNKS + hidden // CHUNKS // LANES) * (nf - 1) + 8 * (ns - 1)
     flat = shape((nf * tok, wide))
     block = shape((nf, tok, D))
     total = CHUNKS * (hidden // CHUNKS // LANES)
-    outs = [block] * 6 + [shape((3, D, wide)), shape((total, nf, D // nf, LANES))]
-    outs += lines.outs() + [flat] * 4
+    outs = [block] * 5 + [shape((3, D, wide)), shape((total, nf, D // nf, LANES))]
+    outs += [shape((wide, D)), shape((3, wide, D)), shape(win.shape)]
+    outs += [shape((STREAMS, tok, D), F32)]
+    slots = tok // STREAMS // ROWS
+    outs += lines.outs() + [flat] * 4 + [shape((slots, STREAMS, ROWS, D), F32)]
+    outs += [shape((tok, STREAMS * HIST), F32), shape((STREAMS + 1, tok, 1), F32)]
+    outs += [shape((tok, units), F32), shape((tok, units)), shape((tok, D))]
     exchange = pltpu.VMEM((4, ns, nf // ns * tok, wide), BF)
     return pl.pallas_call(
         partial(forward_kernel, nf, ns, lines),
         out_shape=tuple(outs),
-        in_specs=[hbm()] * 3
-        + [vmem()]
-        + [hbm()] * 3
-        + [vmem()] * 2
-        + [pl.BlockSpec(memory_space=pltpu.SMEM)],
-        out_specs=(hbm(),) * 9 + (vmem(),) * 4,
+        in_specs=[hbm()] * 8 + [vmem()] * 6,
+        out_specs=(hbm(),) * 17 + (vmem(),) * 5,
         scratch_shapes=[
             pltpu.VMEM((nf, tok, D), BF),
             pltpu.VMEM((nf, tok, D), BF),
             pltpu.VMEM((D, hidden), BF),
             pltpu.VMEM((nf * tok, hidden), BF),
             pltpu.VMEM((nf * tok, hidden), BF),
-            pltpu.VMEM((total, 1, LANES, D), BF),
+            pltpu.VMEM(lines.outs()[0].shape, BF),
             pltpu.VMEM((total, nf, D // nf, LANES), BF),
             pltpu.VMEM((nf, tok, D), BF),
             pltpu.VMEM((3, D, wide), BF),
-            pltpu.VMEM((4, nf * tok, wide), BF),
-            exchange,
             exchange,
             pltpu.VMEM((4, nf * tok, wide), BF),
             pltpu.VMEM((2, ns * tok, HEAD), F32),
+            pltpu.VMEM((hidden, D), BF),
+            pltpu.VMEM((wide, D), BF),
+            pltpu.VMEM((2,) + lines.kinds[0][0][1:], F32),
+            pltpu.VMEM((slots, STREAMS, ROWS, D), F32),
+            pltpu.VMEM((2, STREAMS - 1, ROWS, D), BF),
+            pltpu.VMEM((tok, D), BF),
+            pltpu.VMEM((nf, tok, LANES), F32),
+            pltpu.VMEM((nf // 2, tok, D), BF),
+            pltpu.VMEM((nf // 2 - 1, tok, D), BF),
             pltpu.SemaphoreType.DMA((count,)),
             pltpu.SemaphoreType.DMA((count,)),
-            pltpu.SemaphoreType.DMA((16,)),
+            pltpu.SemaphoreType.DMA((48,)),
         ]
         + lines.scratch(),
-        compiler_params=params(1),
+        compiler_params=params(1, 63),
         name="forward",
-    )(low, g_own, win, wout, *ws, wo, planes, lens)
-
-
-TENSORS = 5
+    )(hist, g_own, win, *ws, wo, wout, table, *mixing)
+
+
+TENSORS = 4
 SMALL = 112
 
 
@@ -987,7 +1113,7 @@
     att_ref, dq_ref, dk_ref, dv_ref, wqkv, wo_ref, p_in, g_ref = refs[:8]
     coef_ref, inv_ref, pre_ref, act_ref, mixed_ref, mix_in_ref, mix_out_ref = refs[8:15]
     again_ref, mgain_ref, xgain_ref = refs[15:18]
-    sources, (pr_ref, py_ref, hist_ref, st_ref) = refs[18:22], refs[22:26]
+    sources, (dxr_ref, py_ref, hist_ref, st_ref) = refs[18:22], refs[22:26]
     lo_ref, sm_out, hg_ref = refs[26:29]
     results, refs = refs[29:34], refs[34:]
     stage, part, sib, rec, grads, p_o, dx_ref, y_ref = refs[:8]
@@ -1012,6 +1138,8 @@
     load = pltpu.make_async_copy(sources[0], stage, copy_sem.at[0])
     load.start()
     pltpu.make_async_copy(hist_ref.at[HIST - 1], h8, copy_sem.at[1]).start()
+    extra = pltpu.make_async_copy(dxr_ref, dx_ref.at[3], copy_sem.at[2 + CHUNKS])
+    extra.start()
     scats = [
         Scatter(
             plane,
@@ -1029,7 +1157,7 @@
     def total(t):
         def total_step(chunk):
             feats = tile(chunk, D // CHUNKS)
-            if t < 4:
+            if t < 3:
                 dx_ref[t, :, feats] = scats[t].total(chunk)
             else:
                 lo_ref[:, feats] = (y_ref[:, feats] + scats[t].total(chunk)).astype(BF)
@@ -1043,8 +1171,7 @@
 
     def fetch(t, chunk):
         feats = slice(chunk * (D // CHUNKS), (chunk + 1) * (D // CHUNKS))
-        src = (pr_ref, py_ref)[t - 3].at[:, :, feats]
-        return pltpu.make_async_copy(src, scats[t].part.at[:, :, feats], copy_sem.at[2 + chunk])
+        return pltpu.make_async_copy(py_ref.at[:, :, feats], scats[t].part.at[:, :, feats], copy_sem.at[2 + chunk])
 
     for t in range(TENSORS):
         if t >= sibs:
@@ -1062,7 +1189,7 @@
                 scats[t].part[:, :, feats] = value.astype(BF).reshape(nf, tok, D // CHUNKS)
             else:
                 fetch(t, chunk).wait()
-            if t == 4:
+            if t == 3:
                 value = dot(att_ref[...], wo_ref[:, feats]).reshape(nf, tok, D // CHUNKS)
                 value = value + scats[t].part[:, :, feats].astype(F32)
                 scats[t].part[:, :, feats] = value.astype(BF)
@@ -1072,7 +1199,7 @@
             if chunk % 2:
                 ticks.tick()
         scats[t].combine(CHUNKS - 1)
-        if t < 4:
+        if t < TENSORS:
             pltpu.make_async_copy(sources[t], stage, copy_sem.at[0]).wait()
 
             def grad_step(i, t=t):
@@ -1096,6 +1223,7 @@
         if t:
             total(t - 1)
 
+    extra.wait()
     gsum[...] = jnp.zeros_like(gsum)
     steps = tok // ROWS
 
@@ -1171,10 +1299,10 @@
     pre, d_coef = pre_ref[...], dcoef[...]
     slope = 0.5 * (1.0 + lax.erf(pre * (0.5**0.5)))
     slope = slope + pre * jnp.exp(-0.5 * pre * pre) * 0.3989422804014327
-    d_pre = (dot(d_coef, mix_out, 1, 1) * slope).astype(BF)
+    d_pre = (dot(d_coef, mix_out) * slope).astype(BF)
     hidden = pre.shape[1]
     sm_ref[0:hidden, :] = dot(d_pre, mixed_ref[...], 0, 0)
-    dmixed[...] = dot(d_pre, mix_in, 1, 1)
+    dmixed[...] = dot(d_pre, mix_in)
     pltpu.make_async_copy(hist_ref.at[HIST - 1], h8, copy_sem.at[1]).wait()
 
     def last_step(i):
@@ -1251,7 +1379,7 @@
             pltpu.SemaphoreType.DMA((few,)),
             pltpu.SemaphoreType.DMA((count,)),
             pltpu.SemaphoreType.DMA((count,)),
-            pltpu.SemaphoreType.DMA((2 + CHUNKS,)),
+            pltpu.SemaphoreType.DMA((3 + CHUNKS,)),
             pltpu.SemaphoreType.DMA((6,)),
             pltpu.SemaphoreType.REGULAR((TENSORS - 2,)),
         ]
@@ -1319,24 +1447,32 @@
 
 
 def finish_kernel(units, *refs):
-    sum_in, sum_q, sum_k, sum_v, out_ref, sm_ref = refs[:6]
-    w_in, wq, wk, wv, w_out, mix_in, mix_out, again, mgain, xgain = refs[6:]
+    sum_in, sum_q, sum_k, sum_v, out_ref, sm_ref, sum_o = refs[:7]
+    w_in, wq, wk, wv, w_out, mix_in, mix_out, again, mgain, xgain, wo = refs[7:]
     for dst, ref in ((w_in, sum_in), (wq, sum_q), (wk, sum_k), (wv, sum_v)):
         for k in range(ref.shape[0]):
             dst[:, k * LANES : (k + 1) * LANES] = ref[k, 0].astype(F32)
-    w_out[...] = out_ref[...].astype(F32)
+    part = out_ref.shape[-1]
+    for k in range(out_ref.shape[1]):
+        w_out[:, k * part : (k + 1) * part] = out_ref[0, k].astype(F32)
     mix_in[...] = sm_ref[0, 0:units, :]
     for k, dst in enumerate((again, mgain, xgain)):
         dst[...] = sm_ref[0, units + k : units + k + 1, :]
 
+    @pl.when(pl.program_id(0) == 0)
+    def _():
+        wo[...] = sum_o[...].astype(F32)
+
     @pl.when(pl.program_id(0) < STREAMS)
     def _():
         mix_out[0] = sm_ref[0, units + 3 : units + 3 + HIST, 0:LANES]
 
 
-def run_finish(nf, units, turned, out, small):
+def run_finish(nf, units, turned, out, small, sum_o):
     cols = D // nf
-    hidden = out.shape[0]
+    _, pieces, width, part = out.shape
+    hidden = out.shape[0] * width
+    high = hidden // nf
     wide = turned[1].shape[0] * LANES
     rows = turned[0].shape[2]
 
@@ -1356,11 +1492,16 @@
             shape((units, D), F32),
             shape((STREAMS, HIST, LANES), F32),
             *[shape((1, D), F32)] * 3,
+            shape((sum_o.shape[0], D), F32),
         ),
         in_specs=[
             *[chunks(part) for part in turned],
-            pl.BlockSpec((hidden // nf, D), lambda i: (i, 0)),
+            pl.BlockSpec(
+                (1, pieces, high, part),
+                lambda i: (i * high // width, 0, lax.rem(i, width // high), 0),
+            ),
             pl.BlockSpec((1, SMALL, cols), lambda i: (i, 0, 0)),
+            pl.BlockSpec((sum_o.shape[0], D), lambda i: (0, 0)),
         ],
         out_specs=(
             block(rows, hidden),
@@ -1369,10 +1510,11 @@
             block(units, cols),
             pl.BlockSpec((1, HIST, LANES), lambda i: (jnp.minimum(i, STREAMS - 1), 0, 0)),
             *[block(1, cols)] * 3,
+            pl.BlockSpec((sum_o.shape[0], D), lambda i: (0, 0)),
         ),
-        compiler_params=pltpu.CompilerParams(vmem_limit_bytes=40 * MIB),
+        compiler_params=pltpu.CompilerParams(vmem_limit_bytes=62 * MIB),
         name="finish",
-    )(*turned, out, small)
+    )(*turned, out, small, sum_o)
 
 
 def local(
@@ -1395,27 +1537,22 @@
 ):
     hist = history[:, 0]
     tok_rows = hist.shape[1]
-    lens = lax.all_gather(seq_lengths, "fsdp", axis=0, tiled=True)
-    slab_index = lax.axis_index("seq") * tok_rows + jnp.arange(tok_rows, dtype=jnp.int32)
-    every_index = jnp.tile(slab_index, nf)
-    _, place = token_marks(every_index, jnp.repeat(lens, tok_rows, axis=0))
-    planes = rope_planes(place)
-    gains = [g[None] for g in (attn_gain, mlp_gain, mix_gain)]
-    low, stream, coef, inv, pre, act, mixed = run_start(hist, mix_in, mix_out, *gains)
+    tok_index = lax.axis_index("seq") * tok_rows + jnp.arange(tok_rows, dtype=jnp.int32)
+    table = token_table(tok_index, seq_lengths[0])
     grad_out = cotangent[0]
-    ws = [w.astype(BF) for w in (wq, wk, wv)]
-    wo_low, win_low, wout_low = wo.astype(BF), w_in.astype(BF), w_out.astype(BF)
-    *xgs, gg, pr, py, wqkv, p_in, sum_out, att, dq, dk, dv = run_forward(
-        nf, ns, low, grad_out, win_low, wout_low, ws, wo_low, planes, lens
+    mixing = (mix_in.T, mix_out.T, attn_gain[None], mlp_gain[None], mix_gain[None])
+    outs = run_forward(
+        nf, ns, hist, grad_out, w_in, (wq, wk, wv), wo, w_out, table, mixing
     )
-    near = (att, dq, dk, dv, wqkv, wo_low, p_in, grad_out)
-    near += (coef, inv, pre, act, mixed, mix_in, mix_out, *gains)
-    far = (*xgs, gg, pr, py, hist, stream)
+    xgs, (gg, py, wqkv, p_in, wo_low, _, _, stream, sum_out) = outs[:3], outs[3:12]
+    (att, dq, dk, dv, dxr), mixed = outs[12:17], outs[17:]
+    dxr = dxr.reshape(tok_rows, D)
+    near = (att, dq, dk, dv, wqkv, wo_low, p_in, grad_out, *mixed, *mixing)
+    far = (*xgs, gg, dxr, py, hist, stream)
     layer_out, small, history_grad, sum_in, *sums, sum_o = run_back(nf, ns, near, far)
-    dwo = sum_o.reshape(wo.shape).astype(F32)
     units = mix_in.shape[1]
-    dw_in, dwq, dwk, dwv, dwout, dmix_in, dmix_out, *dgains = run_finish(
-        nf, units, (sum_in, *sums), sum_out.reshape(w_out.shape), small
+    dw_in, dwq, dwk, dwv, dwout, dmix_in, dmix_out, *dgains, dwo = run_finish(
+        nf, units, (sum_in, *sums), sum_out.reshape(CHUNKS, -1, *sum_out.shape[2:]), small, sum_o.reshape(wo.shape)
     )
     dmix_out = dmix_out.transpose(2, 1, 0).reshape(LANES, STREAMS * HIST)[:units]
     return (

time: 629 us -> 579 us (0.921)
  other arithmetic: 20.2 us -> 2.41 us
  local copies, waits for them, and re-layouts: 22.6 us -> 8.9 us
  blocking collectives: 10.4 us -> 0 us
  Pallas kernels: 566 us -> 556 us
    unnamed x33 -> x4, local copies, waits for them, and re-layouts: 21.7 us -> 6.04 us
    convert_element_type x8 -> x2, other arithmetic: 16.6 us -> 1.38 us  [the longest x1 0.72 us: token_table(): ends = jnp.stack([lengths[0], lengths[0] + lengths[1]]).astype(F32)]
    pallas_call x1 -> x0, Pallas kernels: 11.2 us -> none  [run_start(): pl.pallas_call(start_kernel, out_shape=(shape((STREAMS, tok, D)), shape((...]
    all_gather x1 -> x0, blocking collectives: 10.4 us -> none  [local(): lens = lax.all_gather(seq_lengths, 'fsdp', axis=0, tiled=True)]
    pallas_call x1, Pallas kernels: 8.64 us -> 15.2 us  [run_finish(): pl.pallas_call(partial(finish_kernel, units), grid=(nf,), out_shape=(shap...]
where the time goes in v5:
time: 579 us; the launch traced here: 570 us
  Pallas kernels  556 us (96%)
  local copies, waits for them, and re-layouts  8.9 us (2%)
    pallas_call x1, Pallas kernels, run_forward(): pl.pallas_call(partial(forward_kernel, nf, ns, lines), out_shape=tuple(ou...  277 us
    pallas_call x1, Pallas kernels, run_back(): pl.pallas_call(partial(back_kernel, nf, ns, lines), out_shape=tuple(outs...  264 us
    pallas_call x1, Pallas kernels, run_finish(): pl.pallas_call(partial(finish_kernel, units), grid=(nf,), out_shape=(shap...  15.2 us

profile of v5, /device:TPU:0, one launch (start us, length us, event | category | flops | bytes accessed | tf_op | source)
XLA Modules:
  0.0 570.2 jit_solution(5952927278188977778)
XLA Ops:
  0.7 0.1 pad.3.clone
  0.7 1.3 fusion.3
  3.4 0.7 fusion.2
  4.0 0.7 add_convert_fusion
  4.7 0.1 pad.2.clone
  4.8 0.3 multiply_cosine_fusion
  5.1 0.7 maximum_maximum_fusion.refs_8_
  5.9 277.2 %forward.1 = (bf16[8,128,2048]{2,1,0:T(8,128)(2,1)}, bf16[8,128,2048]{2,1,0:T(8,128)(2,1)}, bf16[8,128,2048]{2,1,0:T(8,128)(2,1)}, bf16[8,128,2048]{2,1,0:T(8,12...) custom-call(bf16[9,128,2048]{2,1,0:T(8,128)(2,1)} %bitcast.26, ...), custom_call_target="tpu_custom_call" | custom-call | tf_op jit(solution)/shard_map/forward/pallas_call | solution.py:1065
  283.0 264.0 %back.1 = (bf16[128,2048]{1,0:T(8,128)(2,1)}, f32[8,112,256]{2,1,0:T(8,128)}, bf16[9,128,2048]{2,1,0:T(8,128)(2,1)}, bf16[8,8,256,128]{3,2,1,0:T(8,128)(2,1)}, b...) custom-call(bf16[1024,256]{1,0:T(8,128)(2,1)} %get-tuple-element.52., ...), custom_call_target="tpu_custom_call" | custom-call | tf_op jit(solution)/shard_map/back/pallas_call | solution.py:1353
  547.1 0.0 copy-start
  547.1 15.2 %finish.1 = (f32[256,8192]{1,0:T(8,128)}, f32[256,2048]{1,0:T(8,128)}, f32[256,2048]{1,0:T(8,128)}, f32[256,2048]{1,0:T(8,128)}, f32[1024,2048]{1,0:T(8,128)}, /...) custom-call(bf16[8,8,256,128]{3,2,1,0:T(8,128)(2,1)} %get-tuple-elem, ...), custom_call_target="tpu_custom_call" | custom-call | tf_op jit(solution)/shard_map/finish/pallas_call | solution.py:1485
  562.3 0.8 copy.31
  563.1 0.6 slice.20
  563.7 0.0 copy-done
  563.7 0.8 copy.35
  564.5 5.2 copy.36
  (2 shorter events, 0.0 us)
Async XLA Ops:
  547.1 16.6 %copy-start = (bf16[128,2048]{1,0:T(8,128)(2,1)S(1)}, bf16[128,2048]{1,0:T(8,128)(2,1)}, u32[]{:S(2)}) copy-start(bf16[128,2048]{1,0:T(8,128)(2,1)} %get-tuple-element.71) | copy-start | bytes 1572868

commit v6 on v5

--- a/solution.py
+++ b/solution.py
@@ -506,7 +506,7 @@
         listed = [partial(self.relay, hop=hop) for hop in range(1, self.ends)]
         listed += [self.meet, self.settle]
         if self.turned:
-            listed += [self.pause, self.spread_end]
+            listed += [self.spread_end]
         listed += [self.pass_on]
         listed += [partial(self.outward_hop, hop=hop) for hop in range(1, self.ends)]
         return listed

time: 579 us -> 579 us (level)
  no operation moved by 1% of the time
where the time goes in v6:
time: 579 us; the launch traced here: 570 us
  Pallas kernels  556 us (96%)
  local copies, waits for them, and re-layouts  8.9 us (2%)
    pallas_call x1, Pallas kernels, run_forward(): pl.pallas_call(partial(forward_kernel, nf, ns, lines), out_shape=tuple(ou...  277 us
    pallas_call x1, Pallas kernels, run_back(): pl.pallas_call(partial(back_kernel, nf, ns, lines), out_shape=tuple(outs...  264 us
    pallas_call x1, Pallas kernels, run_finish(): pl.pallas_call(partial(finish_kernel, units), grid=(nf,), out_shape=(shap...  15.2 us

profile of v6, /device:TPU:0, one launch (start us, length us, event | category | flops | bytes accessed | tf_op | source)
XLA Modules:
  0.0 570.2 jit_solution(9238747886119906272)
XLA Ops:
  0.7 0.1 pad.3.clone
  0.7 1.3 fusion.3
  3.4 0.7 fusion.2
  4.0 0.7 add_convert_fusion
  4.7 0.1 pad.2.clone
  4.8 0.3 multiply_cosine_fusion
  5.1 0.7 maximum_maximum_fusion.refs_8_
  5.9 277.2 %forward.1 = (bf16[8,128,2048]{2,1,0:T(8,128)(2,1)}, bf16[8,128,2048]{2,1,0:T(8,128)(2,1)}, bf16[8,128,2048]{2,1,0:T(8,128)(2,1)}, bf16[8,128,2048]{2,1,0:T(8,12...) custom-call(bf16[9,128,2048]{2,1,0:T(8,128)(2,1)} %bitcast.26, ...), custom_call_target="tpu_custom_call" | custom-call | tf_op jit(solution)/shard_map/forward/pallas_call | solution.py:1065
  283.0 264.0 %back.1 = (bf16[128,2048]{1,0:T(8,128)(2,1)}, f32[8,112,256]{2,1,0:T(8,128)}, bf16[9,128,2048]{2,1,0:T(8,128)(2,1)}, bf16[8,8,256,128]{3,2,1,0:T(8,128)(2,1)}, b...) custom-call(bf16[1024,256]{1,0:T(8,128)(2,1)} %get-tuple-element.52., ...), custom_call_target="tpu_custom_call" | custom-call | tf_op jit(solution)/shard_map/back/pallas_call | solution.py:1353
  547.1 0.0 copy-start
  547.1 15.2 %finish.1 = (f32[256,8192]{1,0:T(8,128)}, f32[256,2048]{1,0:T(8,128)}, f32[256,2048]{1,0:T(8,128)}, f32[256,2048]{1,0:T(8,128)}, f32[1024,2048]{1,0:T(8,128)}, /...) custom-call(bf16[8,8,256,128]{3,2,1,0:T(8,128)(2,1)} %get-tuple-elem, ...), custom_call_target="tpu_custom_call" | custom-call | tf_op jit(solution)/shard_map/finish/pallas_call | solution.py:1485
  562.3 0.8 copy.31
  563.1 0.6 slice.20
  563.7 0.0 copy-done
  563.7 0.8 copy.35
  564.5 5.2 copy.36
  (2 shorter events, 0.0 us)
Async XLA Ops:
  547.1 16.6 %copy-start = (bf16[128,2048]{1,0:T(8,128)(2,1)S(1)}, bf16[128,2048]{1,0:T(8,128)(2,1)}, u32[]{:S(2)}) copy-start(bf16[128,2048]{1,0:T(8,128)(2,1)} %get-tuple-element.71) | copy-start | bytes 1572868
